TPU v7x, 32 devices: a whole 2x2x4 slice. The times are simulated.
32 devices in a mesh: tm: 8 (over z, x), rows: 4 (over y, core).
Axes of the slice: x: 2, y: 2, z: 4, core: 2. Of those that a mesh axis runs over, the one named last changes fastest.
Arguments:
- observed: int32 [32], P('tm'), may hold values from 0 to 255
- pattern: int32 [16, 4], replicated, may hold values from 0 to 15, as said below
- trans_blocks: bfloat16 [16, 4, 64, 64], replicated, may hold values from 0.00077819824 to 0.0078125
- leave_rate: float32 [1024], replicated, may hold values from 0.0078125 to 0.03
- symbol_emit: float32 [256, 1024], replicated, may hold values from 0.25 to 4
- cluster_emit: float32 [16, 1024], replicated, may hold values from 0.25 to 4
- symbol_cluster: int32 [256], replicated, may hold values from 0 to 15
Outputs:
- prefix_rows: float32 [8, 1024, 1024], P('tm', 'rows')
- prefix_rate: float32 [8, 1024], P('tm', 'rows')
Inputs may be any that keep to these rules, and one draw needn't show every extreme that they name: Each row of pattern names 4 different source blocks.
All inputs are finite; a program needn't handle non-finite values.
Results may differ from a plain program's by a relative error of at most 0.0037.
Values sent between devices are 32-bit elements; how exact they have to be, the bound alone decides.
No kernel may reach another device: no remote copies, remote signals or barrier semaphores. Data moves between devices by JAX's collectives and lax.ppermute only.
A program may use at most 64 MiB of HBM per device.

v0:
```python
import jax
import jax.numpy as jnp
from jax import lax
from jax.sharding import PartitionSpec as P


def passed_along(block, axis, distance):
    devices = range(lax.axis_size(axis))
    route = [(i - distance, i) for i in devices if i - distance in devices]
    return lax.ppermute(block, axis, route)


def normalize(product, base_log):
    row_sum = jnp.sum(product, axis=1)
    n_cols = product.shape[1]
    return (product * (n_cols / row_sum)[:, None], base_log + jnp.log(row_sum / n_cols))


def combine(left_r, left_l, right_r, right_l):
    top_log = jnp.max(right_l)
    scaled = left_r * jnp.exp(right_l - top_log)[None, :]
    product = jnp.dot(
        scaled, right_r, precision=lax.Precision.HIGHEST, preferred_element_type=jnp.float32
    )
    return normalize(product, left_l + top_log)


def compose(
    observed, pattern, trans_blocks, leave_rate, symbol_emit, cluster_emit, symbol_cluster, identity
):
    n_blocks, n_source, block_size, _ = trans_blocks.shape
    n_states = leave_rate.shape[0]
    n_symbols = symbol_emit.shape[0]
    n_local = identity.shape[0]
    sym_hot = (observed[:, None] == jnp.arange(n_symbols)[None, :]).astype(jnp.float32)
    clus_table = (symbol_cluster[:, None] == jnp.arange(n_blocks)[None, :]).astype(jnp.float32)
    clus_hot = jnp.dot(sym_hot, clus_table, precision=lax.Precision.HIGHEST)
    emission = jnp.dot(sym_hot, symbol_emit, precision=lax.Precision.HIGHEST)
    emission = emission * jnp.dot(clus_hot, cluster_emit, precision=lax.Precision.HIGHEST)
    src_leave = leave_rate.reshape(n_blocks, block_size)[pattern]
    moved_blocks = (trans_blocks.astype(jnp.float32) * src_leave[..., None]).astype(jnp.bfloat16)
    moved_flat = moved_blocks.reshape(n_blocks, n_source * block_size, block_size)
    stay_rate = 1.0 - leave_rate

    def advance(carried, emission_row):
        current, log_scale = carried
        kept_part = current.astype(jnp.float32) * stay_rate[None, :]
        kept_part = jnp.roll(kept_part.reshape(n_local, n_blocks, block_size), 1, axis=2)
        picked = current.reshape(n_local, n_blocks, block_size)[:, pattern, :]
        picked = picked.reshape(n_local, n_blocks, n_source * block_size)
        moved_part = jnp.einsum(
            "rjc,jcd->rjd", picked, moved_flat, preferred_element_type=jnp.float32
        )
        product = (kept_part + moved_part).reshape(n_local, n_states) * emission_row[None, :]
        new_r, new_l = normalize(product, log_scale)
        return ((new_r.astype(jnp.bfloat16), new_l), None)

    start_value = (identity.astype(jnp.bfloat16), jnp.zeros((n_local,), jnp.float32))
    (seg_r, seg_l), _ = lax.scan(advance, start_value, emission)
    return (seg_r, seg_l)


def body(observed, pattern, trans_blocks, leave_rate, symbol_emit, cluster_emit, symbol_cluster):
    n_states = leave_rate.shape[0]
    n_local = n_states // lax.axis_size("rows")
    row_start = lax.axis_index("rows") * n_local
    identity = (jnp.arange(n_states)[None, :] == (row_start + jnp.arange(n_local))[:, None]).astype(
        jnp.float32
    )
    zero_l = jnp.zeros((n_local,), jnp.float32)
    seg_r, seg_l = compose(
        observed,
        pattern,
        trans_blocks,
        leave_rate,
        symbol_emit,
        cluster_emit,
        symbol_cluster,
        identity,
    )
    own_r = seg_r.astype(jnp.float32)
    full_r, full_l = (
        lax.all_gather(own_r, "rows", axis=0, tiled=True),
        lax.all_gather(seg_l, "rows", axis=0, tiled=True),
    )
    tm_count = lax.axis_size("tm")
    segment_pos = lax.axis_index("tm")
    first_r, first_l = combine(identity, zero_l, full_r, full_l)

    def link(turn_index, carried):
        cur_r, cur_l = carried
        recv_r, recv_l = passed_along((cur_r, cur_l), "tm", 1)
        is_valid = segment_pos >= 1
        recv_r = jnp.where(is_valid, recv_r, identity)
        recv_l = jnp.where(is_valid, recv_l, zero_l)
        new_r, new_l = combine(recv_r, recv_l, full_r, full_l)
        is_turn = segment_pos == turn_index
        return (jnp.where(is_turn, new_r, cur_r), jnp.where(is_turn, new_l, cur_l))

    cur_r, cur_l = lax.fori_loop(1, tm_count, link, (first_r, first_l))
    steps_here = seg_r.shape[0] * 0 + observed.shape[0]
    divisor = (steps_here * (segment_pos + 1)).astype(jnp.float32)
    return (cur_r[None, :, :], (cur_l / divisor)[None, :])


def solution(mesh):
    in_specs = (P("tm"), P(), P(), P(), P(), P(), P())
    out_specs = (P("tm", "rows", None), P("tm", "rows"))
    return jax.shard_map(body, mesh=mesh, in_specs=in_specs, out_specs=out_specs, check_vma=False)
```

profile of v0, /device:TPU:26, one launch (start us, length us, event | category | flops | bytes accessed | tf_op | source)
XLA Modules:
  0.0 331.5 jit_solution(10839008486880544619)
XLA Ops:
  7.3 0.9 reshape.70
  8.1 0.7 broadcast_subtract_fusion
  9.0 0.7 compare_select_fusion.1
  10.5 1.7 multiply_convert_fusion
  13.5 32.8 %while.31 = (s32[]{:T(128)}, bf16[256,1024]{0,1:T(8,128)(2,1)S(1)}, f32[256]{0:T(256)S(1)}, f32[1024]{0:T(1024)S(1)}, s32[16,4]{0,1:T(4,128)S(1)}, /*index=5*/bf...) while((s32[]{:T(128)}, bf16[256,1024]{0,1:T(8,128)(2,1)S(1)}, ...), condition=%wide.region_2.3_spmd.clone, body=%wide.region_0.2_spmd.clone.sunk | while | flops 136579008 | bytes 12136575 | solution.py:59
  14.0 0.7 fusion.42
  15.2 2.0 gather_fusion
  17.2 3.0 multiply_reduce_fusion.2
  20.3 1.4 fusion.43
  22.2 0.7 fusion.42
  23.4 2.0 gather_fusion
  25.4 3.0 multiply_reduce_fusion.2
  28.5 1.4 fusion.43
  30.4 0.7 fusion.42
  31.6 2.0 gather_fusion
  33.6 3.0 multiply_reduce_fusion.2
  36.7 1.4 fusion.43
  38.6 0.7 fusion.42
  39.8 2.0 gather_fusion
  41.8 3.0 multiply_reduce_fusion.2
  44.9 1.4 fusion.43
  46.3 1.0 convert_element_type.30
  47.4 5.1 %all-gather = f32[4,1,256]{2,1,0:T(1,128)S(1)} all-gather(f32[1,1,256]{2,1,0:T(1,128)S(1)} %bitcast.66), channel_id=1, replica_groups=mesh['tm'=8,'rows'=4] {'rows'}, dimensions={0}, use_global_device_ids=true | all-gather | bytes 5120 | tf_op jit(solution)/shard_map/all_gather | solution.py:84
  52.5 0.7 reduce_max.19
  53.8 29.2 %all-gather.3.cloned.1.call-done = f32[1024,1024]{0,1:T(8,128)} async-done(((f32[256,1024]{0,1:T(8,128)}), f32[1024,1024]{0,1:T(8,128)}) %all-gather.3.cloned.1.call-update) | async-done | bytes 4194320 | tf_op jit(solution)/shard_map/all_gather | solution.py:83
  83.0 9.3 %fusion.24 = (f32[256]{0:T(256)S(1)}, f32[256,1024]{1,0:T(8,128)S(1)}) fusion(f32[1024,1024]{0,1:T(8,128)} %all-gather.3.cloned.1.call-done, f32[1024]{0:T(1024)S(1)} %subtract_exponential_fusion.1, s32[256]{0:T(256)S(1)} %iota_add_fusion), kind=kOutput, calls=%fused_computation.54 | convolution fusion | flops 3222011648 | bytes 5249024 | tf_op jit(solution)/shard_map/dot_general | solution.py:22
  92.4 0.6 log_add_fusion
  93.1 5.4 %copy.23 = f32[1024,1024]{1,0:T(8,128)} copy(f32[1024,1024]{0,1:T(8,128)} %all-gather.3.cloned.1.call-done) | data formatting | bytes 8388608
  98.5 225.1 %while.30 = (s32[]{:T(128)}, f32[256,1024]{1,0:T(8,128)S(1)}, f32[256]{0:T(256)S(1)}, s32[]{:T(128)}, pred[]{:T(512)}, /*index=5*/f32[]{:T(128)}, f32[1024]{0:T(...) while((s32[]{:T(128)}, f32[256,1024]{1,0:T(8,128)S(1)}, f32[256]{0:T(256)S(1)}, ...), condition=%wide.region_7.8_spmd.clone, body=%wide.region_5.7_spmd.clone.sunk | while | flops 3223062784 | bytes 13656266 | solution.py:100
  98.5 1.3 collective-permute-start
  99.8 1.3 collective-permute-start.1
  101.7 24.0 %collective-permute-done = f32[256,1024]{1,0:T(8,128)S(1)} collective-permute-done((f32[256,1024]{1,0:T(8,128)S(1)}, f32[256,1024]{1,0:T(8,128)S(1)}, u32[]{:S(2)}, u32[]{:S(2)}) %collective-permute-start) | collective-permute-done | bytes 1048608 | tf_op jit(solution)/shard_map/while/body/eval_jaxpr/ppermute | solution.py:10
  125.7 6.2 %fusion.39 = (f32[256]{0:T(256)S(1)}, f32[256,1024]{1,0:T(8,128)S(1)}) fusion(f32[1024,1024]{1,0:T(8,128)} %get-tuple-element.499, f32[256,1024]{1,0:T(8,128)S(1)} %collective-permute-done, s32[256]{0:T(256)S(1)} %get-tuple-element.500, f32[1024]{0:T(1024)S(1)} %subtract_exponential_fusion.3, pred[]{:T(512)} %get-tuple-element.496), kind=kOutput, calls=%fused_computation.53.clone.1 | convolution fusion | flops 3222535936 | bytes 6297601 | tf_op jit(solution)/shard_map/while/body/eval_jaxpr/dot_general | solution.py:22
  131.9 0.6 add_select_fusion.2
  132.8 1.3 collective-permute-start
  134.1 1.3 collective-permute-start.1
  136.0 23.2 %collective-permute-done = f32[256,1024]{1,0:T(8,128)S(1)} collective-permute-done((f32[256,1024]{1,0:T(8,128)S(1)}, f32[256,1024]{1,0:T(8,128)S(1)}, u32[]{:S(2)}, u32[]{:S(2)}) %collective-permute-start) | collective-permute-done | bytes 1048608 | tf_op jit(solution)/shard_map/while/body/eval_jaxpr/ppermute | solution.py:10
  159.2 6.2 %fusion.39 = (f32[256]{0:T(256)S(1)}, f32[256,1024]{1,0:T(8,128)S(1)}) fusion(f32[1024,1024]{1,0:T(8,128)} %get-tuple-element.499, f32[256,1024]{1,0:T(8,128)S(1)} %collective-permute-done, s32[256]{0:T(256)S(1)} %get-tuple-element.500, f32[1024]{0:T(1024)S(1)} %subtract_exponential_fusion.3, pred[]{:T(512)} %get-tuple-element.496), kind=kOutput, calls=%fused_computation.53.clone.1 | convolution fusion | flops 3222535936 | bytes 6297601 | tf_op jit(solution)/shard_map/while/body/eval_jaxpr/dot_general | solution.py:22
  165.3 0.6 add_select_fusion.2
  166.2 1.3 collective-permute-start
  167.5 1.3 collective-permute-start.1
  169.5 22.8 %collective-permute-done = f32[256,1024]{1,0:T(8,128)S(1)} collective-permute-done((f32[256,1024]{1,0:T(8,128)S(1)}, f32[256,1024]{1,0:T(8,128)S(1)}, u32[]{:S(2)}, u32[]{:S(2)}) %collective-permute-start) | collective-permute-done | bytes 1048608 | tf_op jit(solution)/shard_map/while/body/eval_jaxpr/ppermute | solution.py:10
  192.3 6.2 %fusion.39 = (f32[256]{0:T(256)S(1)}, f32[256,1024]{1,0:T(8,128)S(1)}) fusion(f32[1024,1024]{1,0:T(8,128)} %get-tuple-element.499, f32[256,1024]{1,0:T(8,128)S(1)} %collective-permute-done, s32[256]{0:T(256)S(1)} %get-tuple-element.500, f32[1024]{0:T(1024)S(1)} %subtract_exponential_fusion.3, pred[]{:T(512)} %get-tuple-element.496), kind=kOutput, calls=%fused_computation.53.clone.1 | convolution fusion | flops 3222535936 | bytes 6297601 | tf_op jit(solution)/shard_map/while/body/eval_jaxpr/dot_general | solution.py:22
  198.5 0.6 add_select_fusion.2
  199.3 1.3 collective-permute-start
  200.6 1.3 collective-permute-start.1
  202.6 22.2 %collective-permute-done = f32[256,1024]{1,0:T(8,128)S(1)} collective-permute-done((f32[256,1024]{1,0:T(8,128)S(1)}, f32[256,1024]{1,0:T(8,128)S(1)}, u32[]{:S(2)}, u32[]{:S(2)}) %collective-permute-start) | collective-permute-done | bytes 1048608 | tf_op jit(solution)/shard_map/while/body/eval_jaxpr/ppermute | solution.py:10
  224.8 6.2 %fusion.39 = (f32[256]{0:T(256)S(1)}, f32[256,1024]{1,0:T(8,128)S(1)}) fusion(f32[1024,1024]{1,0:T(8,128)} %get-tuple-element.499, f32[256,1024]{1,0:T(8,128)S(1)} %collective-permute-done, s32[256]{0:T(256)S(1)} %get-tuple-element.500, f32[1024]{0:T(1024)S(1)} %subtract_exponential_fusion.3, pred[]{:T(512)} %get-tuple-element.496), kind=kOutput, calls=%fused_computation.53.clone.1 | convolution fusion | flops 3222535936 | bytes 6297601 | tf_op jit(solution)/shard_map/while/body/eval_jaxpr/dot_general | solution.py:22
  230.9 0.6 add_select_fusion.2
  231.8 1.3 collective-permute-start
  233.1 1.3 collective-permute-start.1
  235.1 21.2 %collective-permute-done = f32[256,1024]{1,0:T(8,128)S(1)} collective-permute-done((f32[256,1024]{1,0:T(8,128)S(1)}, f32[256,1024]{1,0:T(8,128)S(1)}, u32[]{:S(2)}, u32[]{:S(2)}) %collective-permute-start) | collective-permute-done | bytes 1048608 | tf_op jit(solution)/shard_map/while/body/eval_jaxpr/ppermute | solution.py:10
  256.3 6.2 %fusion.39 = (f32[256]{0:T(256)S(1)}, f32[256,1024]{1,0:T(8,128)S(1)}) fusion(f32[1024,1024]{1,0:T(8,128)} %get-tuple-element.499, f32[256,1024]{1,0:T(8,128)S(1)} %collective-permute-done, s32[256]{0:T(256)S(1)} %get-tuple-element.500, f32[1024]{0:T(1024)S(1)} %subtract_exponential_fusion.3, pred[]{:T(512)} %get-tuple-element.496), kind=kOutput, calls=%fused_computation.53.clone.1 | convolution fusion | flops 3222535936 | bytes 6297601 | tf_op jit(solution)/shard_map/while/body/eval_jaxpr/dot_general | solution.py:22
  262.5 0.6 add_select_fusion.2
  263.4 1.3 collective-permute-start
  264.7 1.3 collective-permute-start.1
  266.6 20.3 %collective-permute-done = f32[256,1024]{1,0:T(8,128)S(1)} collective-permute-done((f32[256,1024]{1,0:T(8,128)S(1)}, f32[256,1024]{1,0:T(8,128)S(1)}, u32[]{:S(2)}, u32[]{:S(2)}) %collective-permute-start) | collective-permute-done | bytes 1048608 | tf_op jit(solution)/shard_map/while/body/eval_jaxpr/ppermute | solution.py:10
  286.9 6.2 %fusion.39 = (f32[256]{0:T(256)S(1)}, f32[256,1024]{1,0:T(8,128)S(1)}) fusion(f32[1024,1024]{1,0:T(8,128)} %get-tuple-element.499, f32[256,1024]{1,0:T(8,128)S(1)} %collective-permute-done, s32[256]{0:T(256)S(1)} %get-tuple-element.500, f32[1024]{0:T(1024)S(1)} %subtract_exponential_fusion.3, pred[]{:T(512)} %get-tuple-element.496), kind=kOutput, calls=%fused_computation.53.clone.1 | convolution fusion | flops 3222535936 | bytes 6297601 | tf_op jit(solution)/shard_map/while/body/eval_jaxpr/dot_general | solution.py:22
  293.1 0.6 add_select_fusion.2
  294.0 1.3 collective-permute-start
  295.3 1.3 collective-permute-start.1
  297.2 19.4 %collective-permute-done = f32[256,1024]{1,0:T(8,128)S(1)} collective-permute-done((f32[256,1024]{1,0:T(8,128)S(1)}, f32[256,1024]{1,0:T(8,128)S(1)}, u32[]{:S(2)}, u32[]{:S(2)}) %collective-permute-start) | collective-permute-done | bytes 1048608 | tf_op jit(solution)/shard_map/while/body/eval_jaxpr/ppermute | solution.py:10
  316.6 6.2 %fusion.39 = (f32[256]{0:T(256)S(1)}, f32[256,1024]{1,0:T(8,128)S(1)}) fusion(f32[1024,1024]{1,0:T(8,128)} %get-tuple-element.499, f32[256,1024]{1,0:T(8,128)S(1)} %collective-permute-done, s32[256]{0:T(256)S(1)} %get-tuple-element.500, f32[1024]{0:T(1024)S(1)} %subtract_exponential_fusion.3, pred[]{:T(512)} %get-tuple-element.496), kind=kOutput, calls=%fused_computation.53.clone.1 | convolution fusion | flops 3222535936 | bytes 6297601 | tf_op jit(solution)/shard_map/while/body/eval_jaxpr/dot_general | solution.py:22
  322.8 0.6 add_select_fusion.2
  (85 shorter events, 13.9 us)
Async XLA Ops:
  7.2 5.4 %copy-start = (f32[256,1024]{1,0:T(8,128)S(1)}, f32[256,1024]{1,0:T(8,128)}, u32[]{:S(2)}) copy-start(f32[256,1024]{1,0:T(8,128)} %param.15) | copy-start | bytes 3145732
  7.2 6.3 %copy-start.2 = (s32[16,4]{0,1:T(4,128)S(1)}, s32[16,4]{0,1:T(4,128)}, u32[]{:S(2)}) copy-start(s32[16,4]{0,1:T(4,128)} %param.12) | copy-start | bytes 772
  7.2 5.4 %copy-start.4 = (s32[4]{0:T(128)S(1)}, s32[4]{0:T(128)}, u32[]{:S(2)}) copy-start(s32[4]{0:T(128)} %param.11) | copy-start | bytes 52
  7.2 5.9 %copy-start.5 = (s32[256]{0:T(256)S(1)}, s32[256]{0:T(256)}, u32[]{:S(2)}) copy-start(s32[256]{0:T(256)} %param.17) | copy-start | bytes 3076
  7.2 6.1 %copy-start.3 = (f32[16,1024]{1,0:T(8,128)S(1)}, f32[16,1024]{1,0:T(8,128)}, u32[]{:S(2)}) copy-start(f32[16,1024]{1,0:T(8,128)} %param.16) | copy-start | bytes 196612
  7.2 75.8 %all-gather.3.cloned.1.call-start = ((), (), s32[]{:S(2)}) async-start(), calls=%async_computation | async-start | bytes 5242880 | tf_op jit(solution)/shard_map/all_gather | solution.py:83
  98.5 27.2 %collective-permute-start = (f32[256,1024]{1,0:T(8,128)S(1)}, f32[256,1024]{1,0:T(8,128)S(1)}, u32[]{:S(2)}, u32[]{:S(2)}) collective-permute-start(f32[256,1024]{1,0:T(8,128)S(1)} %get-tuple-element.483), channel_id=1, source_target_pairs={{0,4},{4,8},{8,12},{12,16},{16,20},{20,24},{24,28},{1,5},{5,9},{9,... | collective-permute-start | bytes 3145736 | tf_op jit(solution)/shard_map/while/body/eval_jaxpr/ppermute | solution.py:10
  99.8 32.1 %collective-permute-start.1 = (f32[256]{0:T(256)S(1)}, f32[256]{0:T(256)S(1)}, u32[]{:S(2)}, u32[]{:S(2)}) collective-permute-start(f32[256]{0:T(256)S(1)} %get-tuple-element.484), channel_id=1, source_target_pairs={{0,4},{4,8},{8,12},{12,16},{16,20},{20,24},{24,28},{1,5},{5,9},{9,... | collective-permute-start | bytes 3080 | tf_op jit(solution)/shard_map/while/body/eval_jaxpr/ppermute | solution.py:10
  132.8 26.4 %collective-permute-start = (f32[256,1024]{1,0:T(8,128)S(1)}, f32[256,1024]{1,0:T(8,128)S(1)}, u32[]{:S(2)}, u32[]{:S(2)}) collective-permute-start(f32[256,1024]{1,0:T(8,128)S(1)} %get-tuple-element.483), channel_id=1, source_target_pairs={{0,4},{4,8},{8,12},{12,16},{16,20},{20,24},{24,28},{1,5},{5,9},{9,... | collective-permute-start | bytes 3145736 | tf_op jit(solution)/shard_map/while/body/eval_jaxpr/ppermute | solution.py:10
  134.1 31.3 %collective-permute-start.1 = (f32[256]{0:T(256)S(1)}, f32[256]{0:T(256)S(1)}, u32[]{:S(2)}, u32[]{:S(2)}) collective-permute-start(f32[256]{0:T(256)S(1)} %get-tuple-element.484), channel_id=1, source_target_pairs={{0,4},{4,8},{8,12},{12,16},{16,20},{20,24},{24,28},{1,5},{5,9},{9,... | collective-permute-start | bytes 3080 | tf_op jit(solution)/shard_map/while/body/eval_jaxpr/ppermute | solution.py:10
  166.2 26.1 %collective-permute-start = (f32[256,1024]{1,0:T(8,128)S(1)}, f32[256,1024]{1,0:T(8,128)S(1)}, u32[]{:S(2)}, u32[]{:S(2)}) collective-permute-start(f32[256,1024]{1,0:T(8,128)S(1)} %get-tuple-element.483), channel_id=1, source_target_pairs={{0,4},{4,8},{8,12},{12,16},{16,20},{20,24},{24,28},{1,5},{5,9},{9,... | collective-permute-start | bytes 3145736 | tf_op jit(solution)/shard_map/while/body/eval_jaxpr/ppermute | solution.py:10
  167.5 30.9 %collective-permute-start.1 = (f32[256]{0:T(256)S(1)}, f32[256]{0:T(256)S(1)}, u32[]{:S(2)}, u32[]{:S(2)}) collective-permute-start(f32[256]{0:T(256)S(1)} %get-tuple-element.484), channel_id=1, source_target_pairs={{0,4},{4,8},{8,12},{12,16},{16,20},{20,24},{24,28},{1,5},{5,9},{9,... | collective-permute-start | bytes 3080 | tf_op jit(solution)/shard_map/while/body/eval_jaxpr/ppermute | solution.py:10
  199.3 25.4 %collective-permute-start = (f32[256,1024]{1,0:T(8,128)S(1)}, f32[256,1024]{1,0:T(8,128)S(1)}, u32[]{:S(2)}, u32[]{:S(2)}) collective-permute-start(f32[256,1024]{1,0:T(8,128)S(1)} %get-tuple-element.483), channel_id=1, source_target_pairs={{0,4},{4,8},{8,12},{12,16},{16,20},{20,24},{24,28},{1,5},{5,9},{9,... | collective-permute-start | bytes 3145736 | tf_op jit(solution)/shard_map/while/body/eval_jaxpr/ppermute | solution.py:10
  200.6 30.3 %collective-permute-start.1 = (f32[256]{0:T(256)S(1)}, f32[256]{0:T(256)S(1)}, u32[]{:S(2)}, u32[]{:S(2)}) collective-permute-start(f32[256]{0:T(256)S(1)} %get-tuple-element.484), channel_id=1, source_target_pairs={{0,4},{4,8},{8,12},{12,16},{16,20},{20,24},{24,28},{1,5},{5,9},{9,... | collective-permute-start | bytes 3080 | tf_op jit(solution)/shard_map/while/body/eval_jaxpr/ppermute | solution.py:10
  231.8 24.5 %collective-permute-start = (f32[256,1024]{1,0:T(8,128)S(1)}, f32[256,1024]{1,0:T(8,128)S(1)}, u32[]{:S(2)}, u32[]{:S(2)}) collective-permute-start(f32[256,1024]{1,0:T(8,128)S(1)} %get-tuple-element.483), channel_id=1, source_target_pairs={{0,4},{4,8},{8,12},{12,16},{16,20},{20,24},{24,28},{1,5},{5,9},{9,... | collective-permute-start | bytes 3145736 | tf_op jit(solution)/shard_map/while/body/eval_jaxpr/ppermute | solution.py:10
  233.1 29.4 %collective-permute-start.1 = (f32[256]{0:T(256)S(1)}, f32[256]{0:T(256)S(1)}, u32[]{:S(2)}, u32[]{:S(2)}) collective-permute-start(f32[256]{0:T(256)S(1)} %get-tuple-element.484), channel_id=1, source_target_pairs={{0,4},{4,8},{8,12},{12,16},{16,20},{20,24},{24,28},{1,5},{5,9},{9,... | collective-permute-start | bytes 3080 | tf_op jit(solution)/shard_map/while/body/eval_jaxpr/ppermute | solution.py:10
  263.4 23.6 %collective-permute-start = (f32[256,1024]{1,0:T(8,128)S(1)}, f32[256,1024]{1,0:T(8,128)S(1)}, u32[]{:S(2)}, u32[]{:S(2)}) collective-permute-start(f32[256,1024]{1,0:T(8,128)S(1)} %get-tuple-element.483), channel_id=1, source_target_pairs={{0,4},{4,8},{8,12},{12,16},{16,20},{20,24},{24,28},{1,5},{5,9},{9,... | collective-permute-start | bytes 3145736 | tf_op jit(solution)/shard_map/while/body/eval_jaxpr/ppermute | solution.py:10
  264.7 28.4 %collective-permute-start.1 = (f32[256]{0:T(256)S(1)}, f32[256]{0:T(256)S(1)}, u32[]{:S(2)}, u32[]{:S(2)}) collective-permute-start(f32[256]{0:T(256)S(1)} %get-tuple-element.484), channel_id=1, source_target_pairs={{0,4},{4,8},{8,12},{12,16},{16,20},{20,24},{24,28},{1,5},{5,9},{9,... | collective-permute-start | bytes 3080 | tf_op jit(solution)/shard_map/while/body/eval_jaxpr/ppermute | solution.py:10
  294.0 22.6 %collective-permute-start = (f32[256,1024]{1,0:T(8,128)S(1)}, f32[256,1024]{1,0:T(8,128)S(1)}, u32[]{:S(2)}, u32[]{:S(2)}) collective-permute-start(f32[256,1024]{1,0:T(8,128)S(1)} %get-tuple-element.483), channel_id=1, source_target_pairs={{0,4},{4,8},{8,12},{12,16},{16,20},{20,24},{24,28},{1,5},{5,9},{9,... | collective-permute-start | bytes 3145736 | tf_op jit(solution)/shard_map/while/body/eval_jaxpr/ppermute | solution.py:10
  295.3 27.5 %collective-permute-start.1 = (f32[256]{0:T(256)S(1)}, f32[256]{0:T(256)S(1)}, u32[]{:S(2)}, u32[]{:S(2)}) collective-permute-start(f32[256]{0:T(256)S(1)} %get-tuple-element.484), channel_id=1, source_target_pairs={{0,4},{4,8},{8,12},{12,16},{16,20},{20,24},{24,28},{1,5},{5,9},{9,... | collective-permute-start | bytes 3080 | tf_op jit(solution)/shard_map/while/body/eval_jaxpr/ppermute | solution.py:10
  323.6 1.0 copy-start.1
Sparse Core Ops, SparseCore 0:
  47.5 35.4 all-gather.2
where the time goes:
time: 335 us; the launch traced here: 331 us
  waiting for transfers between devices  182 us (54%)
  matrix products  65.4 us (20%)
  other arithmetic  24.1 us (7%)
  local copies, waits for them, and re-layouts  21.5 us (6%)
  starting transfers between devices  18.1 us (5%)
  between operations  14.2 us (4%)
  blocking collectives  5.07 us (2%)
    ppermute x14, waiting for transfers between devices, passed_along(): return lax.ppermute(block, axis, route)  153 us
    dot_general x8, matrix products, combine(): jnp.dot(scaled, right_r, precision=lax.Precision.HIGHEST, preferred_eleme...  52.4 us
    all_gather x1, waiting for transfers between devices, body(): lax.all_gather(own_r, 'rows', axis=0, tiled=True)  29.2 us
    ppermute x14, starting transfers between devices, passed_along(): return lax.ppermute(block, axis, route)  18.1 us
    dot_general x4, matrix products, advance(): jnp.einsum('rjc,jcd->rjd', picked, moved_flat, preferred_element_type=jnp...  12.1 us
    gather x4, local copies, waits for them, and re-layouts, advance(): picked = current.reshape(n_local, n_blocks, block_size)[:, pattern, :]  8.08 us
  transfers between devices with their start and end apart: 15, of which 8 were waited for; matrix products, arithmetic and copies ran while one was open for 15% of the time, Pallas kernels for 0%

commit v1 on v0

v1 whole, which is shorter than its diff:
```python
import functools

import jax
import jax.numpy as jnp
from jax import lax
from jax.experimental import pallas as pl
from jax.experimental.pallas import tpu as pltpu
from jax.sharding import PartitionSpec as P

LANES = 128
WIDTH = 256


def build_kernel(pattern_ref, blocks_ref, leave_ref, dense_ref, leave_col_ref):
    n_blocks, n_source, size, _ = blocks_ref.shape
    n_states = leave_ref.shape[1]
    leave_col_ref[...] = jnp.broadcast_to(leave_ref[...], (LANES, n_states)).T
    dense_ref[...] = jnp.zeros_like(dense_ref)
    per_tile = LANES // size
    lane = lax.broadcasted_iota(jnp.int32, (size, LANES), 1)
    sub = lax.broadcasted_iota(jnp.int32, (size, LANES), 0)
    for j in range(n_blocks):
        place = (lane == sub + size * (j % per_tile)).astype(jnp.bfloat16)
        tile = pl.ds(LANES * (j // per_tile), LANES)
        for k in range(n_source):
            rows = pl.ds(pl.multiple_of(pattern_ref[j, k] * size, size), size)
            block = jnp.dot(blocks_ref[j, k], place, preferred_element_type=jnp.float32)
            moved = (block * leave_col_ref[rows, :]).astype(jnp.bfloat16)
            dense_ref[rows, tile] = dense_ref[rows, tile] + moved


def shifted(x, size):
    lane = lax.broadcasted_iota(jnp.int32, x.shape, 1)
    return jnp.where(lane % size == 0, pltpu.roll(x, LANES - size + 1, 1), pltpu.roll(x, 1, 1))


def chain_kernel(
    steps,
    size,
    place_ref,
    observed_ref,
    cluster_ref,
    symbol_ref,
    cluster_emit_ref,
    leave_ref,
    dense_ref,
    rows_ref,
    rate_ref,
    cur_ref,
    low_ref,
    log_ref,
):
    n_rows, n_states = cur_ref.shape
    n_segments = place_ref[0]
    row_start = place_ref[1]
    row = lax.broadcasted_iota(jnp.int32, (n_rows, n_states), 0) + row_start
    col = lax.broadcasted_iota(jnp.int32, (n_rows, n_states), 1)
    start = (row == col).astype(jnp.float32)
    cur_ref[...] = start
    low_ref[0] = start.astype(jnp.bfloat16)
    log_ref[...] = jnp.zeros_like(log_ref)

    def segment(g, _):
        for s in range(steps):
            now, later = s % 2, (s + 1) % 2
            symbol = observed_ref[g * steps + s]
            emission = symbol_ref[pl.ds(symbol, 1), :]
            emission = emission * cluster_emit_ref[pl.ds(cluster_ref[symbol], 1), :]
            low = low_ref[now]
            total = None
            for n in range(n_states // WIDTH):
                cols = pl.ds(n * WIDTH, WIDTH)
                moved = jnp.dot(low, dense_ref[:, cols], preferred_element_type=jnp.float32)
                for h in range(WIDTH // LANES):
                    at = n * WIDTH + h * LANES
                    part = pl.ds(at, LANES)
                    kept = cur_ref[:, part] * (1.0 - leave_ref[:, part])
                    new = shifted(kept, size) + moved[:, h * LANES : (h + 1) * LANES]
                    new = new * emission[:, at : at + LANES]
                    cur_ref[:, part] = new
                    if s < steps - 1:
                        low_ref[later, :, part] = new.astype(jnp.bfloat16)
                    else:
                        total = new if total is None else total + new
        row_sum = jnp.sum(total, axis=1, keepdims=True)
        scale = n_states / row_sum
        log_ref[...] = log_ref[...] + jnp.log(row_sum / n_states)
        for n in range(n_states // LANES):
            part = pl.ds(n * LANES, LANES)
            new = cur_ref[:, part] * scale
            cur_ref[:, part] = new
            low_ref[0, :, part] = new.astype(jnp.bfloat16)
        return 0

    lax.fori_loop(0, n_segments, segment, 0)
    rows_ref[0] = cur_ref[...]
    divisor = (n_segments * steps).astype(jnp.float32)
    rate_ref[...] = (log_ref[...] / divisor).T[0:1, :]


def body(observed, pattern, trans_blocks, leave_rate, symbol_emit, cluster_emit, symbol_cluster):
    size = trans_blocks.shape[-1]
    n_states = leave_rate.shape[0]
    steps = observed.shape[0]
    n_rows = n_states // lax.axis_size("rows")
    all_observed = lax.all_gather(observed, "tm", axis=0, tiled=True)
    leave_row = leave_rate.reshape(1, n_states)
    vmem = pl.BlockSpec(memory_space=pltpu.VMEM)
    smem = pl.BlockSpec(memory_space=pltpu.SMEM)
    dense = pl.pallas_call(
        build_kernel,
        out_shape=jax.ShapeDtypeStruct((n_states, n_states), jnp.bfloat16),
        in_specs=[smem, vmem, vmem],
        out_specs=vmem,
        scratch_shapes=[pltpu.VMEM((n_states, LANES), jnp.float32)],
        compiler_params=pltpu.CompilerParams(vmem_limit_bytes=32 << 20),
        cost_estimate=pl.CostEstimate(flops=1 << 30, bytes_accessed=4 << 20, transcendentals=0),
        name="build",
    )(pattern, trans_blocks, leave_row)
    place = jnp.stack([lax.axis_index("tm") + 1, lax.axis_index("rows") * n_rows]).astype(jnp.int32)
    return pl.pallas_call(
        functools.partial(chain_kernel, steps, size),
        out_shape=[
            jax.ShapeDtypeStruct((1, n_rows, n_states), jnp.float32),
            jax.ShapeDtypeStruct((1, n_rows), jnp.float32),
        ],
        in_specs=[smem, smem, smem, vmem, vmem, vmem, vmem],
        out_specs=[vmem, vmem],
        scratch_shapes=[
            pltpu.VMEM((n_rows, n_states), jnp.float32),
            pltpu.VMEM((2, n_rows, n_states), jnp.bfloat16),
            pltpu.VMEM((n_rows, LANES), jnp.float32),
        ],
        compiler_params=pltpu.CompilerParams(vmem_limit_bytes=32 << 20),
        cost_estimate=pl.CostEstimate(flops=1 << 34, bytes_accessed=4 << 20, transcendentals=0),
        name="chain",
    )(place, all_observed, symbol_cluster, symbol_emit, cluster_emit, leave_row, dense)


def solution(mesh):
    in_specs = (P("tm"), P(), P(), P(), P(), P(), P())
    out_specs = (P("tm", "rows", None), P("tm", "rows"))
    return jax.shard_map(body, mesh=mesh, in_specs=in_specs, out_specs=out_specs, check_vma=False)
```

time: 335 us -> 41 us (0.12)
  waiting for transfers between devices: 182 us -> 0 us
  matrix products: 65.4 us -> 0 us
  Pallas kernels: 0 us -> 26.3 us
  other arithmetic: 24.1 us -> 0.08 us
  starting transfers between devices: 18.1 us -> 0 us
  local copies, waits for them, and re-layouts: 21.5 us -> 4.78 us
  between operations: 14.2 us -> 1.34 us
    ppermute x14 -> x0, waiting for transfers between devices: 153 us -> none  [passed_along(): return lax.ppermute(block, axis, route)]
    dot_general x15 -> x0, matrix products: 65.4 us -> none  [the longest x8 52.4 us: combine(): jnp.dot(scaled, right_r, precision=lax.Precision.HIGHEST, preferred_eleme...]
    all_gather x1 -> x0, waiting for transfers between devices: 29.2 us -> none  [body(): lax.all_gather(own_r, 'rows', axis=0, tiled=True)]
    pallas_call x0 -> x2, Pallas kernels: none -> 26.3 us  [the longest x1 24.7 us: body(): pl.pallas_call(functools.partial(chain_kernel, steps, size), out_shape=[j...]
    ppermute x14 -> x0, starting transfers between devices: 18.1 us -> none  [passed_along(): return lax.ppermute(block, axis, route)]
    convert_element_type x7 -> x0, other arithmetic: 8.73 us -> none  [the longest x4 5.72 us: advance(): return ((new_r.astype(jnp.bfloat16), new_l), None)]
    gather x5 -> x0, local copies, waits for them, and re-layouts: 8.68 us -> none  [the longest x4 8.08 us: advance(): picked = current.reshape(n_local, n_blocks, block_size)[:, pattern, :]]
    unnamed x0 -> x1, blocking collectives: none -> 8.23 us
  transfers between devices with their start and end apart: 15 -> 0, of which waited for: 8 -> 0; matrix products, arithmetic and copies ran while one was open for 15% -> 0% of each run, Pallas kernels for 0% -> 0%
where the time goes in v1:
time: 41 us; the launch traced here: 40.7 us
  Pallas kernels  26.3 us (64%)
  blocking collectives  8.23 us (20%)
  local copies, waits for them, and re-layouts  4.78 us (12%)
  between operations  1.34 us (3%)
    pallas_call x1, Pallas kernels, body(): pl.pallas_call(functools.partial(chain_kernel, steps, size), out_shape=[j...  24.7 us
    unnamed x1, blocking collectives  8.23 us
    unnamed x14, local copies, waits for them, and re-layouts  4.78 us
    pallas_call x1, Pallas kernels, body(): pl.pallas_call(build_kernel, out_shape=jax.ShapeDtypeStruct((n_states, n_...  1.63 us

profile of v1, /device:TPU:26, one launch (start us, length us, event | category | flops | bytes accessed | tf_op | source)
XLA Modules:
  0.0 40.7 jit_solution(3931316041606122528)
XLA Ops:
  0.6 0.0 copy-start.4
  0.6 0.1 pad_add_fusion.place_ref
  0.7 1.2 %dynamic-slice = u32[1]{0:T(128)} dynamic-slice(u32[32]{0:T(128)} %constant.16, u32[]{:T(128)S(6)} %add.4), dynamic_slice_sizes={1} | dynamic-slice | bytes 12
  2.6 0.9 %dynamic-update-slice = s32[32]{0:T(128)S(1)} dynamic-update-slice(s32[32]{0:T(128)S(1)} %broadcast, s32[4]{0:T(128)} %param.7, u32[]{:T(128)} %bitcast.2) | dynamic-update-slice | bytes 36
  3.5 8.2 %all-reduce.observed_ref = s32[32]{0:T(128)S(1)} all-reduce(s32[32]{0:T(128)S(1)} %dynamic-update-slice), channel_id=1, replica_groups=mesh['tm'=8,'rows'=4] {'tm'}, use_global_device_ids=true, to_apply=%add | all-reduce | flops 32 | bytes 256
  11.7 0.8 %copy.9.pattern_ref = s32[16,4]{1,0:T(8,128)S(1)} copy(s32[16,4]{0,1:T(4,128)} %param.8) | data formatting | bytes 512 | tf_op args[1]
  12.5 0.0 copy-start
  12.5 1.2 %copy-done = bf16[16,4,64,64]{3,2,1,0:T(8,128)(2,1)S(1)} copy-done((bf16[16,4,64,64]{3,2,1,0:T(8,128)(2,1)S(1)}, bf16[16,4,64,64]{3,2,1,0:T(8,128)(2,1)}, u32[]{:S(2)}) %copy-start) | copy-done | bytes 524312
  13.7 0.0 copy-start.3
  13.7 0.7 %copy-done.3 = f32[1024]{0:T(1024)S(1)} copy-done((f32[1024]{0:T(1024)S(1)}, f32[1024]{0:T(1024)}, u32[]{:S(2)}) %copy-start.3) | copy-done | bytes 4120
  14.4 0.0 copy-start.1
  14.4 0.0 copy-start.2
  14.4 1.6 %build.1.dense_ref = bf16[1024,1024]{1,0:T(8,128)(2,1)S(1)} custom-call(s32[16,4]{1,0:T(8,128)S(1)} %copy.9.pattern_ref, bf16[16,4,64,64]{3,2,1,0:T(8,128)(2,1)S(1)} %copy-done, f32[1,1024]{1,0:T(1,128)S(1)} %bitcast.4), custom_call_target="tpu_custom_call" | custom-call | flops 1073741824 | bytes 4194304 | tf_op jit(solution)/shard_map/build/pallas_call | solution.py:110
  16.0 0.0 copy-done.4
  16.0 0.0 copy-done.1
  16.0 0.0 copy-done.2
  16.1 24.7 %chain.1 = (f32[1,256,1024]{2,1,0:T(8,128)}, f32[1,256]{1,0:T(1,128)}) custom-call(s32[2]{0:T(128)S(1)} %pad_add_fusion.place_ref, s32[32]{0:T(128)S(1)} %all-reduce.observed_ref, s32[256]{0:T(256)S(1)} %copy-done.4, f32[256,1024]{1,0:T(8,128)S(1)} %copy-done.1, f32[16,1024]{1,0:T(8,128)S(1)} %copy-done.2, f32[1,1024]{1,0:T(1,128)S(1)} %bitcast.5, ...), custom_call_target="tpu_custom_call" | custom-call | flops 17179869184 | bytes 4194304 | tf_op jit(solution)/shard_map/chain/pallas_call | solution.py:121
  (1 shorter events, 0.0 us)
Async XLA Ops:
  0.6 15.4 %copy-start.4 = (s32[256]{0:T(256)S(1)}, s32[256]{0:T(256)}, u32[]{:S(2)}) copy-start(s32[256]{0:T(256)} %cluster_ref.1) | copy-start | bytes 3076
  12.5 1.2 %copy-start = (bf16[16,4,64,64]{3,2,1,0:T(8,128)(2,1)S(1)}, bf16[16,4,64,64]{3,2,1,0:T(8,128)(2,1)}, u32[]{:S(2)}) copy-start(bf16[16,4,64,64]{3,2,1,0:T(8,128)(2,1)} %blocks_ref.1) | copy-start | bytes 1572868
  13.7 0.7 %copy-start.3 = (f32[1024]{0:T(1024)S(1)}, f32[1024]{0:T(1024)}, u32[]{:S(2)}) copy-start(f32[1024]{0:T(1024)} %param.10) | copy-start | bytes 12292
  14.4 1.7 %copy-start.1 = (f32[256,1024]{1,0:T(8,128)S(1)}, f32[256,1024]{1,0:T(8,128)}, u32[]{:S(2)}) copy-start(f32[256,1024]{1,0:T(8,128)} %symbol_ref.1) | copy-start | bytes 3145732
  14.4 1.7 %copy-start.2 = (f32[16,1024]{1,0:T(8,128)S(1)}, f32[16,1024]{1,0:T(8,128)}, u32[]{:S(2)}) copy-start(f32[16,1024]{1,0:T(8,128)} %cluster_emit_ref.1) | copy-start | bytes 196612

commit v2 on v1

v2 whole, which is shorter than its diff:
```python
import functools

import jax
import jax.numpy as jnp
from jax import lax
from jax.experimental import pallas as pl
from jax.experimental.pallas import tpu as pltpu
from jax.sharding import PartitionSpec as P

LANES = 128
SUBLANES = 8


def column(row):
    return jnp.broadcast_to(row, (LANES, row.shape[1])).T


def build_kernel(pattern_ref, blocks_ref, leave_ref, weight_ref, stay_ref, leave_col_ref):
    n_blocks, n_source, size, _ = blocks_ref.shape
    n_states = leave_ref.shape[1]
    leave_col = column(leave_ref[...])
    leave_col_ref[...] = leave_col
    for j in range(n_blocks):
        own = leave_col[j * size : (j + 1) * size]
        stay_ref[j * size : (j + 1) * size, :] = 1.0 - pltpu.roll(own, 1, 0)
    for j in range(n_blocks):
        parts = []
        for k in range(n_source):
            rows = pl.ds(pl.multiple_of(pattern_ref[j, k] * size, size), size)
            parts.append(blocks_ref[j, k].astype(jnp.float32) * leave_col_ref[rows, :size])
        moved = jnp.concatenate(parts, axis=0)
        weight_ref[j] = moved.T.astype(jnp.bfloat16)


def chain_kernel(
    steps,
    size,
    place_ref,
    observed_ref,
    cluster_ref,
    pattern_ref,
    symbol_ref,
    cluster_emit_ref,
    weight_ref,
    stay_ref,
    rows_ref,
    rate_ref,
    cur_ref,
    low_ref,
    emit_ref,
    emit_col_ref,
):
    n_half, n_blocks, padded, _ = cur_ref.shape
    n_states = n_blocks * size
    n_rows = n_half * LANES
    n_source = pattern_ref.shape[1]
    first = padded - size
    n_segments = place_ref[0]
    row_start = place_ref[1]

    def store(now, j, h, new):
        cur_ref[h, j, first:, :] = new
        cur_ref[h, j, first - 1 : first, :] = new[size - 1 :, :]
        low_ref[now, j * size : (j + 1) * size, h * LANES : (h + 1) * LANES] = new.astype(jnp.bfloat16)

    state = lax.broadcasted_iota(jnp.int32, (size, LANES), 0)
    row = lax.broadcasted_iota(jnp.int32, (size, LANES), 1)
    for j in range(n_blocks):
        for h in range(n_half):
            start = state + j * size == row + (row_start + h * LANES)
            store(0, j, h, start.astype(jnp.float32))
    emit_ref[...] = jnp.zeros_like(emit_ref)

    def segment(g, carried):
        scale, log_scale = carried
        for s in range(steps):
            symbol = observed_ref[g * steps + s]
            emission = symbol_ref[pl.ds(symbol, 1), :]
            emission = emission * cluster_emit_ref[pl.ds(cluster_ref[symbol], 1), :]
            emit_ref[s : s + 1, :] = emission
        emit_col_ref[...] = emit_ref[...].T
        sums = [jnp.zeros((SUBLANES, LANES), jnp.float32) for _ in range(n_half)]
        for s in range(steps):
            turn = s if steps % 2 == 0 else g * steps + s
            now, later = turn % 2, (turn + 1) % 2
            for j in range(n_blocks):
                states = slice(j * size, (j + 1) * size)
                picked = [
                    low_ref[now, pl.ds(pl.multiple_of(pattern_ref[j, k] * size, size), size), :]
                    for k in range(n_source)
                ]
                moved = jnp.dot(
                    weight_ref[j],
                    jnp.concatenate(picked, axis=0),
                    preferred_element_type=jnp.float32,
                )
                emission = jnp.broadcast_to(emit_col_ref[states, s : s + 1], (size, LANES))
                stay = stay_ref[states, :]
                for h in range(n_half):
                    part = slice(h * LANES, (h + 1) * LANES)
                    kept = cur_ref[h, j, first - 1 : padded - 1, :] * stay
                    new = (kept + moved[:, part]) * emission
                    if s == 0:
                        new = new * scale[:, part]
                    store(later, j, h, new)
                    if s == steps - 1:
                        sums[h] = sums[h] + jnp.sum(new.reshape(-1, SUBLANES, LANES), axis=0)
        row_sum = jnp.concatenate([jnp.sum(t, axis=0, keepdims=True) for t in sums], axis=1)
        return 1.0 / row_sum, log_scale + jnp.log(row_sum)

    ones = jnp.ones((1, n_rows), jnp.float32)
    scale, log_scale = lax.fori_loop(0, n_segments, segment, (ones, jnp.zeros_like(ones)))
    scale = scale * n_states
    for j in range(n_blocks * size // LANES):
        per = LANES // size
        for h in range(n_half):
            part = slice(h * LANES, (h + 1) * LANES)
            block = [cur_ref[h, j * per + i, first:, :] for i in range(per)]
            block = jnp.concatenate(block, axis=0) * scale[:, part]
            rows_ref[0, part, j * LANES : (j + 1) * LANES] = block.T
    divisor = (n_segments * steps).astype(jnp.float32)
    rate_ref[...] = (log_scale - jnp.log(jnp.full_like(ones, n_states))) / divisor


def body(observed, pattern, trans_blocks, leave_rate, symbol_emit, cluster_emit, symbol_cluster):
    n_blocks, n_source, size, _ = trans_blocks.shape
    n_states = leave_rate.shape[0]
    steps = observed.shape[0]
    n_rows = n_states // lax.axis_size("rows")
    all_observed = lax.all_gather(observed, "tm", axis=0, tiled=True)
    leave_row = leave_rate.reshape(1, n_states)
    vmem = pl.BlockSpec(memory_space=pltpu.VMEM)
    smem = pl.BlockSpec(memory_space=pltpu.SMEM)
    weight, stay = pl.pallas_call(
        build_kernel,
        out_shape=[
            jax.ShapeDtypeStruct((n_blocks, size, n_source * size), jnp.bfloat16),
            jax.ShapeDtypeStruct((n_states, LANES), jnp.float32),
        ],
        in_specs=[smem, vmem, vmem],
        out_specs=[vmem, vmem],
        scratch_shapes=[pltpu.VMEM((n_states, LANES), jnp.float32)],
        compiler_params=pltpu.CompilerParams(vmem_limit_bytes=32 << 20),
        cost_estimate=pl.CostEstimate(flops=1 << 30, bytes_accessed=4 << 20, transcendentals=0),
        name="build",
    )(pattern, trans_blocks, leave_row)
    place = jnp.stack([lax.axis_index("tm") + 1, lax.axis_index("rows") * n_rows]).astype(jnp.int32)
    return pl.pallas_call(
        functools.partial(chain_kernel, steps, size),
        out_shape=[
            jax.ShapeDtypeStruct((1, n_rows, n_states), jnp.float32),
            jax.ShapeDtypeStruct((1, n_rows), jnp.float32),
        ],
        in_specs=[smem, smem, smem, smem, vmem, vmem, vmem, vmem],
        out_specs=[vmem, vmem],
        scratch_shapes=[
            pltpu.VMEM((n_rows // LANES, n_blocks, size + SUBLANES, LANES), jnp.float32),
            pltpu.VMEM((2, n_states, n_rows), jnp.bfloat16),
            pltpu.VMEM((LANES, n_states), jnp.float32),
            pltpu.VMEM((n_states, LANES), jnp.float32),
        ],
        compiler_params=pltpu.CompilerParams(vmem_limit_bytes=32 << 20),
        cost_estimate=pl.CostEstimate(flops=1 << 34, bytes_accessed=4 << 20, transcendentals=0),
        name="chain",
    )(place, all_observed, symbol_cluster, pattern, symbol_emit, cluster_emit, weight, stay)


def solution(mesh):
    in_specs = (P("tm"), P(), P(), P(), P(), P(), P())
    out_specs = (P("tm", "rows", None), P("tm", "rows"))
    return jax.shard_map(body, mesh=mesh, in_specs=in_specs, out_specs=out_specs, check_vma=False)
```

time: 41 us -> 104 us (2.54)
  Pallas kernels: 26.3 us -> 89.1 us
    pallas_call x1, Pallas kernels: 24.7 us -> 87.9 us  [body(): pl.pallas_call(functools.partial(chain_kernel, steps, size), out_shape=[j...]
    unnamed x14 -> x20, local copies, waits for them, and re-layouts: 4.78 us -> 4.56 us
where the time goes in v2:
time: 104 us; the launch traced here: 103 us
  Pallas kernels  89.1 us (86%)
  blocking collectives  8.23 us (8%)
  local copies, waits for them, and re-layouts  4.56 us (4%)
  between operations  1.35 us (1%)
    pallas_call x1, Pallas kernels, body(): pl.pallas_call(functools.partial(chain_kernel, steps, size), out_shape=[j...  87.9 us
    unnamed x1, blocking collectives  8.23 us
    unnamed x20, local copies, waits for them, and re-layouts  4.56 us

profile of v2, /device:TPU:26, one launch (start us, length us, event | category | flops | bytes accessed | tf_op | source)
XLA Modules:
  0.0 103.3 jit_solution(13460931011204380957)
XLA Ops:
  0.6 0.0 copy-start.7
  0.7 0.1 pad_add_fusion.place_ref
  0.7 0.6 copy-done.7
  1.3 0.6 dynamic-slice
  2.5 0.0 copy-start.6
  2.6 0.6 copy-done.6
  3.2 0.0 copy-start.5
  3.2 0.2 dynamic-update-slice
  3.4 8.2 %all-reduce.observed_ref = s32[32]{0:T(128)S(1)} all-reduce(s32[32]{0:T(128)S(1)} %dynamic-update-slice), channel_id=1, replica_groups=mesh['tm'=8,'rows'=4] {'tm'}, use_global_device_ids=true, to_apply=%add | all-reduce | flops 32 | bytes 256
  11.6 0.0 copy-done.5
  11.6 0.0 copy-start.3
  11.6 0.1 copy.10.pattern_ref
  11.7 0.6 copy-done.3
  12.3 0.0 copy-start
  12.3 1.2 %copy-done = bf16[16,4,64,64]{3,2,1,0:T(8,128)(2,1)S(1)} copy-done((bf16[16,4,64,64]{3,2,1,0:T(8,128)(2,1)S(1)}, bf16[16,4,64,64]{3,2,1,0:T(8,128)(2,1)}, u32[]{:S(2)}) %copy-start) | copy-done | bytes 524312
  13.5 0.0 copy-start.1
  13.5 0.0 copy-start.2
  13.5 1.2 %build.1 = (bf16[16,64,256]{2,1,0:T(8,128)(2,1)S(1)}, f32[1024,128]{1,0:T(8,128)S(1)}) custom-call(s32[16,4]{1,0:T(8,128)S(1)} %copy.10.pattern_ref, bf16[16,4,64,64]{3,2,1,0:T(8,128)(2,1)S(1)} %copy-done, f32[1,1024]{1,0:T(1,128)S(1)} %bitcast.4), custom_call_target="tpu_custom_call" | custom-call | flops 1073741824 | bytes 4194304 | tf_op jit(solution)/shard_map/build/pallas_call | solution.py:134
  14.7 0.0 copy-start.4
  14.7 0.0 copy-done.1
  14.8 0.0 copy-done.2
  14.8 0.7 copy-done.4
  15.4 87.9 %chain.1 = (f32[1,256,1024]{2,1,0:T(8,128)}, f32[1,256]{1,0:T(1,128)}) custom-call(s32[2]{0:T(128)S(1)} %pad_add_fusion.place_ref, s32[32]{0:T(128)S(1)} %all-reduce.observed_ref, s32[256]{0:T(256)S(1)} %copy-done.4, s32[16,4]{1,0:T(8,128)S(1)} %copy.10.pattern_ref, f32[256,1024]{1,0:T(8,128)S(1)} %copy-done.1, f32[16,1024]{1,0:T(8,128)S(1)} %copy-done.2, ...), custom_call_target="tpu_custom_call" | custom-call | flops 17179869184 | bytes 4194304 | tf_op jit(solution)/shard_map/chain/pallas_call | solution.py:148
  (1 shorter events, 0.0 us)
Async XLA Ops:
  0.6 0.7 copy-start.7
  2.5 0.7 copy-start.6
  3.2 8.4 %copy-start.5 = (s32[16,4]{0,1:T(4,128)S(1)}, s32[16,4]{0,1:T(4,128)}, u32[]{:S(2)}) copy-start(s32[16,4]{0,1:T(4,128)} %param.8) | copy-start | bytes 772
  11.6 0.7 copy-start.3
  12.3 1.2 %copy-start = (bf16[16,4,64,64]{3,2,1,0:T(8,128)(2,1)S(1)}, bf16[16,4,64,64]{3,2,1,0:T(8,128)(2,1)}, u32[]{:S(2)}) copy-start(bf16[16,4,64,64]{3,2,1,0:T(8,128)(2,1)} %blocks_ref.1) | copy-start | bytes 1572868
  13.5 1.2 %copy-start.1 = (f32[256,1024]{1,0:T(8,128)S(1)}, f32[256,1024]{1,0:T(8,128)}, u32[]{:S(2)}) copy-start(f32[256,1024]{1,0:T(8,128)} %symbol_ref.1) | copy-start | bytes 3145732
  13.5 1.2 %copy-start.2 = (f32[16,1024]{1,0:T(8,128)S(1)}, f32[16,1024]{1,0:T(8,128)}, u32[]{:S(2)}) copy-start(f32[16,1024]{1,0:T(8,128)} %cluster_emit_ref.1) | copy-start | bytes 196612
  14.7 0.7 copy-start.4

commit v3 on v2

--- a/solution.py
+++ b/solution.py
@@ -46,7 +46,8 @@
     rows_ref,
     rate_ref,
     cur_ref,
-    low_ref,
+    low_a_ref,
+    low_b_ref,
     emit_ref,
     emit_col_ref,
 ):
@@ -58,17 +59,19 @@
     n_segments = place_ref[0]
     row_start = place_ref[1]
 
-    def store(now, j, h, new):
+    lows = (low_a_ref, low_b_ref)
+
+    def store(low_ref, j, h, new):
         cur_ref[h, j, first:, :] = new
         cur_ref[h, j, first - 1 : first, :] = new[size - 1 :, :]
-        low_ref[now, j * size : (j + 1) * size, h * LANES : (h + 1) * LANES] = new.astype(jnp.bfloat16)
+        low_ref[j * size : (j + 1) * size, h * LANES : (h + 1) * LANES] = new.astype(jnp.bfloat16)
 
     state = lax.broadcasted_iota(jnp.int32, (size, LANES), 0)
     row = lax.broadcasted_iota(jnp.int32, (size, LANES), 1)
     for j in range(n_blocks):
         for h in range(n_half):
             start = state + j * size == row + (row_start + h * LANES)
-            store(0, j, h, start.astype(jnp.float32))
+            store(low_a_ref, j, h, start.astype(jnp.float32))
     emit_ref[...] = jnp.zeros_like(emit_ref)
 
     def segment(g, carried):
@@ -81,12 +84,11 @@
         emit_col_ref[...] = emit_ref[...].T
         sums = [jnp.zeros((SUBLANES, LANES), jnp.float32) for _ in range(n_half)]
         for s in range(steps):
-            turn = s if steps % 2 == 0 else g * steps + s
-            now, later = turn % 2, (turn + 1) % 2
+            now, later = lows[s % 2], lows[(s + 1) % 2]
             for j in range(n_blocks):
                 states = slice(j * size, (j + 1) * size)
                 picked = [
-                    low_ref[now, pl.ds(pl.multiple_of(pattern_ref[j, k] * size, size), size), :]
+                    now[pl.ds(pl.multiple_of(pattern_ref[j, k] * size, size), size), :]
                     for k in range(n_source)
                 ]
                 moved = jnp.dot(
@@ -105,6 +107,8 @@
                     store(later, j, h, new)
                     if s == steps - 1:
                         sums[h] = sums[h] + jnp.sum(new.reshape(-1, SUBLANES, LANES), axis=0)
+        if steps % 2:
+            low_a_ref[...] = low_b_ref[...]
         row_sum = jnp.concatenate([jnp.sum(t, axis=0, keepdims=True) for t in sums], axis=1)
         return 1.0 / row_sum, log_scale + jnp.log(row_sum)
 
@@ -155,7 +159,8 @@
         out_specs=[vmem, vmem],
         scratch_shapes=[
             pltpu.VMEM((n_rows // LANES, n_blocks, size + SUBLANES, LANES), jnp.float32),
-            pltpu.VMEM((2, n_states, n_rows), jnp.bfloat16),
+            pltpu.VMEM((n_states, n_rows), jnp.bfloat16),
+            pltpu.VMEM((n_states, n_rows), jnp.bfloat16),
             pltpu.VMEM((LANES, n_states), jnp.float32),
             pltpu.VMEM((n_states, LANES), jnp.float32),
         ],

time: 104 us -> 36.1 us (0.35)
  Pallas kernels: 89.1 us -> 21.6 us
    pallas_call x1, Pallas kernels: 87.9 us -> 20.4 us  [body(): pl.pallas_call(functools.partial(chain_kernel, steps, size), out_shape=[j...]
where the time goes in v3:
time: 36.1 us; the launch traced here: 35.8 us
  Pallas kernels  21.6 us (60%)
  blocking collectives  8.23 us (23%)
  local copies, waits for them, and re-layouts  4.56 us (13%)
  between operations  1.35 us (4%)
    pallas_call x1, Pallas kernels, body(): pl.pallas_call(functools.partial(chain_kernel, steps, size), out_shape=[j...  20.4 us
    unnamed x1, blocking collectives  8.23 us
    unnamed x20, local copies, waits for them, and re-layouts  4.56 us
    pallas_call x1, Pallas kernels, body(): pl.pallas_call(build_kernel, out_shape=[jax.ShapeDtypeStruct((n_blocks, s...  1.2 us

profile of v3, /device:TPU:26, one launch (start us, length us, event | category | flops | bytes accessed | tf_op | source)
XLA Modules:
  0.0 35.8 jit_solution(12957423681121365919)
XLA Ops:
  0.6 0.0 copy-start.7
  0.7 0.1 pad_add_fusion.place_ref
  0.7 0.6 %copy-done.7 = u32[32]{0:T(128)S(1)} copy-done((u32[32]{0:T(128)S(1)}, u32[32]{0:T(128)}, u32[]{:S(2)}) %copy-start.7) | copy-done | bytes 152
  1.3 0.6 %dynamic-slice = u32[1]{0:T(128)} dynamic-slice(u32[32]{0:T(128)S(1)} %copy-done.7, u32[]{:T(128)S(6)} %add.4), dynamic_slice_sizes={1} | dynamic-slice | bytes 12
  2.5 0.0 copy-start.6
  2.6 0.6 %copy-done.6 = s32[4]{0:T(128)S(1)} copy-done((s32[4]{0:T(128)S(1)}, s32[4]{0:T(128)}, u32[]{:S(2)}) %copy-start.6) | copy-done | bytes 40
  3.2 0.0 copy-start.5
  3.2 0.2 dynamic-update-slice
  3.4 8.2 %all-reduce.observed_ref = s32[32]{0:T(128)S(1)} all-reduce(s32[32]{0:T(128)S(1)} %dynamic-update-slice), channel_id=1, replica_groups=mesh['tm'=8,'rows'=4] {'tm'}, use_global_device_ids=true, to_apply=%add | all-reduce | flops 32 | bytes 256
  11.6 0.0 copy-done.5
  11.6 0.0 copy-start.3
  11.6 0.1 copy.10.pattern_ref
  11.7 0.6 %copy-done.3 = f32[1024]{0:T(1024)S(1)} copy-done((f32[1024]{0:T(1024)S(1)}, f32[1024]{0:T(1024)}, u32[]{:S(2)}) %copy-start.3) | copy-done | bytes 4120
  12.3 0.0 copy-start
  12.3 1.2 %copy-done = bf16[16,4,64,64]{3,2,1,0:T(8,128)(2,1)S(1)} copy-done((bf16[16,4,64,64]{3,2,1,0:T(8,128)(2,1)S(1)}, bf16[16,4,64,64]{3,2,1,0:T(8,128)(2,1)}, u32[]{:S(2)}) %copy-start) | copy-done | bytes 524312
  13.5 0.0 copy-start.1
  13.5 0.0 copy-start.2
  13.5 1.2 %build.1 = (bf16[16,64,256]{2,1,0:T(8,128)(2,1)S(1)}, f32[1024,128]{1,0:T(8,128)S(1)}) custom-call(s32[16,4]{1,0:T(8,128)S(1)} %copy.10.pattern_ref, bf16[16,4,64,64]{3,2,1,0:T(8,128)(2,1)S(1)} %copy-done, f32[1,1024]{1,0:T(1,128)S(1)} %bitcast.4), custom_call_target="tpu_custom_call" | custom-call | flops 1073741824 | bytes 4194304 | tf_op jit(solution)/shard_map/build/pallas_call | solution.py:138
  14.7 0.0 copy-start.4
  14.7 0.0 copy-done.1
  14.8 0.0 copy-done.2
  14.8 0.7 %copy-done.4 = s32[256]{0:T(256)S(1)} copy-done((s32[256]{0:T(256)S(1)}, s32[256]{0:T(256)}, u32[]{:S(2)}) %copy-start.4) | copy-done | bytes 1048
  15.4 20.4 %chain.1 = (f32[1,256,1024]{2,1,0:T(8,128)}, f32[1,256]{1,0:T(1,128)}) custom-call(s32[2]{0:T(128)S(1)} %pad_add_fusion.place_ref, s32[32]{0:T(128)S(1)} %all-reduce.observed_ref, s32[256]{0:T(256)S(1)} %copy-done.4, s32[16,4]{1,0:T(8,128)S(1)} %copy.10.pattern_ref, f32[256,1024]{1,0:T(8,128)S(1)} %copy-done.1, f32[16,1024]{1,0:T(8,128)S(1)} %copy-done.2, ...), custom_call_target="tpu_custom_call" | custom-call | flops 17179869184 | bytes 4194304 | tf_op jit(solution)/shard_map/chain/pallas_call | solution.py:152
  (1 shorter events, 0.0 us)
Async XLA Ops:
  0.6 0.7 %copy-start.7 = (u32[32]{0:T(128)S(1)}, u32[32]{0:T(128)}, u32[]{:S(2)}) copy-start(u32[32]{0:T(128)} %constant.16) | copy-start | bytes 388
  2.5 0.7 %copy-start.6 = (s32[4]{0:T(128)S(1)}, s32[4]{0:T(128)}, u32[]{:S(2)}) copy-start(s32[4]{0:T(128)} %param.7) | copy-start | bytes 52
  3.2 8.4 %copy-start.5 = (s32[16,4]{0,1:T(4,128)S(1)}, s32[16,4]{0,1:T(4,128)}, u32[]{:S(2)}) copy-start(s32[16,4]{0,1:T(4,128)} %param.8) | copy-start | bytes 772
  11.6 0.7 %copy-start.3 = (f32[1024]{0:T(1024)S(1)}, f32[1024]{0:T(1024)}, u32[]{:S(2)}) copy-start(f32[1024]{0:T(1024)} %param.10) | copy-start | bytes 12292
  12.3 1.2 %copy-start = (bf16[16,4,64,64]{3,2,1,0:T(8,128)(2,1)S(1)}, bf16[16,4,64,64]{3,2,1,0:T(8,128)(2,1)}, u32[]{:S(2)}) copy-start(bf16[16,4,64,64]{3,2,1,0:T(8,128)(2,1)} %blocks_ref.1) | copy-start | bytes 1572868
  13.5 1.2 %copy-start.1 = (f32[256,1024]{1,0:T(8,128)S(1)}, f32[256,1024]{1,0:T(8,128)}, u32[]{:S(2)}) copy-start(f32[256,1024]{1,0:T(8,128)} %symbol_ref.1) | copy-start | bytes 3145732
  13.5 1.2 %copy-start.2 = (f32[16,1024]{1,0:T(8,128)S(1)}, f32[16,1024]{1,0:T(8,128)}, u32[]{:S(2)}) copy-start(f32[16,1024]{1,0:T(8,128)} %cluster_emit_ref.1) | copy-start | bytes 196612
  14.7 0.7 %copy-start.4 = (s32[256]{0:T(256)S(1)}, s32[256]{0:T(256)}, u32[]{:S(2)}) copy-start(s32[256]{0:T(256)} %cluster_ref.1) | copy-start | bytes 3076

commit v4 on v3

v4 whole, which is shorter than its diff:
```python
import functools

import jax
import jax.numpy as jnp
from jax import lax
from jax.experimental import pallas as pl
from jax.experimental.pallas import tpu as pltpu
from jax.sharding import PartitionSpec as P

LANES = 128
SUBLANES = 8


def column(row):
    return jnp.broadcast_to(row, (LANES, row.shape[1])).T


def chain_kernel(
    place_ref,
    observed_ref,
    pattern_hbm,
    cluster_hbm,
    leave_hbm,
    blocks_hbm,
    cluster_emit_hbm,
    symbol_hbm,
    rows_hbm,
    rate_ref,
    pattern_ref,
    cluster_ref,
    leave_ref,
    blocks_ref,
    cluster_emit_ref,
    symbol_ref,
    rows_ref,
    leave_col_ref,
    stay_ref,
    weight_ref,
    cur_ref,
    low_a_ref,
    low_b_ref,
    emit_ref,
    emit_col_ref,
    sems,
    block_sems,
    out_sems,
):
    steps = observed_ref.shape[1]
    n_half, n_blocks, padded, _ = cur_ref.shape
    size = blocks_ref.shape[-1]
    n_states = n_blocks * size
    n_rows = n_half * LANES
    n_source = pattern_ref.shape[0]
    first = padded - size
    n_segments = place_ref[0]
    row_start = place_ref[1]
    lows = (low_a_ref, low_b_ref)

    small = [
        pltpu.make_async_copy(source, target, sems.at[i])
        for i, (source, target) in enumerate(
            [
                (leave_hbm, leave_ref),
                (pattern_hbm, pattern_ref),
                (cluster_hbm, cluster_ref),
                (cluster_emit_hbm, cluster_emit_ref),
                (symbol_hbm, symbol_ref),
            ]
        )
    ]
    n_chunks = block_sems.shape[0]
    per_chunk = n_blocks // n_chunks
    chunks = [
        pltpu.make_async_copy(
            blocks_hbm.at[pl.ds(i * per_chunk, per_chunk)],
            blocks_ref.at[pl.ds(i * per_chunk, per_chunk)],
            block_sems.at[i],
        )
        for i in range(n_chunks)
    ]
    for copy in small[:2] + chunks + small[2:]:
        copy.start()

    def store(low_ref, j, h, new):
        cur_ref[h, j, first:, :] = new
        cur_ref[h, j, first - 1 : first, :] = new[size - 1 :, :]
        low_ref[j * size : (j + 1) * size, h * LANES : (h + 1) * LANES] = new.astype(jnp.bfloat16)

    state = lax.broadcasted_iota(jnp.int32, (size, LANES), 0)
    row = lax.broadcasted_iota(jnp.int32, (size, LANES), 1)
    for j in range(n_blocks):
        for h in range(n_half):
            start = state + j * size == row + (row_start + h * LANES)
            store(low_a_ref, j, h, start.astype(jnp.float32))
    emit_ref[...] = jnp.zeros_like(emit_ref)

    small[0].wait()
    leave_col = column(leave_ref[...])
    leave_col_ref[...] = leave_col
    for j in range(n_blocks):
        own = leave_col[j * size : (j + 1) * size]
        stay_ref[j * size : (j + 1) * size, :] = 1.0 - pltpu.roll(own, 1, 0)
    small[1].wait()
    for j in range(n_blocks):
        if j % per_chunk == 0:
            chunks[j // per_chunk].wait()
        parts = []
        for k in range(n_source):
            rows = pl.ds(pl.multiple_of(pattern_ref[k, j] * size, size), size)
            parts.append(blocks_ref[j, k].astype(jnp.float32) * leave_col_ref[rows, :size])
        moved = jnp.concatenate(parts, axis=0)
        weight_ref[j] = moved.T.astype(jnp.bfloat16)
    for copy in small[2:]:
        copy.wait()

    def segment(g, carried):
        scale, log_scale = carried
        for s in range(steps):
            symbol = observed_ref[g, s]
            emission = symbol_ref[pl.ds(symbol, 1), :]
            emission = emission * cluster_emit_ref[pl.ds(cluster_ref[symbol], 1), :]
            emit_ref[s : s + 1, :] = emission
        emit_col_ref[...] = emit_ref[...].T
        sums = [jnp.zeros((SUBLANES, LANES), jnp.float32) for _ in range(n_half)]
        for s in range(steps):
            now, later = lows[s % 2], lows[(s + 1) % 2]
            for j in range(n_blocks):
                states = slice(j * size, (j + 1) * size)
                picked = [
                    now[pl.ds(pl.multiple_of(pattern_ref[k, j] * size, size), size), :]
                    for k in range(n_source)
                ]
                moved = jnp.dot(
                    weight_ref[j],
                    jnp.concatenate(picked, axis=0),
                    preferred_element_type=jnp.float32,
                )
                emission = jnp.broadcast_to(emit_col_ref[states, s : s + 1], (size, LANES))
                stay = stay_ref[states, :]
                for h in range(n_half):
                    part = slice(h * LANES, (h + 1) * LANES)
                    kept = cur_ref[h, j, first - 1 : padded - 1, :] * stay
                    new = (kept + moved[:, part]) * emission
                    if s == 0:
                        new = new * scale[:, part]
                    store(later, j, h, new)
                    if s == steps - 1:
                        sums[h] = sums[h] + jnp.sum(new.reshape(-1, SUBLANES, LANES), axis=0)
        if steps % 2:
            low_a_ref[...] = low_b_ref[...]
        row_sum = jnp.concatenate([jnp.sum(t, axis=0, keepdims=True) for t in sums], axis=1)
        return 1.0 / row_sum, log_scale + jnp.log(row_sum)

    ones = jnp.ones((1, n_rows), jnp.float32)
    scale, log_scale = lax.fori_loop(0, n_segments, segment, (ones, jnp.zeros_like(ones)))
    scale = scale * n_states
    per = LANES // size
    out = []
    for h in range(n_half):
        part = slice(h * LANES, (h + 1) * LANES)
        for j in range(n_states // LANES):
            block = [cur_ref[h, j * per + i, first:, :] for i in range(per)]
            block = jnp.concatenate(block, axis=0) * scale[:, part]
            rows_ref[part, j * LANES : (j + 1) * LANES] = block.T
        rows = pl.ds(h * LANES, LANES)
        out.append(
            pltpu.make_async_copy(rows_ref.at[rows], rows_hbm.at[0, rows], out_sems.at[h])
        )
        out[-1].start()
    divisor = (n_segments * steps).astype(jnp.float32)
    rate_ref[...] = (log_scale - jnp.log(jnp.full_like(ones, n_states))) / divisor
    for copy in out:
        copy.wait()


def body(observed, pattern, trans_blocks, leave_rate, symbol_emit, cluster_emit, symbol_cluster):
    n_blocks, n_source, size, _ = trans_blocks.shape
    n_states = leave_rate.shape[0]
    steps = observed.shape[0]
    n_rows = n_states // lax.axis_size("rows")
    tm = lax.axis_index("tm")
    segments = jnp.arange(lax.axis_size("tm"))
    own = jnp.where(segments[:, None] == tm, observed[None, :], 0)
    all_observed = lax.psum(own, "tm")
    place = jnp.stack([tm + 1, lax.axis_index("rows") * n_rows]).astype(jnp.int32)
    vmem = pl.BlockSpec(memory_space=pltpu.VMEM)
    smem = pl.BlockSpec(memory_space=pltpu.SMEM)
    hbm = pl.BlockSpec(memory_space=pltpu.HBM)
    f32, bf16 = jnp.float32, jnp.bfloat16
    return pl.pallas_call(
        chain_kernel,
        out_shape=[
            jax.ShapeDtypeStruct((1, n_rows, n_states), f32),
            jax.ShapeDtypeStruct((1, n_rows), f32),
        ],
        in_specs=[smem, smem] + [hbm] * 6,
        out_specs=[hbm, vmem],
        scratch_shapes=[
            pltpu.SMEM((n_source, n_blocks), jnp.int32),
            pltpu.SMEM(symbol_cluster.shape, jnp.int32),
            pltpu.VMEM((1, n_states), f32),
            pltpu.VMEM(trans_blocks.shape, bf16),
            pltpu.VMEM(cluster_emit.shape, f32),
            pltpu.VMEM(symbol_emit.shape, f32),
            pltpu.VMEM((n_rows, n_states), f32),
            pltpu.VMEM((n_states, LANES), f32),
            pltpu.VMEM((n_states, LANES), f32),
            pltpu.VMEM((n_blocks, size, n_source * size), bf16),
            pltpu.VMEM((n_rows // LANES, n_blocks, size + SUBLANES, LANES), f32),
            pltpu.VMEM((n_states, n_rows), bf16),
            pltpu.VMEM((n_states, n_rows), bf16),
            pltpu.VMEM((LANES, n_states), f32),
            pltpu.VMEM((n_states, LANES), f32),
            pltpu.SemaphoreType.DMA((5,)),
            pltpu.SemaphoreType.DMA((4,)),
            pltpu.SemaphoreType.DMA((n_rows // LANES,)),
        ],
        compiler_params=pltpu.CompilerParams(vmem_limit_bytes=60 << 20),
        cost_estimate=pl.CostEstimate(flops=1 << 34, bytes_accessed=4 << 20, transcendentals=0),
        name="chain",
    )(
        place,
        all_observed,
        pattern.T,
        symbol_cluster,
        leave_rate.reshape(1, n_states),
        trans_blocks,
        cluster_emit,
        symbol_emit,
    )


def solution(mesh):
    in_specs = (P("tm"), P(), P(), P(), P(), P(), P())
    out_specs = (P("tm", "rows", None), P("tm", "rows"))
    return jax.shard_map(body, mesh=mesh, in_specs=in_specs, out_specs=out_specs, check_vma=False)
```

time: 36.1 us -> 32.8 us (0.909)
  local copies, waits for them, and re-layouts: 4.56 us -> 0.65 us
  between operations: 1.35 us -> 0.64 us
  blocking collectives: 8.23 us -> 8.82 us
  other arithmetic: 0.08 us -> 0.66 us
    psum x0 -> x1, blocking collectives: none -> 8.82 us  [body(): all_observed = lax.psum(own, 'tm')]
    unnamed x1 -> x0, blocking collectives: 8.23 us -> none
    unnamed x20 -> x2, local copies, waits for them, and re-layouts: 4.56 us -> 0.65 us
    another operation x1, other arithmetic: 0.08 us -> 0.58 us  [body(): jnp.stack([tm + 1, lax.axis_index('rows') * n_rows]).astype(jnp.int32)]
    pallas_call x2 -> x1, Pallas kernels: 21.6 us -> 21.8 us  [body(): pl.pallas_call(chain_kernel, out_shape=[jax.ShapeDtypeStruct((1, n_rows,...]
where the time goes in v4:
time: 32.8 us; the launch traced here: 32.5 us
  Pallas kernels  21.8 us (66%)
  blocking collectives  8.82 us (27%)
  other arithmetic  0.66 us (2%)
  local copies, waits for them, and re-layouts  0.65 us (2%)
  between operations  0.64 us (2%)
    pallas_call x1, Pallas kernels, body(): pl.pallas_call(chain_kernel, out_shape=[jax.ShapeDtypeStruct((1, n_rows,...  21.8 us
    psum x1, blocking collectives, body(): all_observed = lax.psum(own, 'tm')  8.82 us

profile of v4, /device:TPU:26, one launch (start us, length us, event | category | flops | bytes accessed | tf_op | source)
XLA Modules:
  0.0 32.5 jit_solution(12505618913558958666)
XLA Ops:
  0.6 0.6 %pad_add_fusion.place_ref = s32[2]{0:T(128)} fusion(s32[1]{0:T(128)} %bitcast.1, s32[1]{0:T(128)} %bitcast), kind=kLoop, calls=%fused_computation.1 | loop fusion | flops 2 | bytes 16 | tf_op jit(solution)/shard_map/stack | solution.py:185
  1.2 0.0 copy-start
  1.2 0.7 %copy-done = s32[4]{0:T(128)S(1)} copy-done((s32[4]{0:T(128)S(1)}, s32[4]{0:T(128)}, u32[]{:S(2)}) %copy-start) | copy-done | bytes 40
  1.9 0.1 broadcast_select_fusion
  1.9 8.8 %psum.7.observed_ref = s32[8,4]{1,0:T(8,128)} all-reduce(s32[8,4]{1,0:T(8,128)S(1)} %broadcast_select_fusion), channel_id=1, replica_groups=mesh['tm'=8,'rows'=4] {'tm'}, use_global_device_ids=true, to_apply=%region_0.1 | all-reduce | flops 32 | bytes 256 | tf_op jit(solution)/shard_map/psum | solution.py:184
  10.8 21.8 %chain.1 = (f32[1,256,1024]{2,1,0:T(8,128)}, f32[1,256]{1,0:T(1,128)}) custom-call(s32[2]{0:T(128)} %pad_add_fusion.place_ref, s32[8,4]{1,0:T(8,128)} %psum.7.observed_ref, s32[4,16]{1,0:T(4,128)} %bitcast.5, s32[256]{0:T(256)} %cluster_hbm.1, f32[1,1024]{1,0:T(1,128)} %bitcast.4, bf16[16,4,64,64]{3,2,1,0:T(8,128)(2,1)} %blocks_hbm.1, ...), custom_call_target="tpu_custom_call" | custom-call | flops 17179869184 | bytes 4194304 | tf_op jit(solution)/shard_map/chain/pallas_call | solution.py:190
  (1 shorter events, 0.0 us)
Async XLA Ops:
  1.2 0.7 %copy-start = (s32[4]{0:T(128)S(1)}, s32[4]{0:T(128)}, u32[]{:S(2)}) copy-start(s32[4]{0:T(128)} %param.7) | copy-start | bytes 52

commit v5 on v4

--- a/solution.py
+++ b/solution.py
@@ -16,7 +16,6 @@
 
 
 def chain_kernel(
-    place_ref,
     observed_ref,
     pattern_hbm,
     cluster_hbm,
@@ -36,9 +35,8 @@
     leave_col_ref,
     stay_ref,
     weight_ref,
-    cur_ref,
-    low_a_ref,
-    low_b_ref,
+    cur_refs,
+    low_refs,
     emit_ref,
     emit_col_ref,
     sems,
@@ -46,15 +44,15 @@
     out_sems,
 ):
     steps = observed_ref.shape[1]
-    n_half, n_blocks, padded, _ = cur_ref.shape
+    n_half = len(cur_refs)
+    n_blocks, padded, _ = cur_refs[0].shape
     size = blocks_ref.shape[-1]
     n_states = n_blocks * size
     n_rows = n_half * LANES
     n_source = pattern_ref.shape[0]
     first = padded - size
-    n_segments = place_ref[0]
-    row_start = place_ref[1]
-    lows = (low_a_ref, low_b_ref)
+    n_segments = lax.axis_index("tm") + 1
+    row_start = lax.axis_index("rows") * n_rows
 
     small = [
         pltpu.make_async_copy(source, target, sems.at[i])
@@ -81,17 +79,17 @@
     for copy in small[:2] + chunks + small[2:]:
         copy.start()
 
-    def store(low_ref, j, h, new):
-        cur_ref[h, j, first:, :] = new
-        cur_ref[h, j, first - 1 : first, :] = new[size - 1 :, :]
-        low_ref[j * size : (j + 1) * size, h * LANES : (h + 1) * LANES] = new.astype(jnp.bfloat16)
+    def store(cur_ref, low_ref, j, new):
+        cur_ref[j, first:, :] = new
+        cur_ref[j, first - 1 : first, :] = new[size - 1 :, :]
+        low_ref[j * size : (j + 1) * size, :] = new.astype(jnp.bfloat16)
 
     state = lax.broadcasted_iota(jnp.int32, (size, LANES), 0)
     row = lax.broadcasted_iota(jnp.int32, (size, LANES), 1)
     for j in range(n_blocks):
         for h in range(n_half):
             start = state + j * size == row + (row_start + h * LANES)
-            store(low_a_ref, j, h, start.astype(jnp.float32))
+            store(cur_refs[h], low_refs[h][0], j, start.astype(jnp.float32))
     emit_ref[...] = jnp.zeros_like(emit_ref)
 
     small[0].wait()
@@ -123,31 +121,31 @@
         emit_col_ref[...] = emit_ref[...].T
         sums = [jnp.zeros((SUBLANES, LANES), jnp.float32) for _ in range(n_half)]
         for s in range(steps):
-            now, later = lows[s % 2], lows[(s + 1) % 2]
-            for j in range(n_blocks):
-                states = slice(j * size, (j + 1) * size)
-                picked = [
-                    now[pl.ds(pl.multiple_of(pattern_ref[k, j] * size, size), size), :]
-                    for k in range(n_source)
-                ]
-                moved = jnp.dot(
-                    weight_ref[j],
-                    jnp.concatenate(picked, axis=0),
-                    preferred_element_type=jnp.float32,
-                )
-                emission = jnp.broadcast_to(emit_col_ref[states, s : s + 1], (size, LANES))
-                stay = stay_ref[states, :]
-                for h in range(n_half):
-                    part = slice(h * LANES, (h + 1) * LANES)
-                    kept = cur_ref[h, j, first - 1 : padded - 1, :] * stay
-                    new = (kept + moved[:, part]) * emission
+            for h in range(n_half):
+                now, later = low_refs[h][s % 2], low_refs[h][(s + 1) % 2]
+                part = slice(h * LANES, (h + 1) * LANES)
+                for j in range(n_blocks):
+                    states = slice(j * size, (j + 1) * size)
+                    picked = [
+                        now[pl.ds(pl.multiple_of(pattern_ref[k, j] * size, size), size), :]
+                        for k in range(n_source)
+                    ]
+                    moved = jnp.dot(
+                        weight_ref[j],
+                        jnp.concatenate(picked, axis=0),
+                        preferred_element_type=jnp.float32,
+                    )
+                    emission = jnp.broadcast_to(emit_col_ref[states, s : s + 1], (size, LANES))
+                    kept = cur_refs[h][j, first - 1 : padded - 1, :] * stay_ref[states, :]
+                    new = (kept + moved) * emission
                     if s == 0:
                         new = new * scale[:, part]
-                    store(later, j, h, new)
+                    store(cur_refs[h], later, j, new)
                     if s == steps - 1:
                         sums[h] = sums[h] + jnp.sum(new.reshape(-1, SUBLANES, LANES), axis=0)
         if steps % 2:
-            low_a_ref[...] = low_b_ref[...]
+            for h in range(n_half):
+                low_refs[h][0][...] = low_refs[h][1][...]
         row_sum = jnp.concatenate([jnp.sum(t, axis=0, keepdims=True) for t in sums], axis=1)
         return 1.0 / row_sum, log_scale + jnp.log(row_sum)
 
@@ -159,7 +157,7 @@
     for h in range(n_half):
         part = slice(h * LANES, (h + 1) * LANES)
         for j in range(n_states // LANES):
-            block = [cur_ref[h, j * per + i, first:, :] for i in range(per)]
+            block = [cur_refs[h][j * per + i, first:, :] for i in range(per)]
             block = jnp.concatenate(block, axis=0) * scale[:, part]
             rows_ref[part, j * LANES : (j + 1) * LANES] = block.T
         rows = pl.ds(h * LANES, LANES)
@@ -178,11 +176,11 @@
     n_states = leave_rate.shape[0]
     steps = observed.shape[0]
     n_rows = n_states // lax.axis_size("rows")
+    n_half = n_rows // LANES
     tm = lax.axis_index("tm")
     segments = jnp.arange(lax.axis_size("tm"))
     own = jnp.where(segments[:, None] == tm, observed[None, :], 0)
     all_observed = lax.psum(own, "tm")
-    place = jnp.stack([tm + 1, lax.axis_index("rows") * n_rows]).astype(jnp.int32)
     vmem = pl.BlockSpec(memory_space=pltpu.VMEM)
     smem = pl.BlockSpec(memory_space=pltpu.SMEM)
     hbm = pl.BlockSpec(memory_space=pltpu.HBM)
@@ -193,7 +191,7 @@
             jax.ShapeDtypeStruct((1, n_rows, n_states), f32),
             jax.ShapeDtypeStruct((1, n_rows), f32),
         ],
-        in_specs=[smem, smem] + [hbm] * 6,
+        in_specs=[smem] + [hbm] * 6,
         out_specs=[hbm, vmem],
         scratch_shapes=[
             pltpu.SMEM((n_source, n_blocks), jnp.int32),
@@ -206,20 +204,18 @@
             pltpu.VMEM((n_states, LANES), f32),
             pltpu.VMEM((n_states, LANES), f32),
             pltpu.VMEM((n_blocks, size, n_source * size), bf16),
-            pltpu.VMEM((n_rows // LANES, n_blocks, size + SUBLANES, LANES), f32),
-            pltpu.VMEM((n_states, n_rows), bf16),
-            pltpu.VMEM((n_states, n_rows), bf16),
+            [pltpu.VMEM((n_blocks, size + SUBLANES, LANES), f32) for _ in range(n_half)],
+            [[pltpu.VMEM((n_states, LANES), bf16) for _ in range(2)] for _ in range(n_half)],
             pltpu.VMEM((LANES, n_states), f32),
             pltpu.VMEM((n_states, LANES), f32),
             pltpu.SemaphoreType.DMA((5,)),
             pltpu.SemaphoreType.DMA((4,)),
-            pltpu.SemaphoreType.DMA((n_rows // LANES,)),
+            pltpu.SemaphoreType.DMA((n_half,)),
         ],
         compiler_params=pltpu.CompilerParams(vmem_limit_bytes=60 << 20),
         cost_estimate=pl.CostEstimate(flops=1 << 34, bytes_accessed=4 << 20, transcendentals=0),
         name="chain",
     )(
-        place,
         all_observed,
         pattern.T,
         symbol_cluster,

time: 32.8 us -> 33.1 us (level)
  Pallas kernels: 21.8 us -> 22.7 us
  other arithmetic: 0.66 us -> 0.08 us
    pallas_call x1, Pallas kernels: 21.8 us -> 22.7 us  [body(): pl.pallas_call(chain_kernel, out_shape=[jax.ShapeDtypeStruct((1, n_rows,...]
    another operation x1 -> x0, other arithmetic: 0.58 us -> none  [body(): jnp.stack([tm + 1, lax.axis_index('rows') * n_rows]).astype(jnp.int32)]
where the time goes in v5:
time: 33.1 us; the launch traced here: 32.9 us
  Pallas kernels  22.7 us (69%)
  blocking collectives  8.82 us (27%)
  local copies, waits for them, and re-layouts  0.65 us (2%)
  between operations  0.65 us (2%)
    pallas_call x1, Pallas kernels, body(): pl.pallas_call(chain_kernel, out_shape=[jax.ShapeDtypeStruct((1, n_rows,...  22.7 us
    psum x1, blocking collectives, body(): all_observed = lax.psum(own, 'tm')  8.82 us

profile of v5, /device:TPU:26, one launch (start us, length us, event | category | flops | bytes accessed | tf_op | source)
XLA Modules:
  0.0 32.9 jit_solution(13859956084366931885)
XLA Ops:
  0.6 0.0 copy-start
  0.7 0.6 %copy-done = s32[4]{0:T(128)S(1)} copy-done((s32[4]{0:T(128)S(1)}, s32[4]{0:T(128)}, u32[]{:S(2)}) %copy-start) | copy-done | bytes 40
  1.3 0.1 broadcast_select_fusion
  1.4 8.8 %psum.7.observed_ref = s32[8,4]{1,0:T(8,128)} all-reduce(s32[8,4]{1,0:T(8,128)S(1)} %broadcast_select_fusion), channel_id=1, replica_groups=mesh['tm'=8,'rows'=4] {'tm'}, use_global_device_ids=true, to_apply=%region_0.1 | all-reduce | flops 32 | bytes 256 | tf_op jit(solution)/shard_map/psum | solution.py:183
  10.2 22.7 %chain.1 = (f32[1,256,1024]{2,1,0:T(8,128)}, f32[1,256]{1,0:T(1,128)}) custom-call(s32[8,4]{1,0:T(8,128)} %psum.7.observed_ref, s32[4,16]{1,0:T(4,128)} %bitcast.3, s32[256]{0:T(256)} %cluster_hbm.1, f32[1,1024]{1,0:T(1,128)} %bitcast.2, bf16[16,4,64,64]{3,2,1,0:T(8,128)(2,1)} %blocks_hbm.1, f32[16,1024]{1,0:T(8,128)} %cluster_emit_hbm.1, f32[256,1024]{1,0:T(8,128)} %symbol_hbm.1), custom_call_target="tpu_custom_call" | custom-call | flops 17179869184 | bytes 4194304 | tf_op jit(solution)/shard_map/chain/pallas_call | solution.py:188
  (1 shorter events, 0.0 us)
Async XLA Ops:
  0.6 0.7 %copy-start = (s32[4]{0:T(128)S(1)}, s32[4]{0:T(128)}, u32[]{:S(2)}) copy-start(s32[4]{0:T(128)} %param.7) | copy-start | bytes 52

commit v6 on v4

--- a/solution.py
+++ b/solution.py
@@ -16,7 +16,6 @@
 
 
 def chain_kernel(
-    place_ref,
     observed_ref,
     pattern_hbm,
     cluster_hbm,
@@ -36,11 +35,18 @@
     leave_col_ref,
     stay_ref,
     weight_ref,
+    back_ref,
     cur_ref,
+    base_ref,
     low_a_ref,
     low_b_ref,
     emit_ref,
     emit_col_ref,
+    stay_slab_ref,
+    emit_slab_ref,
+    sum_refs,
+    part_refs,
+    change_ref,
     sems,
     block_sems,
     out_sems,
@@ -52,8 +58,8 @@
     n_rows = n_half * LANES
     n_source = pattern_ref.shape[0]
     first = padded - size
-    n_segments = place_ref[0]
-    row_start = place_ref[1]
+    n_segments = lax.axis_index("tm") + 1
+    row_start = lax.axis_index("rows") * n_rows
     lows = (low_a_ref, low_b_ref)
 
     small = [
@@ -81,9 +87,9 @@
     for copy in small[:2] + chunks + small[2:]:
         copy.start()
 
-    def store(low_ref, j, h, new):
-        cur_ref[h, j, first:, :] = new
-        cur_ref[h, j, first - 1 : first, :] = new[size - 1 :, :]
+    def store(target_ref, low_ref, j, h, new):
+        target_ref[h, j, first:, :] = new
+        target_ref[h, j, :first, :] = new[size - first :, :]
         low_ref[j * size : (j + 1) * size, h * LANES : (h + 1) * LANES] = new.astype(jnp.bfloat16)
 
     state = lax.broadcasted_iota(jnp.int32, (size, LANES), 0)
@@ -91,10 +97,21 @@
     for j in range(n_blocks):
         for h in range(n_half):
             start = state + j * size == row + (row_start + h * LANES)
-            store(low_a_ref, j, h, start.astype(jnp.float32))
+            store(base_ref, low_a_ref, j, h, start.astype(jnp.float32))
     emit_ref[...] = jnp.zeros_like(emit_ref)
 
+    per = LANES // size
+    low_half = lax.broadcasted_iota(jnp.int32, (1, LANES), 1) < size
+
+    def twice(tile, at):
+        other = pltpu.roll(tile, size, 1)
+        return jnp.where(low_half, tile, other) if at == 0 else jnp.where(low_half, other, tile)
+
     small[0].wait()
+    for j in range(n_blocks):
+        tile = leave_ref[:, j // per * LANES : (j // per + 1) * LANES]
+        tile = jnp.broadcast_to(1.0 - tile, (SUBLANES, LANES))
+        stay_slab_ref[j] = twice(tile, j % per)
     leave_col = column(leave_ref[...])
     leave_col_ref[...] = leave_col
     for j in range(n_blocks):
@@ -108,18 +125,83 @@
         for k in range(n_source):
             rows = pl.ds(pl.multiple_of(pattern_ref[k, j] * size, size), size)
             parts.append(blocks_ref[j, k].astype(jnp.float32) * leave_col_ref[rows, :size])
-        moved = jnp.concatenate(parts, axis=0)
-        weight_ref[j] = moved.T.astype(jnp.bfloat16)
+        moved = jnp.concatenate(parts, axis=0).T
+        weight_ref[j] = moved.astype(jnp.bfloat16)
+        for k in range(n_source):
+            tile = moved[:, k // per * LANES : (k // per + 1) * LANES]
+            back_ref[j, :, k * LANES : (k + 1) * LANES] = twice(tile, k % per).astype(jnp.bfloat16)
     for copy in small[2:]:
         copy.wait()
+
+    n_tm = observed_ref.shape[0]
+
+    def emission_of(g, s):
+        symbol = observed_ref[g, s]
+        row = symbol_ref[pl.ds(symbol, 1), :]
+        return row * cluster_emit_ref[pl.ds(cluster_ref[symbol], 1), :]
+
+    for s in range(steps):
+        emission = jnp.concatenate([emission_of(g, s) for g in range(n_tm)], axis=0)
+        for j in range(n_blocks):
+            tile = emission[:, j // per * LANES : (j // per + 1) * LANES]
+            emit_slab_ref[s, j] = twice(tile, j % per)
+    stays = [jnp.broadcast_to(stay_slab_ref[j][:1], (n_tm, LANES)) for j in range(n_blocks)]
+
+    for l in range(steps):
+        n_pos = steps - l
+        for ref in part_refs:
+            ref[...] = jnp.zeros_like(ref)
+        for j in range(n_blocks):
+            images = []
+            for p in range(n_pos):
+                image = emit_slab_ref[p, j]
+                if l:
+                    image = image * sum_refs[l - 1][p + 1, j]
+                images.append(image)
+                sum_refs[l][p, j] = stays[j] * pltpu.roll(image, LANES - 1, 1)
+            images = jnp.concatenate(images, axis=0)[:, :size].astype(jnp.bfloat16)
+            moved = jnp.dot(images, back_ref[j], preferred_element_type=jnp.float32)
+            for k in range(n_source):
+                part = moved[:, k * LANES : (k + 1) * LANES].reshape(n_pos, n_tm, LANES)
+                source = pattern_ref[k, j]
+                for p in range(n_pos):
+                    part_refs[k][p, source] = part_refs[k][p, source] + part[p]
+        for j in range(n_blocks):
+            for p in range(n_pos):
+                total = sum_refs[l][p, j]
+                for ref in part_refs:
+                    total = total + ref[p, j]
+                sum_refs[l][p, j] = total
+
+    changes = []
+    for j in range(n_blocks):
+        exact = jnp.ones((n_tm, LANES), jnp.float32)
+        weight = exact
+        deviation = []
+        for s in range(steps):
+            row_sum = pltpu.roll(sum_refs[s][0, j], 1, 1)
+            for q in range(s):
+                row_sum = row_sum + deviation[q] * sum_refs[s - q - 1][q + 1, j]
+                row_sum = pltpu.roll(row_sum, 1, 1)
+            emission = emit_slab_ref[s, j]
+            exact = pltpu.roll(exact * stays[j], 1, 1) * emission
+            weight = pltpu.roll(weight * stays[j], 1, 1) * emission
+            rounded = (weight * (n_states / row_sum)).astype(jnp.bfloat16).astype(jnp.float32)
+            rounded = rounded * (row_sum * (1.0 / n_states))
+            deviation.append(rounded - weight)
+            weight = rounded
+        changes.append(weight - exact)
+    for m in range(n_states // LANES):
+        tile = changes[m * per + per - 1]
+        for i in range(per - 1):
+            tile = jnp.where(low_half, changes[m * per + i], tile)
+        change_ref[:, m * LANES : (m + 1) * LANES] = tile
 
     def segment(g, carried):
         scale, log_scale = carried
         for s in range(steps):
-            symbol = observed_ref[g, s]
-            emission = symbol_ref[pl.ds(symbol, 1), :]
-            emission = emission * cluster_emit_ref[pl.ds(cluster_ref[symbol], 1), :]
-            emit_ref[s : s + 1, :] = emission
+            emit_ref[s : s + 1, :] = emission_of(g, s)
+        emit_ref[steps : steps + 1, :] = change_ref[pl.ds(g, 1), :]
         emit_col_ref[...] = emit_ref[...].T
         sums = [jnp.zeros((SUBLANES, LANES), jnp.float32) for _ in range(n_half)]
         for s in range(steps):
@@ -137,15 +219,21 @@
                 )
                 emission = jnp.broadcast_to(emit_col_ref[states, s : s + 1], (size, LANES))
                 stay = stay_ref[states, :]
+                from_ref = base_ref if s == 0 else cur_ref
+                to_ref = base_ref if s == steps - 1 else cur_ref
+                if s == steps - 1:
+                    change = jnp.broadcast_to(emit_col_ref[states, steps : steps + 1], (size, LANES))
                 for h in range(n_half):
                     part = slice(h * LANES, (h + 1) * LANES)
-                    kept = cur_ref[h, j, first - 1 : padded - 1, :] * stay
+                    kept = from_ref[h, j, first - 1 : padded - 1, :] * stay
                     new = (kept + moved[:, part]) * emission
                     if s == 0:
                         new = new * scale[:, part]
-                    store(later, j, h, new)
                     if s == steps - 1:
+                        start = base_ref[h, j, first - steps : padded - steps, :]
+                        new = new + start * change * scale[:, part]
                         sums[h] = sums[h] + jnp.sum(new.reshape(-1, SUBLANES, LANES), axis=0)
+                    store(to_ref, later, j, h, new)
         if steps % 2:
             low_a_ref[...] = low_b_ref[...]
         row_sum = jnp.concatenate([jnp.sum(t, axis=0, keepdims=True) for t in sums], axis=1)
@@ -154,12 +242,11 @@
     ones = jnp.ones((1, n_rows), jnp.float32)
     scale, log_scale = lax.fori_loop(0, n_segments, segment, (ones, jnp.zeros_like(ones)))
     scale = scale * n_states
-    per = LANES // size
     out = []
     for h in range(n_half):
         part = slice(h * LANES, (h + 1) * LANES)
         for j in range(n_states // LANES):
-            block = [cur_ref[h, j * per + i, first:, :] for i in range(per)]
+            block = [base_ref[h, j * per + i, first:, :] for i in range(per)]
             block = jnp.concatenate(block, axis=0) * scale[:, part]
             rows_ref[part, j * LANES : (j + 1) * LANES] = block.T
         rows = pl.ds(h * LANES, LANES)
@@ -178,11 +265,9 @@
     n_states = leave_rate.shape[0]
     steps = observed.shape[0]
     n_rows = n_states // lax.axis_size("rows")
-    tm = lax.axis_index("tm")
-    segments = jnp.arange(lax.axis_size("tm"))
-    own = jnp.where(segments[:, None] == tm, observed[None, :], 0)
-    all_observed = lax.psum(own, "tm")
-    place = jnp.stack([tm + 1, lax.axis_index("rows") * n_rows]).astype(jnp.int32)
+    n_tm = lax.axis_size("tm")
+    own = jnp.broadcast_to(observed[None, :], (n_tm, steps))
+    all_observed = lax.all_to_all(own, "tm", 0, 0, tiled=True)
     vmem = pl.BlockSpec(memory_space=pltpu.VMEM)
     smem = pl.BlockSpec(memory_space=pltpu.SMEM)
     hbm = pl.BlockSpec(memory_space=pltpu.HBM)
@@ -193,7 +278,7 @@
             jax.ShapeDtypeStruct((1, n_rows, n_states), f32),
             jax.ShapeDtypeStruct((1, n_rows), f32),
         ],
-        in_specs=[smem, smem] + [hbm] * 6,
+        in_specs=[smem] + [hbm] * 6,
         out_specs=[hbm, vmem],
         scratch_shapes=[
             pltpu.SMEM((n_source, n_blocks), jnp.int32),
@@ -206,11 +291,18 @@
             pltpu.VMEM((n_states, LANES), f32),
             pltpu.VMEM((n_states, LANES), f32),
             pltpu.VMEM((n_blocks, size, n_source * size), bf16),
+            pltpu.VMEM((n_blocks, size, n_source * LANES), bf16),
+            pltpu.VMEM((n_rows // LANES, n_blocks, size + SUBLANES, LANES), f32),
             pltpu.VMEM((n_rows // LANES, n_blocks, size + SUBLANES, LANES), f32),
             pltpu.VMEM((n_states, n_rows), bf16),
             pltpu.VMEM((n_states, n_rows), bf16),
             pltpu.VMEM((LANES, n_states), f32),
             pltpu.VMEM((n_states, LANES), f32),
+            pltpu.VMEM((n_blocks, SUBLANES, LANES), f32),
+            pltpu.VMEM((steps, n_blocks, n_tm, LANES), f32),
+            [pltpu.VMEM((steps - l, n_blocks, n_tm, LANES), f32) for l in range(steps)],
+            [pltpu.VMEM((steps, n_blocks, n_tm, LANES), f32) for _ in range(n_source)],
+            pltpu.VMEM((n_tm, n_states), f32),
             pltpu.SemaphoreType.DMA((5,)),
             pltpu.SemaphoreType.DMA((4,)),
             pltpu.SemaphoreType.DMA((n_rows // LANES,)),
@@ -219,7 +311,6 @@
         cost_estimate=pl.CostEstimate(flops=1 << 34, bytes_accessed=4 << 20, transcendentals=0),
         name="chain",
     )(
-        place,
         all_observed,
         pattern.T,
         symbol_cluster,

time: 32.8 us -> 35.6 us (1.085)
  Pallas kernels: 21.8 us -> 25.8 us
  other arithmetic: 0.66 us -> 0 us
  blocking collectives: 8.82 us -> 8.18 us
    psum x1 -> x0, blocking collectives: 8.82 us -> none  [body(): all_observed = lax.psum(own, 'tm')]
    all_to_all x0 -> x1, blocking collectives: none -> 8.18 us  [body(): all_observed = lax.all_to_all(own, 'tm', 0, 0, tiled=True)]
    pallas_call x1, Pallas kernels: 21.8 us -> 25.8 us  [body(): pl.pallas_call(chain_kernel, out_shape=[jax.ShapeDtypeStruct((1, n_rows,...]
    broadcast_in_dim x0 -> x1, local copies, waits for them, and re-layouts: none -> 0.66 us  [body(): own = jnp.broadcast_to(observed[None, :], (n_tm, steps))]
    unnamed x2 -> x0, local copies, waits for them, and re-layouts: 0.65 us -> none
    another operation x1 -> x0, other arithmetic: 0.58 us -> none  [body(): jnp.stack([tm + 1, lax.axis_index('rows') * n_rows]).astype(jnp.int32)]
where the time goes in v6:
time: 35.6 us; the launch traced here: 35.3 us
  Pallas kernels  25.8 us (72%)
  blocking collectives  8.18 us (23%)
  local copies, waits for them, and re-layouts  0.66 us (2%)
  between operations  0.63 us (2%)
    pallas_call x1, Pallas kernels, body(): pl.pallas_call(chain_kernel, out_shape=[jax.ShapeDtypeStruct((1, n_rows,...  25.8 us
    all_to_all x1, blocking collectives, body(): all_observed = lax.all_to_all(own, 'tm', 0, 0, tiled=True)  8.18 us

profile of v6, /device:TPU:26, one launch (start us, length us, event | category | flops | bytes accessed | tf_op | source)
XLA Modules:
  0.0 35.3 jit_solution(13467958114221840990)
XLA Ops:
  0.6 0.7 %broadcast_in_dim.2 = s32[8,1,4]{2,1,0:T(1,128)S(1)} broadcast(s32[4]{0:T(128)} %param.7), dimensions={2} | broadcast | bytes 144 | tf_op jit(solution)/shard_map/broadcast_in_dim | solution.py:269
  1.3 8.2 %all_to_all.8 = s32[8,1,4]{2,1,0:T(1,128)} all-to-all(s32[8,1,4]{2,1,0:T(1,128)S(1)} %broadcast_in_dim.2), channel_id=1, replica_groups=mesh['tm'=8,'rows'=4] {'tm'}, dimensions={0} | all-to-all | bytes 256 | tf_op jit(solution)/shard_map/all_to_all | solution.py:270
  9.5 25.8 %chain.1 = (f32[1,256,1024]{2,1,0:T(8,128)}, f32[1,256]{1,0:T(1,128)}) custom-call(s32[8,4]{1,0:T(8,128)} %bitcast.3, s32[4,16]{1,0:T(4,128)} %bitcast.5, s32[256]{0:T(256)} %cluster_hbm.1, f32[1,1024]{1,0:T(1,128)} %bitcast.4, bf16[16,4,64,64]{3,2,1,0:T(8,128)(2,1)} %blocks_hbm.1, f32[16,1024]{1,0:T(8,128)} %cluster_emit_hbm.1, f32[256,1024]{1,0:T(8,128)} %symbol_hbm.1), custom_call_target="tpu_custom_call" | custom-call | flops 17179869184 | bytes 4194304 | tf_op jit(solution)/shard_map/chain/pallas_call | solution.py:275

commit v7 on v6

--- a/solution.py
+++ b/solution.py
@@ -15,45 +15,63 @@
     return jnp.broadcast_to(row, (LANES, row.shape[1])).T
 
 
+def twice(tile, at, size):
+    other = pltpu.roll(tile, size, 1)
+    low_half = lax.broadcasted_iota(jnp.int32, (1, LANES), 1) < size
+    return jnp.where(low_half, tile, other) if at == 0 else jnp.where(low_half, other, tile)
+
+
+def build_kernel(
+    pattern_ref, leave_ref, blocks_ref, weight_ref, stay_ref, stay_slab_ref, leave_col_ref
+):
+    n_blocks, n_source, size, _ = blocks_ref.shape
+    per = LANES // size
+    for j in range(n_blocks):
+        tile = leave_ref[:, j // per * LANES : (j // per + 1) * LANES]
+        tile = jnp.broadcast_to(1.0 - tile, (SUBLANES, LANES))
+        stay_slab_ref[j] = twice(tile, j % per, size)
+    leave_col = column(leave_ref[...])
+    leave_col_ref[...] = leave_col
+    for j in range(n_blocks):
+        own = leave_col[j * size : (j + 1) * size]
+        stay_ref[j * size : (j + 1) * size, :] = 1.0 - pltpu.roll(own, 1, 0)
+    for j in range(n_blocks):
+        parts = []
+        for k in range(n_source):
+            rows = pl.ds(pl.multiple_of(pattern_ref[k, j] * size, size), size)
+            parts.append(blocks_ref[j, k].astype(jnp.float32) * leave_col_ref[rows, :size])
+        weight_ref[j] = jnp.concatenate(parts, axis=0).T.astype(jnp.bfloat16)
+
+
 def chain_kernel(
     observed_ref,
-    pattern_hbm,
-    cluster_hbm,
-    leave_hbm,
-    blocks_hbm,
-    cluster_emit_hbm,
-    symbol_hbm,
+    pattern_ref,
+    cluster_ref,
+    cluster_emit_ref,
+    symbol_ref,
+    weight_ref,
+    stay_ref,
+    stay_slab_ref,
     rows_hbm,
     rate_ref,
-    pattern_ref,
-    cluster_ref,
-    leave_ref,
-    blocks_ref,
-    cluster_emit_ref,
-    symbol_ref,
     rows_ref,
-    leave_col_ref,
-    stay_ref,
-    weight_ref,
-    back_ref,
     cur_ref,
     base_ref,
     low_a_ref,
     low_b_ref,
     emit_ref,
     emit_col_ref,
-    stay_slab_ref,
     emit_slab_ref,
     sum_refs,
     part_refs,
     change_ref,
-    sems,
-    block_sems,
     out_sems,
 ):
     steps = observed_ref.shape[1]
     n_half, n_blocks, padded, _ = cur_ref.shape
-    size = blocks_ref.shape[-1]
+    size = weight_ref.shape[1]
+    per = LANES // size
+    low_half = lax.broadcasted_iota(jnp.int32, (1, LANES), 1) < size
     n_states = n_blocks * size
     n_rows = n_half * LANES
     n_source = pattern_ref.shape[0]
@@ -62,31 +80,6 @@
     row_start = lax.axis_index("rows") * n_rows
     lows = (low_a_ref, low_b_ref)
 
-    small = [
-        pltpu.make_async_copy(source, target, sems.at[i])
-        for i, (source, target) in enumerate(
-            [
-                (leave_hbm, leave_ref),
-                (pattern_hbm, pattern_ref),
-                (cluster_hbm, cluster_ref),
-                (cluster_emit_hbm, cluster_emit_ref),
-                (symbol_hbm, symbol_ref),
-            ]
-        )
-    ]
-    n_chunks = block_sems.shape[0]
-    per_chunk = n_blocks // n_chunks
-    chunks = [
-        pltpu.make_async_copy(
-            blocks_hbm.at[pl.ds(i * per_chunk, per_chunk)],
-            blocks_ref.at[pl.ds(i * per_chunk, per_chunk)],
-            block_sems.at[i],
-        )
-        for i in range(n_chunks)
-    ]
-    for copy in small[:2] + chunks + small[2:]:
-        copy.start()
-
     def store(target_ref, low_ref, j, h, new):
         target_ref[h, j, first:, :] = new
         target_ref[h, j, :first, :] = new[size - first :, :]
@@ -100,39 +93,6 @@
             store(base_ref, low_a_ref, j, h, start.astype(jnp.float32))
     emit_ref[...] = jnp.zeros_like(emit_ref)
 
-    per = LANES // size
-    low_half = lax.broadcasted_iota(jnp.int32, (1, LANES), 1) < size
-
-    def twice(tile, at):
-        other = pltpu.roll(tile, size, 1)
-        return jnp.where(low_half, tile, other) if at == 0 else jnp.where(low_half, other, tile)
-
-    small[0].wait()
-    for j in range(n_blocks):
-        tile = leave_ref[:, j // per * LANES : (j // per + 1) * LANES]
-        tile = jnp.broadcast_to(1.0 - tile, (SUBLANES, LANES))
-        stay_slab_ref[j] = twice(tile, j % per)
-    leave_col = column(leave_ref[...])
-    leave_col_ref[...] = leave_col
-    for j in range(n_blocks):
-        own = leave_col[j * size : (j + 1) * size]
-        stay_ref[j * size : (j + 1) * size, :] = 1.0 - pltpu.roll(own, 1, 0)
-    small[1].wait()
-    for j in range(n_blocks):
-        if j % per_chunk == 0:
-            chunks[j // per_chunk].wait()
-        parts = []
-        for k in range(n_source):
-            rows = pl.ds(pl.multiple_of(pattern_ref[k, j] * size, size), size)
-            parts.append(blocks_ref[j, k].astype(jnp.float32) * leave_col_ref[rows, :size])
-        moved = jnp.concatenate(parts, axis=0).T
-        weight_ref[j] = moved.astype(jnp.bfloat16)
-        for k in range(n_source):
-            tile = moved[:, k // per * LANES : (k // per + 1) * LANES]
-            back_ref[j, :, k * LANES : (k + 1) * LANES] = twice(tile, k % per).astype(jnp.bfloat16)
-    for copy in small[2:]:
-        copy.wait()
-
     n_tm = observed_ref.shape[0]
 
     def emission_of(g, s):
@@ -144,7 +104,7 @@
         emission = jnp.concatenate([emission_of(g, s) for g in range(n_tm)], axis=0)
         for j in range(n_blocks):
             tile = emission[:, j // per * LANES : (j // per + 1) * LANES]
-            emit_slab_ref[s, j] = twice(tile, j % per)
+            emit_slab_ref[s, j] = twice(tile, j % per, size)
     stays = [jnp.broadcast_to(stay_slab_ref[j][:1], (n_tm, LANES)) for j in range(n_blocks)]
 
     for l in range(steps):
@@ -160,18 +120,22 @@
                 images.append(image)
                 sum_refs[l][p, j] = stays[j] * pltpu.roll(image, LANES - 1, 1)
             images = jnp.concatenate(images, axis=0)[:, :size].astype(jnp.bfloat16)
-            moved = jnp.dot(images, back_ref[j], preferred_element_type=jnp.float32)
+            moved = jnp.dot(images, weight_ref[j], preferred_element_type=jnp.float32)
             for k in range(n_source):
-                part = moved[:, k * LANES : (k + 1) * LANES].reshape(n_pos, n_tm, LANES)
+                tile = moved[:, k // per * LANES : (k // per + 1) * LANES]
+                tile = tile.reshape(n_pos, n_tm, LANES)
                 source = pattern_ref[k, j]
                 for p in range(n_pos):
-                    part_refs[k][p, source] = part_refs[k][p, source] + part[p]
+                    part_refs[k][p, source] = part_refs[k][p, source] + tile[p]
         for j in range(n_blocks):
             for p in range(n_pos):
-                total = sum_refs[l][p, j]
-                for ref in part_refs:
-                    total = total + ref[p, j]
-                sum_refs[l][p, j] = total
+                sides = []
+                for i in range(per):
+                    sides.append(sum(ref[p, j] for ref in part_refs[i + per :: per]))
+                    sides[i] = sides[i] + part_refs[i][p, j]
+                total = jnp.where(low_half, sides[0], sides[1])
+                total = total + pltpu.roll(total, size, 1)
+                sum_refs[l][p, j] = sum_refs[l][p, j] + total
 
     changes = []
     for j in range(n_blocks):
@@ -264,60 +228,64 @@
     n_blocks, n_source, size, _ = trans_blocks.shape
     n_states = leave_rate.shape[0]
     steps = observed.shape[0]
+    n_tm = lax.axis_size("tm")
     n_rows = n_states // lax.axis_size("rows")
-    n_tm = lax.axis_size("tm")
-    own = jnp.broadcast_to(observed[None, :], (n_tm, steps))
-    all_observed = lax.all_to_all(own, "tm", 0, 0, tiled=True)
+    n_half = n_rows // LANES
+    own = jnp.pad(observed, (0, LANES - steps)).reshape(1, 1, LANES)
+    all_observed = lax.all_gather(own, "tm", axis=0, tiled=True)[:, 0, :steps]
     vmem = pl.BlockSpec(memory_space=pltpu.VMEM)
     smem = pl.BlockSpec(memory_space=pltpu.SMEM)
     hbm = pl.BlockSpec(memory_space=pltpu.HBM)
     f32, bf16 = jnp.float32, jnp.bfloat16
+    sources = pattern.T
+    weight, stay, stay_slab = pl.pallas_call(
+        build_kernel,
+        out_shape=[
+            jax.ShapeDtypeStruct((n_blocks, size, n_source * size), bf16),
+            jax.ShapeDtypeStruct((n_states, LANES), f32),
+            jax.ShapeDtypeStruct((n_blocks, SUBLANES, LANES), f32),
+        ],
+        in_specs=[smem, vmem, vmem],
+        out_specs=[vmem] * 3,
+        scratch_shapes=[pltpu.VMEM((n_states, LANES), f32)],
+        compiler_params=pltpu.CompilerParams(vmem_limit_bytes=16 << 20),
+        cost_estimate=pl.CostEstimate(flops=1 << 31, bytes_accessed=4 << 20, transcendentals=0),
+        name="build",
+    )(sources, leave_rate.reshape(1, n_states), trans_blocks)
     return pl.pallas_call(
         chain_kernel,
         out_shape=[
             jax.ShapeDtypeStruct((1, n_rows, n_states), f32),
             jax.ShapeDtypeStruct((1, n_rows), f32),
         ],
-        in_specs=[smem] + [hbm] * 6,
+        in_specs=[smem] * 3 + [vmem] * 5,
         out_specs=[hbm, vmem],
         scratch_shapes=[
-            pltpu.SMEM((n_source, n_blocks), jnp.int32),
-            pltpu.SMEM(symbol_cluster.shape, jnp.int32),
-            pltpu.VMEM((1, n_states), f32),
-            pltpu.VMEM(trans_blocks.shape, bf16),
-            pltpu.VMEM(cluster_emit.shape, f32),
-            pltpu.VMEM(symbol_emit.shape, f32),
             pltpu.VMEM((n_rows, n_states), f32),
-            pltpu.VMEM((n_states, LANES), f32),
-            pltpu.VMEM((n_states, LANES), f32),
-            pltpu.VMEM((n_blocks, size, n_source * size), bf16),
-            pltpu.VMEM((n_blocks, size, n_source * LANES), bf16),
-            pltpu.VMEM((n_rows // LANES, n_blocks, size + SUBLANES, LANES), f32),
-            pltpu.VMEM((n_rows // LANES, n_blocks, size + SUBLANES, LANES), f32),
+            pltpu.VMEM((n_half, n_blocks, size + SUBLANES, LANES), f32),
+            pltpu.VMEM((n_half, n_blocks, size + SUBLANES, LANES), f32),
             pltpu.VMEM((n_states, n_rows), bf16),
             pltpu.VMEM((n_states, n_rows), bf16),
             pltpu.VMEM((LANES, n_states), f32),
             pltpu.VMEM((n_states, LANES), f32),
-            pltpu.VMEM((n_blocks, SUBLANES, LANES), f32),
             pltpu.VMEM((steps, n_blocks, n_tm, LANES), f32),
             [pltpu.VMEM((steps - l, n_blocks, n_tm, LANES), f32) for l in range(steps)],
             [pltpu.VMEM((steps, n_blocks, n_tm, LANES), f32) for _ in range(n_source)],
             pltpu.VMEM((n_tm, n_states), f32),
-            pltpu.SemaphoreType.DMA((5,)),
-            pltpu.SemaphoreType.DMA((4,)),
-            pltpu.SemaphoreType.DMA((n_rows // LANES,)),
+            pltpu.SemaphoreType.DMA((n_half,)),
         ],
-        compiler_params=pltpu.CompilerParams(vmem_limit_bytes=60 << 20),
+        compiler_params=pltpu.CompilerParams(vmem_limit_bytes=32 << 20),
         cost_estimate=pl.CostEstimate(flops=1 << 34, bytes_accessed=4 << 20, transcendentals=0),
         name="chain",
     )(
         all_observed,
-        pattern.T,
+        sources,
         symbol_cluster,
-        leave_rate.reshape(1, n_states),
-        trans_blocks,
         cluster_emit,
         symbol_emit,
+        weight,
+        stay,
+        stay_slab,
     )
 
 

time: 35.6 us -> 45.4 us (1.28)
  blocking collectives: 8.18 us -> 16 us
  local copies, waits for them, and re-layouts: 0.66 us -> 3.25 us
  Pallas kernels: 25.8 us -> 25.2 us
    all_gather x0 -> x1, blocking collectives: none -> 16 us  [body(): all_observed = lax.all_gather(own, 'tm', axis=0, tiled=True)[:, 0, :steps]]
    all_to_all x1 -> x0, blocking collectives: 8.18 us -> none  [body(): all_observed = lax.all_to_all(own, 'tm', 0, 0, tiled=True)]
    unnamed x0 -> x15, local copies, waits for them, and re-layouts: none -> 3.25 us
    pallas_call x1, Pallas kernels: 25.8 us -> 24 us  [body(): pl.pallas_call(chain_kernel, out_shape=[jax.ShapeDtypeStruct((1, n_rows,...]
    pallas_call x0 -> x1, Pallas kernels: none -> 1.16 us  [body(): pl.pallas_call(build_kernel, out_shape=[jax.ShapeDtypeStruct((n_blocks, s...]
    broadcast_in_dim x1 -> x0, local copies, waits for them, and re-layouts: 0.66 us -> none  [body(): own = jnp.broadcast_to(observed[None, :], (n_tm, steps))]
where the time goes in v7:
time: 45.4 us; the launch traced here: 45.2 us
  Pallas kernels  25.2 us (56%)
  blocking collectives  16 us (35%)
  local copies, waits for them, and re-layouts  3.25 us (7%)
  between operations  0.66 us (1%)
    pallas_call x1, Pallas kernels, body(): pl.pallas_call(chain_kernel, out_shape=[jax.ShapeDtypeStruct((1, n_rows,...  24 us
    all_gather x1, blocking collectives, body(): all_observed = lax.all_gather(own, 'tm', axis=0, tiled=True)[:, 0, :steps]  16 us
    unnamed x15, local copies, waits for them, and re-layouts  3.25 us
    pallas_call x1, Pallas kernels, body(): pl.pallas_call(build_kernel, out_shape=[jax.ShapeDtypeStruct((n_blocks, s...  1.16 us

profile of v7, /device:TPU:26, one launch (start us, length us, event | category | flops | bytes accessed | tf_op | source)
XLA Modules:
  0.0 45.2 jit_solution(5665704963401895081)
XLA Ops:
  0.6 0.0 copy-start.6
  0.6 0.6 %copy-done.6 = s32[4]{0:T(128)S(1)} copy-done((s32[4]{0:T(128)S(1)}, s32[4]{0:T(128)}, u32[]{:S(2)}) %copy-start.6) | copy-done | bytes 40
  1.3 0.0 copy-start.3
  1.3 16.0 %all-gather.1 = s32[8,1,128]{2,1,0:T(1,128)S(1)} all-gather(s32[1,1,128]{2,1,0:T(1,128)S(1)} %pad_bitcast_fusion), channel_id=2, replica_groups=mesh['tm'=8,'rows'=4] {'tm'}, dimensions={0}, use_global_device_ids=true | all-gather | bytes 4608 | tf_op jit(solution)/shard_map/all_gather | solution.py:235
  17.3 0.0 copy-start.4
  17.3 0.0 copy-done.3
  17.3 0.7 %copy-done.4 = s32[16,4]{0,1:T(4,128)S(1)} copy-done((s32[16,4]{0,1:T(4,128)S(1)}, s32[16,4]{0,1:T(4,128)}, u32[]{:S(2)}) %copy-start.4) | copy-done | bytes 280
  18.0 0.0 copy-start
  18.0 1.2 %copy-done = bf16[16,4,64,64]{3,2,1,0:T(8,128)(2,1)S(1)} copy-done((bf16[16,4,64,64]{3,2,1,0:T(8,128)(2,1)S(1)}, bf16[16,4,64,64]{3,2,1,0:T(8,128)(2,1)}, u32[]{:S(2)}) %copy-start) | copy-done | bytes 524312
  19.2 0.0 copy-start.1
  19.2 0.0 copy-start.2
  19.3 1.2 %build.1 = (bf16[16,64,256]{2,1,0:T(8,128)(2,1)S(1)}, f32[1024,128]{1,0:T(8,128)S(1)}, f32[16,8,128]{2,1,0:T(8,128)S(1)}) custom-call(s32[4,16]{1,0:T(4,128)S(1)} %bitcast.8, f32[1,1024]{1,0:T(1,128)S(1)} %bitcast.7, bf16[16,4,64,64]{3,2,1,0:T(8,128)(2,1)S(1)} %copy-done), custom_call_target="tpu_custom_call" | custom-call | flops 2147483648 | bytes 4194304 | tf_op jit(solution)/shard_map/build/pallas_call | solution.py:241
  20.4 0.0 copy-start.5
  20.4 0.0 copy-done.1
  20.5 0.0 copy-done.2
  20.5 0.6 %copy-done.5 = s32[256]{0:T(256)S(1)} copy-done((s32[256]{0:T(256)S(1)}, s32[256]{0:T(256)}, u32[]{:S(2)}) %copy-start.5) | copy-done | bytes 1048
  21.1 24.0 %chain.1 = (f32[1,256,1024]{2,1,0:T(8,128)}, f32[1,256]{1,0:T(1,128)}) custom-call(s32[8,4]{1,0:T(8,128)S(1)} %bitcast.6, s32[4,16]{1,0:T(4,128)S(1)} %bitcast.9, s32[256]{0:T(256)S(1)} %copy-done.5, f32[16,1024]{1,0:T(8,128)S(1)} %copy-done.2, f32[256,1024]{1,0:T(8,128)S(1)} %copy-done.1, bf16[16,64,256]{2,1,0:T(8,128)(2,1)S(1)} %get-tuple-element.5.weight_ref, ...), custom_call_target="tpu_custom_call" | custom-call | flops 17179869184 | bytes 4194304 | tf_op jit(solution)/shard_map/chain/pallas_call | solution.py:255
  (1 shorter events, 0.0 us)
Async XLA Ops:
  0.6 0.7 %copy-start.6 = (s32[4]{0:T(128)S(1)}, s32[4]{0:T(128)}, u32[]{:S(2)}) copy-start(s32[4]{0:T(128)} %param.7) | copy-start | bytes 52
  1.3 16.1 %copy-start.3 = (f32[1024]{0:T(1024)S(1)}, f32[1024]{0:T(1024)}, u32[]{:S(2)}) copy-start(f32[1024]{0:T(1024)} %param.10) | copy-start | bytes 12292
  17.3 0.7 %copy-start.4 = (s32[16,4]{0,1:T(4,128)S(1)}, s32[16,4]{0,1:T(4,128)}, u32[]{:S(2)}) copy-start(s32[16,4]{0,1:T(4,128)} %param.8) | copy-start | bytes 772
  18.0 1.2 %copy-start = (bf16[16,4,64,64]{3,2,1,0:T(8,128)(2,1)S(1)}, bf16[16,4,64,64]{3,2,1,0:T(8,128)(2,1)}, u32[]{:S(2)}) copy-start(bf16[16,4,64,64]{3,2,1,0:T(8,128)(2,1)} %blocks_ref.1) | copy-start | bytes 1572868
  19.2 1.2 %copy-start.1 = (f32[256,1024]{1,0:T(8,128)S(1)}, f32[256,1024]{1,0:T(8,128)}, u32[]{:S(2)}) copy-start(f32[256,1024]{1,0:T(8,128)} %symbol_ref.1) | copy-start | bytes 3145732
  19.2 1.2 %copy-start.2 = (f32[16,1024]{1,0:T(8,128)S(1)}, f32[16,1024]{1,0:T(8,128)}, u32[]{:S(2)}) copy-start(f32[16,1024]{1,0:T(8,128)} %cluster_emit_ref.1) | copy-start | bytes 196612
  20.4 0.7 %copy-start.5 = (s32[256]{0:T(256)S(1)}, s32[256]{0:T(256)}, u32[]{:S(2)}) copy-start(s32[256]{0:T(256)} %cluster_ref.1) | copy-start | bytes 3076

commit v8 on v6

--- a/solution.py
+++ b/solution.py
@@ -13,6 +13,12 @@
 
 def column(row):
     return jnp.broadcast_to(row, (LANES, row.shape[1])).T
+
+
+def twice(tile, at, size):
+    other = pltpu.roll(tile, size, 1)
+    low_half = lax.broadcasted_iota(jnp.int32, (1, LANES), 1) < size
+    return jnp.where(low_half, tile, other) if at == 0 else jnp.where(low_half, other, tile)
 
 
 def chain_kernel(
@@ -35,13 +41,13 @@
     leave_col_ref,
     stay_ref,
     weight_ref,
-    back_ref,
     cur_ref,
     base_ref,
     low_a_ref,
     low_b_ref,
     emit_ref,
     emit_col_ref,
+    change_col_ref,
     stay_slab_ref,
     emit_slab_ref,
     sum_refs,
@@ -51,7 +57,7 @@
     block_sems,
     out_sems,
 ):
-    steps = observed_ref.shape[1]
+    n_tm, steps = observed_ref.shape
     n_half, n_blocks, padded, _ = cur_ref.shape
     size = blocks_ref.shape[-1]
     n_states = n_blocks * size
@@ -99,19 +105,18 @@
             start = state + j * size == row + (row_start + h * LANES)
             store(base_ref, low_a_ref, j, h, start.astype(jnp.float32))
     emit_ref[...] = jnp.zeros_like(emit_ref)
+    for refs in part_refs:
+        for ref in refs:
+            ref[...] = jnp.zeros_like(ref)
 
     per = LANES // size
     low_half = lax.broadcasted_iota(jnp.int32, (1, LANES), 1) < size
-
-    def twice(tile, at):
-        other = pltpu.roll(tile, size, 1)
-        return jnp.where(low_half, tile, other) if at == 0 else jnp.where(low_half, other, tile)
 
     small[0].wait()
     for j in range(n_blocks):
         tile = leave_ref[:, j // per * LANES : (j // per + 1) * LANES]
-        tile = jnp.broadcast_to(1.0 - tile, (SUBLANES, LANES))
-        stay_slab_ref[j] = twice(tile, j % per)
+        tile = jnp.broadcast_to(1.0 - tile, (n_tm, LANES))
+        stay_slab_ref[j] = twice(tile, j % per, size)
     leave_col = column(leave_ref[...])
     leave_col_ref[...] = leave_col
     for j in range(n_blocks):
@@ -125,84 +130,85 @@
         for k in range(n_source):
             rows = pl.ds(pl.multiple_of(pattern_ref[k, j] * size, size), size)
             parts.append(blocks_ref[j, k].astype(jnp.float32) * leave_col_ref[rows, :size])
-        moved = jnp.concatenate(parts, axis=0).T
-        weight_ref[j] = moved.astype(jnp.bfloat16)
-        for k in range(n_source):
-            tile = moved[:, k // per * LANES : (k // per + 1) * LANES]
-            back_ref[j, :, k * LANES : (k + 1) * LANES] = twice(tile, k % per).astype(jnp.bfloat16)
+        weight_ref[j] = jnp.concatenate(parts, axis=0).T.astype(jnp.bfloat16)
     for copy in small[2:]:
         copy.wait()
-
-    n_tm = observed_ref.shape[0]
 
     def emission_of(g, s):
         symbol = observed_ref[g, s]
         row = symbol_ref[pl.ds(symbol, 1), :]
         return row * cluster_emit_ref[pl.ds(cluster_ref[symbol], 1), :]
 
-    for s in range(steps):
-        emission = jnp.concatenate([emission_of(g, s) for g in range(n_tm)], axis=0)
-        for j in range(n_blocks):
-            tile = emission[:, j // per * LANES : (j // per + 1) * LANES]
-            emit_slab_ref[s, j] = twice(tile, j % per)
-    stays = [jnp.broadcast_to(stay_slab_ref[j][:1], (n_tm, LANES)) for j in range(n_blocks)]
-
-    for l in range(steps):
-        n_pos = steps - l
-        for ref in part_refs:
-            ref[...] = jnp.zeros_like(ref)
-        for j in range(n_blocks):
+    def find_changes():
+        rows = n_blocks * n_tm
+        stays = stay_slab_ref[...].reshape(rows, LANES)
+        for s in range(steps):
+            emission = jnp.concatenate([emission_of(g, s) for g in range(n_tm)], axis=0)
+            for j in range(n_blocks):
+                tile = emission[:, j // per * LANES : (j // per + 1) * LANES]
+                emit_slab_ref[s, j] = twice(tile, j % per, size)
+
+        def row_sums(l, p):
+            return sum_refs[l][p].reshape(rows, LANES)
+
+        for l in range(steps):
+            n_pos = steps - l
             images = []
             for p in range(n_pos):
-                image = emit_slab_ref[p, j]
+                image = emit_slab_ref[p].reshape(rows, LANES)
                 if l:
-                    image = image * sum_refs[l - 1][p + 1, j]
+                    image = image * row_sums(l - 1, p + 1)
                 images.append(image)
-                sum_refs[l][p, j] = stays[j] * pltpu.roll(image, LANES - 1, 1)
-            images = jnp.concatenate(images, axis=0)[:, :size].astype(jnp.bfloat16)
-            moved = jnp.dot(images, back_ref[j], preferred_element_type=jnp.float32)
-            for k in range(n_source):
-                part = moved[:, k * LANES : (k + 1) * LANES].reshape(n_pos, n_tm, LANES)
-                source = pattern_ref[k, j]
-                for p in range(n_pos):
-                    part_refs[k][p, source] = part_refs[k][p, source] + part[p]
-        for j in range(n_blocks):
+            for j in range(n_blocks):
+                own = [image[j * n_tm : (j + 1) * n_tm] for image in images]
+                own = jnp.concatenate(own, axis=0)[:, :size].astype(jnp.bfloat16)
+                moved = jnp.dot(own, weight_ref[j], preferred_element_type=jnp.float32)
+                for k in range(n_source):
+                    tile = moved[:, k // per * LANES : (k // per + 1) * LANES]
+                    tile = tile.reshape(n_pos, n_tm, LANES)
+                    ref = part_refs[l][k % per]
+                    source = pattern_ref[k, j]
+                    for p in range(n_pos):
+                        ref[p, source] = ref[p, source] + tile[p]
             for p in range(n_pos):
-                total = sum_refs[l][p, j]
-                for ref in part_refs:
-                    total = total + ref[p, j]
-                sum_refs[l][p, j] = total
-
-    changes = []
-    for j in range(n_blocks):
-        exact = jnp.ones((n_tm, LANES), jnp.float32)
+                sides = [ref[p].reshape(rows, LANES) for ref in part_refs[l]]
+                total = jnp.where(low_half, sides[0], sides[1])
+                total = total + pltpu.roll(total, size, 1)
+                total = total + stays * pltpu.roll(images[p], LANES - 1, 1)
+                sum_refs[l][p] = total.reshape(n_blocks, n_tm, LANES)
+
+        exact = jnp.ones((rows, LANES), jnp.float32)
         weight = exact
         deviation = []
         for s in range(steps):
-            row_sum = pltpu.roll(sum_refs[s][0, j], 1, 1)
+            row_sum = pltpu.roll(row_sums(s, 0), 1, 1)
             for q in range(s):
-                row_sum = row_sum + deviation[q] * sum_refs[s - q - 1][q + 1, j]
+                row_sum = row_sum + deviation[q] * row_sums(s - q - 1, q + 1)
                 row_sum = pltpu.roll(row_sum, 1, 1)
-            emission = emit_slab_ref[s, j]
-            exact = pltpu.roll(exact * stays[j], 1, 1) * emission
-            weight = pltpu.roll(weight * stays[j], 1, 1) * emission
+            emission = emit_slab_ref[s].reshape(rows, LANES)
+            exact = pltpu.roll(exact * stays, 1, 1) * emission
+            weight = pltpu.roll(weight * stays, 1, 1) * emission
             rounded = (weight * (n_states / row_sum)).astype(jnp.bfloat16).astype(jnp.float32)
             rounded = rounded * (row_sum * (1.0 / n_states))
             deviation.append(rounded - weight)
             weight = rounded
-        changes.append(weight - exact)
-    for m in range(n_states // LANES):
-        tile = changes[m * per + per - 1]
-        for i in range(per - 1):
-            tile = jnp.where(low_half, changes[m * per + i], tile)
-        change_ref[:, m * LANES : (m + 1) * LANES] = tile
-
-    def segment(g, carried):
+        change = (weight - exact).reshape(n_blocks, n_tm, LANES)
+        for m in range(n_states // LANES):
+            tile = change[m * per + per - 1]
+            for i in range(per - 1):
+                tile = jnp.where(low_half, change[m * per + i], tile)
+            change_ref[:, m * LANES : (m + 1) * LANES] = tile
+
+    def segment(g, carried, is_first=False):
         scale, log_scale = carried
         for s in range(steps):
             emit_ref[s : s + 1, :] = emission_of(g, s)
-        emit_ref[steps : steps + 1, :] = change_ref[pl.ds(g, 1), :]
+        if not is_first:
+            emit_ref[steps : steps + 1, :] = change_ref[pl.ds(g, 1), :]
         emit_col_ref[...] = emit_ref[...].T
+        if is_first:
+            find_changes()
+            change_col_ref[...] = column(change_ref[:1, :])
         sums = [jnp.zeros((SUBLANES, LANES), jnp.float32) for _ in range(n_half)]
         for s in range(steps):
             now, later = lows[s % 2], lows[(s + 1) % 2]
@@ -222,7 +228,11 @@
                 from_ref = base_ref if s == 0 else cur_ref
                 to_ref = base_ref if s == steps - 1 else cur_ref
                 if s == steps - 1:
-                    change = jnp.broadcast_to(emit_col_ref[states, steps : steps + 1], (size, LANES))
+                    if is_first:
+                        change = change_col_ref[states, :]
+                    else:
+                        change = emit_col_ref[states, steps : steps + 1]
+                        change = jnp.broadcast_to(change, (size, LANES))
                 for h in range(n_half):
                     part = slice(h * LANES, (h + 1) * LANES)
                     kept = from_ref[h, j, first - 1 : padded - 1, :] * stay
@@ -240,7 +250,8 @@
         return 1.0 / row_sum, log_scale + jnp.log(row_sum)
 
     ones = jnp.ones((1, n_rows), jnp.float32)
-    scale, log_scale = lax.fori_loop(0, n_segments, segment, (ones, jnp.zeros_like(ones)))
+    carried = segment(0, (ones, jnp.zeros_like(ones)), is_first=True)
+    scale, log_scale = lax.fori_loop(1, n_segments, segment, carried)
     scale = scale * n_states
     out = []
     for h in range(n_half):
@@ -291,17 +302,20 @@
             pltpu.VMEM((n_states, LANES), f32),
             pltpu.VMEM((n_states, LANES), f32),
             pltpu.VMEM((n_blocks, size, n_source * size), bf16),
-            pltpu.VMEM((n_blocks, size, n_source * LANES), bf16),
             pltpu.VMEM((n_rows // LANES, n_blocks, size + SUBLANES, LANES), f32),
             pltpu.VMEM((n_rows // LANES, n_blocks, size + SUBLANES, LANES), f32),
             pltpu.VMEM((n_states, n_rows), bf16),
             pltpu.VMEM((n_states, n_rows), bf16),
             pltpu.VMEM((LANES, n_states), f32),
             pltpu.VMEM((n_states, LANES), f32),
-            pltpu.VMEM((n_blocks, SUBLANES, LANES), f32),
+            pltpu.VMEM((n_states, LANES), f32),
+            pltpu.VMEM((n_blocks, n_tm, LANES), f32),
             pltpu.VMEM((steps, n_blocks, n_tm, LANES), f32),
             [pltpu.VMEM((steps - l, n_blocks, n_tm, LANES), f32) for l in range(steps)],
-            [pltpu.VMEM((steps, n_blocks, n_tm, LANES), f32) for _ in range(n_source)],
+            [
+                [pltpu.VMEM((steps - l, n_blocks, n_tm, LANES), f32) for _ in range(LANES // size)]
+                for l in range(steps)
+            ],
             pltpu.VMEM((n_tm, n_states), f32),
             pltpu.SemaphoreType.DMA((5,)),
             pltpu.SemaphoreType.DMA((4,)),

time: 35.6 us -> 33.9 us (0.952)
  Pallas kernels: 25.8 us -> 24.2 us
    pallas_call x1, Pallas kernels: 25.8 us -> 24.2 us  [body(): pl.pallas_call(chain_kernel, out_shape=[jax.ShapeDtypeStruct((1, n_rows,...]
where the time goes in v8:
time: 33.9 us; the launch traced here: 33.6 us
  Pallas kernels  24.2 us (71%)
  blocking collectives  8.18 us (24%)
  local copies, waits for them, and re-layouts  0.66 us (2%)
  between operations  0.63 us (2%)
    pallas_call x1, Pallas kernels, body(): pl.pallas_call(chain_kernel, out_shape=[jax.ShapeDtypeStruct((1, n_rows,...  24.2 us
    all_to_all x1, blocking collectives, body(): all_observed = lax.all_to_all(own, 'tm', 0, 0, tiled=True)  8.18 us

profile of v8, /device:TPU:26, one launch (start us, length us, event | category | flops | bytes accessed | tf_op | source)
XLA Modules:
  0.0 33.6 jit_solution(16808887072571798385)
XLA Ops:
  0.6 0.7 %broadcast_in_dim.2 = s32[8,1,4]{2,1,0:T(1,128)S(1)} broadcast(s32[4]{0:T(128)} %param.7), dimensions={2} | broadcast | bytes 144 | tf_op jit(solution)/shard_map/broadcast_in_dim | solution.py:280
  1.3 8.2 %all_to_all.8 = s32[8,1,4]{2,1,0:T(1,128)} all-to-all(s32[8,1,4]{2,1,0:T(1,128)S(1)} %broadcast_in_dim.2), channel_id=1, replica_groups=mesh['tm'=8,'rows'=4] {'tm'}, dimensions={0} | all-to-all | bytes 256 | tf_op jit(solution)/shard_map/all_to_all | solution.py:281
  9.5 24.2 %chain.1 = (f32[1,256,1024]{2,1,0:T(8,128)}, f32[1,256]{1,0:T(1,128)}) custom-call(s32[8,4]{1,0:T(8,128)} %bitcast.3, s32[4,16]{1,0:T(4,128)} %bitcast.5, s32[256]{0:T(256)} %cluster_hbm.1, f32[1,1024]{1,0:T(1,128)} %bitcast.4, bf16[16,4,64,64]{3,2,1,0:T(8,128)(2,1)} %blocks_hbm.1, f32[16,1024]{1,0:T(8,128)} %cluster_emit_hbm.1, f32[256,1024]{1,0:T(8,128)} %symbol_hbm.1), custom_call_target="tpu_custom_call" | custom-call | flops 17179869184 | bytes 4194304 | tf_op jit(solution)/shard_map/chain/pallas_call | solution.py:286

commit v9 on v8

--- a/solution.py
+++ b/solution.py
@@ -41,6 +41,7 @@
     leave_col_ref,
     stay_ref,
     weight_ref,
+    dense_ref,
     cur_ref,
     base_ref,
     low_a_ref,
@@ -105,6 +106,7 @@
             start = state + j * size == row + (row_start + h * LANES)
             store(base_ref, low_a_ref, j, h, start.astype(jnp.float32))
     emit_ref[...] = jnp.zeros_like(emit_ref)
+    dense_ref[...] = jnp.zeros_like(dense_ref)
     for refs in part_refs:
         for ref in refs:
             ref[...] = jnp.zeros_like(ref)
@@ -130,7 +132,15 @@
         for k in range(n_source):
             rows = pl.ds(pl.multiple_of(pattern_ref[k, j] * size, size), size)
             parts.append(blocks_ref[j, k].astype(jnp.float32) * leave_col_ref[rows, :size])
-        weight_ref[j] = jnp.concatenate(parts, axis=0).T.astype(jnp.bfloat16)
+        moved = jnp.concatenate(parts, axis=0).T.astype(jnp.bfloat16)
+        weight_ref[j] = moved
+        states = slice(j * size, (j + 1) * size)
+        moved = moved.astype(jnp.float32)
+        for k in range(n_source):
+            source = pattern_ref[k, j]
+            tile = twice(moved[:, k // per * LANES : (k // per + 1) * LANES], k % per, size)
+            tile = jnp.where(low_half == (source % per == 0), tile, 0.0).astype(jnp.bfloat16)
+            dense_ref[source // per, states, :] = dense_ref[source // per, states, :] + tile
     for copy in small[2:]:
         copy.wait()
 
@@ -212,17 +222,11 @@
         sums = [jnp.zeros((SUBLANES, LANES), jnp.float32) for _ in range(n_half)]
         for s in range(steps):
             now, later = lows[s % 2], lows[(s + 1) % 2]
+            dense = jnp.concatenate([dense_ref[m] for m in range(n_states // LANES)], axis=1)
+            all_moved = jnp.dot(dense, now[...], preferred_element_type=jnp.float32)
             for j in range(n_blocks):
                 states = slice(j * size, (j + 1) * size)
-                picked = [
-                    now[pl.ds(pl.multiple_of(pattern_ref[k, j] * size, size), size), :]
-                    for k in range(n_source)
-                ]
-                moved = jnp.dot(
-                    weight_ref[j],
-                    jnp.concatenate(picked, axis=0),
-                    preferred_element_type=jnp.float32,
-                )
+                moved = all_moved[states, :]
                 emission = jnp.broadcast_to(emit_col_ref[states, s : s + 1], (size, LANES))
                 stay = stay_ref[states, :]
                 from_ref = base_ref if s == 0 else cur_ref
@@ -302,6 +306,7 @@
             pltpu.VMEM((n_states, LANES), f32),
             pltpu.VMEM((n_states, LANES), f32),
             pltpu.VMEM((n_blocks, size, n_source * size), bf16),
+            pltpu.VMEM((n_states // LANES, n_states, LANES), bf16),
             pltpu.VMEM((n_rows // LANES, n_blocks, size + SUBLANES, LANES), f32),
             pltpu.VMEM((n_rows // LANES, n_blocks, size + SUBLANES, LANES), f32),
             pltpu.VMEM((n_states, n_rows), bf16),

time: 33.9 us -> 51.4 us (1.52)
  Pallas kernels: 24.2 us -> 41.6 us
    pallas_call x1, Pallas kernels: 24.2 us -> 41.6 us  [body(): pl.pallas_call(chain_kernel, out_shape=[jax.ShapeDtypeStruct((1, n_rows,...]
where the time goes in v9:
time: 51.4 us; the launch traced here: 51.1 us
  Pallas kernels  41.6 us (81%)
  blocking collectives  8.18 us (16%)
  local copies, waits for them, and re-layouts  0.66 us (1%)
  between operations  0.63 us (1%)
    pallas_call x1, Pallas kernels, body(): pl.pallas_call(chain_kernel, out_shape=[jax.ShapeDtypeStruct((1, n_rows,...  41.6 us
    all_to_all x1, blocking collectives, body(): all_observed = lax.all_to_all(own, 'tm', 0, 0, tiled=True)  8.18 us

profile of v9, /device:TPU:26, one launch (start us, length us, event | category | flops | bytes accessed | tf_op | source)
XLA Modules:
  0.0 51.1 jit_solution(13372591985298103506)
XLA Ops:
  0.6 0.7 %broadcast_in_dim.2 = s32[8,1,4]{2,1,0:T(1,128)S(1)} broadcast(s32[4]{0:T(128)} %param.7), dimensions={2} | broadcast | bytes 144 | tf_op jit(solution)/shard_map/broadcast_in_dim | solution.py:284
  1.3 8.2 %all_to_all.8 = s32[8,1,4]{2,1,0:T(1,128)} all-to-all(s32[8,1,4]{2,1,0:T(1,128)S(1)} %broadcast_in_dim.2), channel_id=1, replica_groups=mesh['tm'=8,'rows'=4] {'tm'}, dimensions={0} | all-to-all | bytes 256 | tf_op jit(solution)/shard_map/all_to_all | solution.py:285
  9.5 41.6 %chain.1 = (f32[1,256,1024]{2,1,0:T(8,128)}, f32[1,256]{1,0:T(1,128)}) custom-call(s32[8,4]{1,0:T(8,128)} %bitcast.3, s32[4,16]{1,0:T(4,128)} %bitcast.5, s32[256]{0:T(256)} %cluster_hbm.1, f32[1,1024]{1,0:T(1,128)} %bitcast.4, bf16[16,4,64,64]{3,2,1,0:T(8,128)(2,1)} %blocks_hbm.1, f32[16,1024]{1,0:T(8,128)} %cluster_emit_hbm.1, f32[256,1024]{1,0:T(8,128)} %symbol_hbm.1), custom_call_target="tpu_custom_call" | custom-call | flops 17179869184 | bytes 4194304 | tf_op jit(solution)/shard_map/chain/pallas_call | solution.py:290

commit v10 on v8

--- a/solution.py
+++ b/solution.py
@@ -41,6 +41,8 @@
     leave_col_ref,
     stay_ref,
     weight_ref,
+    stored_ref,
+    half_ref,
     cur_ref,
     base_ref,
     low_a_ref,
@@ -64,6 +66,7 @@
     n_rows = n_half * LANES
     n_source = pattern_ref.shape[0]
     first = padded - size
+    groups = size // SUBLANES
     n_segments = lax.axis_index("tm") + 1
     row_start = lax.axis_index("rows") * n_rows
     lows = (low_a_ref, low_b_ref)
@@ -93,17 +96,25 @@
     for copy in small[:2] + chunks + small[2:]:
         copy.start()
 
-    def store(target_ref, low_ref, j, h, new):
+    def store(target_ref, low_ref, j, h, new, ahead):
         target_ref[h, j, first:, :] = new
-        target_ref[h, j, :first, :] = new[size - first :, :]
+        for m in range(1, ahead + 1):
+            group = new[size - m * SUBLANES : size - (m - 1) * SUBLANES, :]
+            at = first - m * SUBLANES
+            target_ref[h, j, at : at + SUBLANES, :] = pltpu.roll(group, 1, 0)
         low_ref[j * size : (j + 1) * size, h * LANES : (h + 1) * LANES] = new.astype(jnp.bfloat16)
 
+    def stored_order(ref, j):
+        rows = [ref[pl.ds(j * size + m, SUBLANES, stride=groups), :] for m in range(groups)]
+        return jnp.concatenate(rows, axis=0)
+
     state = lax.broadcasted_iota(jnp.int32, (size, LANES), 0)
+    state = state % SUBLANES * groups + state // SUBLANES
     row = lax.broadcasted_iota(jnp.int32, (size, LANES), 1)
     for j in range(n_blocks):
         for h in range(n_half):
             start = state + j * size == row + (row_start + h * LANES)
-            store(base_ref, low_a_ref, j, h, start.astype(jnp.float32))
+            store(base_ref, low_a_ref, j, h, start.astype(jnp.float32), steps)
     emit_ref[...] = jnp.zeros_like(emit_ref)
     for refs in part_refs:
         for ref in refs:
@@ -121,7 +132,13 @@
     leave_col_ref[...] = leave_col
     for j in range(n_blocks):
         own = leave_col[j * size : (j + 1) * size]
-        stay_ref[j * size : (j + 1) * size, :] = 1.0 - pltpu.roll(own, 1, 0)
+        emit_col_ref[j * size : (j + 1) * size, :] = 1.0 - pltpu.roll(own, 1, 0)
+    for j in range(n_blocks):
+        stay_ref[j * size : (j + 1) * size, :] = stored_order(emit_col_ref, j)
+    row = lax.broadcasted_iota(jnp.int32, (size, size), 0)
+    col = lax.broadcasted_iota(jnp.int32, (size, size), 1)
+    to_stored = (col == row % SUBLANES * groups + row // SUBLANES).astype(jnp.float32)
+    to_stored = to_stored.astype(jnp.bfloat16)
     small[1].wait()
     for j in range(n_blocks):
         if j % per_chunk == 0:
@@ -130,7 +147,17 @@
         for k in range(n_source):
             rows = pl.ds(pl.multiple_of(pattern_ref[k, j] * size, size), size)
             parts.append(blocks_ref[j, k].astype(jnp.float32) * leave_col_ref[rows, :size])
-        weight_ref[j] = jnp.concatenate(parts, axis=0).T.astype(jnp.bfloat16)
+        weight = jnp.concatenate(parts, axis=0).T.astype(jnp.bfloat16)
+        weight_ref[j] = weight
+        weight = jnp.dot(to_stored, weight, preferred_element_type=jnp.float32)
+        half_ref[j * size : (j + 1) * size, :] = weight.astype(jnp.bfloat16)
+    width = n_source * size
+    row = lax.broadcasted_iota(jnp.int32, (width, width), 0)
+    col = lax.broadcasted_iota(jnp.int32, (width, width), 1)
+    source = col // size * size + col % SUBLANES * groups + col % size // SUBLANES
+    from_stored = (row == source).astype(jnp.float32).astype(jnp.bfloat16)
+    stored = jnp.dot(half_ref[...], from_stored, preferred_element_type=jnp.float32)
+    stored_ref[...] = stored.astype(jnp.bfloat16)
     for copy in small[2:]:
         copy.wait()
 
@@ -219,31 +246,31 @@
                     for k in range(n_source)
                 ]
                 moved = jnp.dot(
-                    weight_ref[j],
+                    stored_ref[states, :],
                     jnp.concatenate(picked, axis=0),
                     preferred_element_type=jnp.float32,
                 )
-                emission = jnp.broadcast_to(emit_col_ref[states, s : s + 1], (size, LANES))
+                columns = stored_order(emit_col_ref, j)
+                emission = jnp.broadcast_to(columns[:, s : s + 1], (size, LANES))
                 stay = stay_ref[states, :]
                 from_ref = base_ref if s == 0 else cur_ref
                 to_ref = base_ref if s == steps - 1 else cur_ref
                 if s == steps - 1:
                     if is_first:
-                        change = change_col_ref[states, :]
+                        change = stored_order(change_col_ref, j)
                     else:
-                        change = emit_col_ref[states, steps : steps + 1]
-                        change = jnp.broadcast_to(change, (size, LANES))
+                        change = jnp.broadcast_to(columns[:, steps : steps + 1], (size, LANES))
                 for h in range(n_half):
                     part = slice(h * LANES, (h + 1) * LANES)
-                    kept = from_ref[h, j, first - 1 : padded - 1, :] * stay
+                    kept = from_ref[h, j, first - SUBLANES : padded - SUBLANES, :] * stay
                     new = (kept + moved[:, part]) * emission
                     if s == 0:
                         new = new * scale[:, part]
                     if s == steps - 1:
-                        start = base_ref[h, j, first - steps : padded - steps, :]
+                        start = base_ref[h, j, first - steps * SUBLANES : padded - steps * SUBLANES, :]
                         new = new + start * change * scale[:, part]
                         sums[h] = sums[h] + jnp.sum(new.reshape(-1, SUBLANES, LANES), axis=0)
-                    store(to_ref, later, j, h, new)
+                    store(to_ref, later, j, h, new, steps if to_ref is base_ref else 1)
         if steps % 2:
             low_a_ref[...] = low_b_ref[...]
         row_sum = jnp.concatenate([jnp.sum(t, axis=0, keepdims=True) for t in sums], axis=1)
@@ -257,7 +284,11 @@
     for h in range(n_half):
         part = slice(h * LANES, (h + 1) * LANES)
         for j in range(n_states // LANES):
-            block = [base_ref[h, j * per + i, first:, :] for i in range(per)]
+            block = [
+                base_ref[h, j * per + i, pl.ds(first + q, groups, stride=SUBLANES), :]
+                for i in range(per)
+                for q in range(SUBLANES)
+            ]
             block = jnp.concatenate(block, axis=0) * scale[:, part]
             rows_ref[part, j * LANES : (j + 1) * LANES] = block.T
         rows = pl.ds(h * LANES, LANES)
@@ -302,8 +333,10 @@
             pltpu.VMEM((n_states, LANES), f32),
             pltpu.VMEM((n_states, LANES), f32),
             pltpu.VMEM((n_blocks, size, n_source * size), bf16),
-            pltpu.VMEM((n_rows // LANES, n_blocks, size + SUBLANES, LANES), f32),
-            pltpu.VMEM((n_rows // LANES, n_blocks, size + SUBLANES, LANES), f32),
+            pltpu.VMEM((n_states, n_source * size), bf16),
+            pltpu.VMEM((n_states, n_source * size), bf16),
+            pltpu.VMEM((n_rows // LANES, n_blocks, size + steps * SUBLANES, LANES), f32),
+            pltpu.VMEM((n_rows // LANES, n_blocks, size + steps * SUBLANES, LANES), f32),
             pltpu.VMEM((n_states, n_rows), bf16),
             pltpu.VMEM((n_states, n_rows), bf16),
             pltpu.VMEM((LANES, n_states), f32),

time: 33.9 us -> 35.7 us (1.053)
  Pallas kernels: 24.2 us -> 25.9 us
    pallas_call x1, Pallas kernels: 24.2 us -> 25.9 us  [body(): pl.pallas_call(chain_kernel, out_shape=[jax.ShapeDtypeStruct((1, n_rows,...]
where the time goes in v10:
time: 35.7 us; the launch traced here: 35.4 us
  Pallas kernels  25.9 us (73%)
  blocking collectives  8.18 us (23%)
  local copies, waits for them, and re-layouts  0.66 us (2%)
  between operations  0.63 us (2%)
    pallas_call x1, Pallas kernels, body(): pl.pallas_call(chain_kernel, out_shape=[jax.ShapeDtypeStruct((1, n_rows,...  25.9 us
    all_to_all x1, blocking collectives, body(): all_observed = lax.all_to_all(own, 'tm', 0, 0, tiled=True)  8.18 us

profile of v10, /device:TPU:26, one launch (start us, length us, event | category | flops | bytes accessed | tf_op | source)
XLA Modules:
  0.0 35.4 jit_solution(11016094916300964018)
XLA Ops:
  0.6 0.7 %broadcast_in_dim.2 = s32[8,1,4]{2,1,0:T(1,128)S(1)} broadcast(s32[4]{0:T(128)} %param.7), dimensions={2} | broadcast | bytes 144 | tf_op jit(solution)/shard_map/broadcast_in_dim | solution.py:311
  1.3 8.2 %all_to_all.8 = s32[8,1,4]{2,1,0:T(1,128)} all-to-all(s32[8,1,4]{2,1,0:T(1,128)S(1)} %broadcast_in_dim.2), channel_id=1, replica_groups=mesh['tm'=8,'rows'=4] {'tm'}, dimensions={0} | all-to-all | bytes 256 | tf_op jit(solution)/shard_map/all_to_all | solution.py:312
  9.5 25.9 %chain.1 = (f32[1,256,1024]{2,1,0:T(8,128)}, f32[1,256]{1,0:T(1,128)}) custom-call(s32[8,4]{1,0:T(8,128)} %bitcast.3, s32[4,16]{1,0:T(4,128)} %bitcast.5, s32[256]{0:T(256)} %cluster_hbm.1, f32[1,1024]{1,0:T(1,128)} %bitcast.4, bf16[16,4,64,64]{3,2,1,0:T(8,128)(2,1)} %blocks_hbm.1, f32[16,1024]{1,0:T(8,128)} %cluster_emit_hbm.1, f32[256,1024]{1,0:T(8,128)} %symbol_hbm.1), custom_call_target="tpu_custom_call" | custom-call | flops 17179869184 | bytes 4194304 | tf_op jit(solution)/shard_map/chain/pallas_call | solution.py:317

commit v11 on v7

--- a/solution.py
+++ b/solution.py
@@ -28,7 +28,7 @@
     per = LANES // size
     for j in range(n_blocks):
         tile = leave_ref[:, j // per * LANES : (j // per + 1) * LANES]
-        tile = jnp.broadcast_to(1.0 - tile, (SUBLANES, LANES))
+        tile = jnp.broadcast_to(1.0 - tile, stay_slab_ref.shape[1:])
         stay_slab_ref[j] = twice(tile, j % per, size)
     leave_col = column(leave_ref[...])
     leave_col_ref[...] = leave_col
@@ -61,17 +61,16 @@
     low_b_ref,
     emit_ref,
     emit_col_ref,
+    change_col_ref,
     emit_slab_ref,
     sum_refs,
     part_refs,
     change_ref,
     out_sems,
 ):
-    steps = observed_ref.shape[1]
+    n_tm, steps = observed_ref.shape
     n_half, n_blocks, padded, _ = cur_ref.shape
     size = weight_ref.shape[1]
-    per = LANES // size
-    low_half = lax.broadcasted_iota(jnp.int32, (1, LANES), 1) < size
     n_states = n_blocks * size
     n_rows = n_half * LANES
     n_source = pattern_ref.shape[0]
@@ -92,81 +91,88 @@
             start = state + j * size == row + (row_start + h * LANES)
             store(base_ref, low_a_ref, j, h, start.astype(jnp.float32))
     emit_ref[...] = jnp.zeros_like(emit_ref)
-
-    n_tm = observed_ref.shape[0]
+    for refs in part_refs:
+        for ref in refs:
+            ref[...] = jnp.zeros_like(ref)
+
+    per = LANES // size
+    low_half = lax.broadcasted_iota(jnp.int32, (1, LANES), 1) < size
 
     def emission_of(g, s):
-        symbol = observed_ref[g, s]
+        symbol = observed_ref[(n_segments - 1 - g + n_tm) % n_tm, s]
         row = symbol_ref[pl.ds(symbol, 1), :]
         return row * cluster_emit_ref[pl.ds(cluster_ref[symbol], 1), :]
 
-    for s in range(steps):
-        emission = jnp.concatenate([emission_of(g, s) for g in range(n_tm)], axis=0)
-        for j in range(n_blocks):
-            tile = emission[:, j // per * LANES : (j // per + 1) * LANES]
-            emit_slab_ref[s, j] = twice(tile, j % per, size)
-    stays = [jnp.broadcast_to(stay_slab_ref[j][:1], (n_tm, LANES)) for j in range(n_blocks)]
-
-    for l in range(steps):
-        n_pos = steps - l
-        for ref in part_refs:
-            ref[...] = jnp.zeros_like(ref)
-        for j in range(n_blocks):
+    def find_changes():
+        rows = n_blocks * n_tm
+        stays = stay_slab_ref[...].reshape(rows, LANES)
+        for s in range(steps):
+            emission = jnp.concatenate([emission_of(g, s) for g in range(n_tm)], axis=0)
+            for j in range(n_blocks):
+                tile = emission[:, j // per * LANES : (j // per + 1) * LANES]
+                emit_slab_ref[s, j] = twice(tile, j % per, size)
+
+        def row_sums(l, p):
+            return sum_refs[l][p].reshape(rows, LANES)
+
+        for l in range(steps):
+            n_pos = steps - l
             images = []
             for p in range(n_pos):
-                image = emit_slab_ref[p, j]
+                image = emit_slab_ref[p].reshape(rows, LANES)
                 if l:
-                    image = image * sum_refs[l - 1][p + 1, j]
+                    image = image * row_sums(l - 1, p + 1)
                 images.append(image)
-                sum_refs[l][p, j] = stays[j] * pltpu.roll(image, LANES - 1, 1)
-            images = jnp.concatenate(images, axis=0)[:, :size].astype(jnp.bfloat16)
-            moved = jnp.dot(images, weight_ref[j], preferred_element_type=jnp.float32)
-            for k in range(n_source):
-                tile = moved[:, k // per * LANES : (k // per + 1) * LANES]
-                tile = tile.reshape(n_pos, n_tm, LANES)
-                source = pattern_ref[k, j]
-                for p in range(n_pos):
-                    part_refs[k][p, source] = part_refs[k][p, source] + tile[p]
-        for j in range(n_blocks):
+            for j in range(n_blocks):
+                own = [image[j * n_tm : (j + 1) * n_tm] for image in images]
+                own = jnp.concatenate(own, axis=0)[:, :size].astype(jnp.bfloat16)
+                moved = jnp.dot(own, weight_ref[j], preferred_element_type=jnp.float32)
+                for k in range(n_source):
+                    tile = moved[:, k // per * LANES : (k // per + 1) * LANES]
+                    tile = tile.reshape(n_pos, n_tm, LANES)
+                    ref = part_refs[l][k % per]
+                    source = pattern_ref[k, j]
+                    for p in range(n_pos):
+                        ref[p, source] = ref[p, source] + tile[p]
             for p in range(n_pos):
-                sides = []
-                for i in range(per):
-                    sides.append(sum(ref[p, j] for ref in part_refs[i + per :: per]))
-                    sides[i] = sides[i] + part_refs[i][p, j]
+                sides = [ref[p].reshape(rows, LANES) for ref in part_refs[l]]
                 total = jnp.where(low_half, sides[0], sides[1])
                 total = total + pltpu.roll(total, size, 1)
-                sum_refs[l][p, j] = sum_refs[l][p, j] + total
-
-    changes = []
-    for j in range(n_blocks):
-        exact = jnp.ones((n_tm, LANES), jnp.float32)
+                total = total + stays * pltpu.roll(images[p], LANES - 1, 1)
+                sum_refs[l][p] = total.reshape(n_blocks, n_tm, LANES)
+
+        exact = jnp.ones((rows, LANES), jnp.float32)
         weight = exact
         deviation = []
         for s in range(steps):
-            row_sum = pltpu.roll(sum_refs[s][0, j], 1, 1)
+            row_sum = pltpu.roll(row_sums(s, 0), 1, 1)
             for q in range(s):
-                row_sum = row_sum + deviation[q] * sum_refs[s - q - 1][q + 1, j]
+                row_sum = row_sum + deviation[q] * row_sums(s - q - 1, q + 1)
                 row_sum = pltpu.roll(row_sum, 1, 1)
-            emission = emit_slab_ref[s, j]
-            exact = pltpu.roll(exact * stays[j], 1, 1) * emission
-            weight = pltpu.roll(weight * stays[j], 1, 1) * emission
+            emission = emit_slab_ref[s].reshape(rows, LANES)
+            exact = pltpu.roll(exact * stays, 1, 1) * emission
+            weight = pltpu.roll(weight * stays, 1, 1) * emission
             rounded = (weight * (n_states / row_sum)).astype(jnp.bfloat16).astype(jnp.float32)
             rounded = rounded * (row_sum * (1.0 / n_states))
             deviation.append(rounded - weight)
             weight = rounded
-        changes.append(weight - exact)
-    for m in range(n_states // LANES):
-        tile = changes[m * per + per - 1]
-        for i in range(per - 1):
-            tile = jnp.where(low_half, changes[m * per + i], tile)
-        change_ref[:, m * LANES : (m + 1) * LANES] = tile
-
-    def segment(g, carried):
+        change = (weight - exact).reshape(n_blocks, n_tm, LANES)
+        for m in range(n_states // LANES):
+            tile = change[m * per + per - 1]
+            for i in range(per - 1):
+                tile = jnp.where(low_half, change[m * per + i], tile)
+            change_ref[:, m * LANES : (m + 1) * LANES] = tile
+
+    def segment(g, carried, is_first=False):
         scale, log_scale = carried
         for s in range(steps):
             emit_ref[s : s + 1, :] = emission_of(g, s)
-        emit_ref[steps : steps + 1, :] = change_ref[pl.ds(g, 1), :]
+        if not is_first:
+            emit_ref[steps : steps + 1, :] = change_ref[pl.ds(g, 1), :]
         emit_col_ref[...] = emit_ref[...].T
+        if is_first:
+            find_changes()
+            change_col_ref[...] = column(change_ref[:1, :])
         sums = [jnp.zeros((SUBLANES, LANES), jnp.float32) for _ in range(n_half)]
         for s in range(steps):
             now, later = lows[s % 2], lows[(s + 1) % 2]
@@ -186,7 +192,11 @@
                 from_ref = base_ref if s == 0 else cur_ref
                 to_ref = base_ref if s == steps - 1 else cur_ref
                 if s == steps - 1:
-                    change = jnp.broadcast_to(emit_col_ref[states, steps : steps + 1], (size, LANES))
+                    if is_first:
+                        change = change_col_ref[states, :]
+                    else:
+                        change = emit_col_ref[states, steps : steps + 1]
+                        change = jnp.broadcast_to(change, (size, LANES))
                 for h in range(n_half):
                     part = slice(h * LANES, (h + 1) * LANES)
                     kept = from_ref[h, j, first - 1 : padded - 1, :] * stay
@@ -204,7 +214,8 @@
         return 1.0 / row_sum, log_scale + jnp.log(row_sum)
 
     ones = jnp.ones((1, n_rows), jnp.float32)
-    scale, log_scale = lax.fori_loop(0, n_segments, segment, (ones, jnp.zeros_like(ones)))
+    carried = segment(0, (ones, jnp.zeros_like(ones)), is_first=True)
+    scale, log_scale = lax.fori_loop(1, n_segments, segment, carried)
     scale = scale * n_states
     out = []
     for h in range(n_half):
@@ -231,8 +242,13 @@
     n_tm = lax.axis_size("tm")
     n_rows = n_states // lax.axis_size("rows")
     n_half = n_rows // LANES
-    own = jnp.pad(observed, (0, LANES - steps)).reshape(1, 1, LANES)
-    all_observed = lax.all_gather(own, "tm", axis=0, tiled=True)[:, 0, :steps]
+    all_observed = observed.reshape(1, steps)
+    while all_observed.shape[0] < n_tm:
+        distance = all_observed.shape[0]
+        route = [(i, i + distance) for i in range(n_tm - distance)]
+        earlier = lax.ppermute(all_observed, "tm", route)
+        all_observed = jnp.concatenate([all_observed, earlier], axis=0)
+    all_observed = all_observed[:n_tm]
     vmem = pl.BlockSpec(memory_space=pltpu.VMEM)
     smem = pl.BlockSpec(memory_space=pltpu.SMEM)
     hbm = pl.BlockSpec(memory_space=pltpu.HBM)
@@ -243,7 +259,7 @@
         out_shape=[
             jax.ShapeDtypeStruct((n_blocks, size, n_source * size), bf16),
             jax.ShapeDtypeStruct((n_states, LANES), f32),
-            jax.ShapeDtypeStruct((n_blocks, SUBLANES, LANES), f32),
+            jax.ShapeDtypeStruct((n_blocks, n_tm, LANES), f32),
         ],
         in_specs=[smem, vmem, vmem],
         out_specs=[vmem] * 3,
@@ -268,9 +284,13 @@
             pltpu.VMEM((n_states, n_rows), bf16),
             pltpu.VMEM((LANES, n_states), f32),
             pltpu.VMEM((n_states, LANES), f32),
+            pltpu.VMEM((n_states, LANES), f32),
             pltpu.VMEM((steps, n_blocks, n_tm, LANES), f32),
             [pltpu.VMEM((steps - l, n_blocks, n_tm, LANES), f32) for l in range(steps)],
-            [pltpu.VMEM((steps, n_blocks, n_tm, LANES), f32) for _ in range(n_source)],
+            [
+                [pltpu.VMEM((steps - l, n_blocks, n_tm, LANES), f32) for _ in range(LANES // size)]
+                for l in range(steps)
+            ],
             pltpu.VMEM((n_tm, n_states), f32),
             pltpu.SemaphoreType.DMA((n_half,)),
         ],

time: 45.4 us -> 42.3 us (0.932)
  blocking collectives: 16 us -> 0 us
  waiting for transfers between devices: 0 us -> 11 us
  starting transfers between devices: 0 us -> 3.86 us
  Pallas kernels: 25.2 us -> 23.9 us
  local copies, waits for them, and re-layouts: 3.25 us -> 2.54 us
    all_gather x1 -> x0, blocking collectives: 16 us -> none  [body(): all_observed = lax.all_gather(own, 'tm', axis=0, tiled=True)[:, 0, :steps]]
    ppermute x0 -> x3, waiting for transfers between devices: none -> 11 us  [body(): earlier = lax.ppermute(all_observed, 'tm', route)]
    ppermute x0 -> x3, starting transfers between devices: none -> 3.86 us  [body(): earlier = lax.ppermute(all_observed, 'tm', route)]
    pallas_call x1, Pallas kernels: 24 us -> 22.8 us  [body(): pl.pallas_call(chain_kernel, out_shape=[jax.ShapeDtypeStruct((1, n_rows,...]
    unnamed x15 -> x14, local copies, waits for them, and re-layouts: 3.25 us -> 2.54 us
  transfers between devices with their start and end apart: 0 -> 3, of which waited for: 0 -> 3; matrix products, arithmetic and copies ran while one was open for 0% -> 0% of each run, Pallas kernels for 0% -> 3%
where the time goes in v11:
time: 42.3 us; the launch traced here: 42.1 us
  Pallas kernels  23.9 us (57%)
  waiting for transfers between devices  11 us (26%)
  starting transfers between devices  3.86 us (9%)
  local copies, waits for them, and re-layouts  2.54 us (6%)
  between operations  0.74 us (2%)
    pallas_call x1, Pallas kernels, body(): pl.pallas_call(chain_kernel, out_shape=[jax.ShapeDtypeStruct((1, n_rows,...  22.8 us
    ppermute x3, waiting for transfers between devices, body(): earlier = lax.ppermute(all_observed, 'tm', route)  11 us
    ppermute x3, starting transfers between devices, body(): earlier = lax.ppermute(all_observed, 'tm', route)  3.86 us
    unnamed x14, local copies, waits for them, and re-layouts  2.54 us
    pallas_call x1, Pallas kernels, body(): pl.pallas_call(build_kernel, out_shape=[jax.ShapeDtypeStruct((n_blocks, s...  1.16 us
  transfers between devices with their start and end apart: 3, of which 3 were waited for; matrix products, arithmetic and copies ran while one was open for 0% of the time, Pallas kernels for 3%

profile of v11, /device:TPU:26, one launch (start us, length us, event | category | flops | bytes accessed | tf_op | source)
XLA Modules:
  0.0 42.1 jit_solution(6592987064350952746)
XLA Ops:
  0.6 0.0 copy-start.6
  0.6 0.6 %copy-done.6 = s32[4]{0:T(128)S(1)} copy-done((s32[4]{0:T(128)S(1)}, s32[4]{0:T(128)}, u32[]{:S(2)}) %copy-start.6) | copy-done | bytes 40
  1.3 1.3 %collective-permute-start = (s32[1,4]{1,0:T(1,128)S(1)}, s32[1,4]{1,0:T(1,128)S(1)}, u32[]{:S(2)}, u32[]{:S(2)}) collective-permute-start(s32[1,4]{1,0:T(1,128)S(1)} %bitcast.6), channel_id=1, source_target_pairs={{0,4},{4,8},{8,12},{12,16},{16,20},{20,24},{24,28},{1,5},{5,9},{9,... | collective-permute-start | bytes 56 | tf_op jit(solution)/shard_map/ppermute | solution.py:249
  2.6 4.1 %collective-permute-done = s32[1,4]{1,0:T(1,128)S(1)} collective-permute-done((s32[1,4]{1,0:T(1,128)S(1)}, s32[1,4]{1,0:T(1,128)S(1)}, u32[]{:S(2)}, u32[]{:S(2)}) %collective-permute-start) | collective-permute-done | bytes 48 | tf_op jit(solution)/shard_map/ppermute | solution.py:249
  6.7 0.0 copy-start.3
  6.7 1.3 %collective-permute-start.1 = (s32[2,4]{1,0:T(2,128)S(1)}, s32[2,4]{1,0:T(2,128)S(1)}, u32[]{:S(2)}, u32[]{:S(2)}) collective-permute-start(s32[2,4]{1,0:T(2,128)S(1)} %pad_add_fusion.2), channel_id=1, source_target_pairs={{0,8},{4,12},{8,16},{12,20},{16,24},{20,28},{1,9},{5,13},{9,17},{1... | collective-permute-start | bytes 104 | tf_op jit(solution)/shard_map/ppermute | solution.py:249
  8.0 4.2 %collective-permute-done.1 = s32[2,4]{1,0:T(2,128)S(1)} collective-permute-done((s32[2,4]{1,0:T(2,128)S(1)}, s32[2,4]{1,0:T(2,128)S(1)}, u32[]{:S(2)}, u32[]{:S(2)}) %collective-permute-start.1) | collective-permute-done | bytes 64 | tf_op jit(solution)/shard_map/ppermute | solution.py:249
  12.2 0.0 copy-start.4
  12.2 1.3 %collective-permute-start.2 = (s32[4,4]{1,0:T(4,128)S(1)}, s32[4,4]{1,0:T(4,128)S(1)}, u32[]{:S(2)}, u32[]{:S(2)}) collective-permute-start(s32[4,4]{1,0:T(4,128)S(1)} %pad_add_fusion.1), channel_id=1, source_target_pairs={{0,16},{4,20},{8,24},{12,28},{1,17},{5,21},{9,25},{13,29},{2,18},{... | collective-permute-start | bytes 200 | tf_op jit(solution)/shard_map/ppermute | solution.py:249
  13.5 0.0 copy-done.3
  13.5 0.0 copy-done.4
  13.5 0.0 copy-start
  13.5 1.2 %copy-done = bf16[16,4,64,64]{3,2,1,0:T(8,128)(2,1)S(1)} copy-done((bf16[16,4,64,64]{3,2,1,0:T(8,128)(2,1)S(1)}, bf16[16,4,64,64]{3,2,1,0:T(8,128)(2,1)}, u32[]{:S(2)}) %copy-start) | copy-done | bytes 524312
  14.8 0.0 copy-start.1
  14.8 0.0 copy-start.2
  14.8 1.2 %build.1 = (bf16[16,64,256]{2,1,0:T(8,128)(2,1)S(1)}, f32[1024,128]{1,0:T(8,128)S(1)}, f32[16,8,128]{2,1,0:T(8,128)S(1)}) custom-call(s32[4,16]{1,0:T(4,128)S(1)} %bitcast.4, f32[1,1024]{1,0:T(1,128)S(1)} %bitcast.3, bf16[16,4,64,64]{3,2,1,0:T(8,128)(2,1)S(1)} %copy-done), custom_call_target="tpu_custom_call" | custom-call | flops 2147483648 | bytes 4194304 | tf_op jit(solution)/shard_map/build/pallas_call | solution.py:257
  15.9 2.7 %collective-permute-done.2 = s32[4,4]{1,0:T(4,128)S(1)} collective-permute-done((s32[4,4]{1,0:T(4,128)S(1)}, s32[4,4]{1,0:T(4,128)S(1)}, u32[]{:S(2)}, u32[]{:S(2)}) %collective-permute-start.2) | collective-permute-done | bytes 96 | tf_op jit(solution)/shard_map/ppermute | solution.py:249
  18.6 0.0 copy-start.5
  18.6 0.0 copy-done.1
  18.6 0.0 copy-done.2
  18.6 0.7 %copy-done.5 = s32[256]{0:T(256)S(1)} copy-done((s32[256]{0:T(256)S(1)}, s32[256]{0:T(256)}, u32[]{:S(2)}) %copy-start.5) | copy-done | bytes 1048
  19.3 22.8 %chain.1 = (f32[1,256,1024]{2,1,0:T(8,128)}, f32[1,256]{1,0:T(1,128)}) custom-call(s32[8,4]{1,0:T(8,128)S(1)} %pad_add_fusion.observed_ref, s32[4,16]{1,0:T(4,128)S(1)} %bitcast.5, s32[256]{0:T(256)S(1)} %copy-done.5, f32[16,1024]{1,0:T(8,128)S(1)} %copy-done.2, f32[256,1024]{1,0:T(8,128)S(1)} %copy-done.1, ...), custom_call_target="tpu_custom_call" | custom-call | flops 17179869184 | bytes 4194304 | tf_op jit(solution)/shard_map/chain/pallas_call | solution.py:271
  (3 shorter events, 0.0 us)
Async XLA Ops:
  0.6 0.7 %copy-start.6 = (s32[4]{0:T(128)S(1)}, s32[4]{0:T(128)}, u32[]{:S(2)}) copy-start(s32[4]{0:T(128)} %param.7) | copy-start | bytes 52
  1.3 5.4 %collective-permute-start = (s32[1,4]{1,0:T(1,128)S(1)}, s32[1,4]{1,0:T(1,128)S(1)}, u32[]{:S(2)}, u32[]{:S(2)}) collective-permute-start(s32[1,4]{1,0:T(1,128)S(1)} %bitcast.6), channel_id=1, source_target_pairs={{0,4},{4,8},{8,12},{12,16},{16,20},{20,24},{24,28},{1,5},{5,9},{9,... | collective-permute-start | bytes 56 | tf_op jit(solution)/shard_map/ppermute | solution.py:249
  6.7 6.8 %copy-start.3 = (f32[1024]{0:T(1024)S(1)}, f32[1024]{0:T(1024)}, u32[]{:S(2)}) copy-start(f32[1024]{0:T(1024)} %param.10) | copy-start | bytes 12292
  6.7 5.5 %collective-permute-start.1 = (s32[2,4]{1,0:T(2,128)S(1)}, s32[2,4]{1,0:T(2,128)S(1)}, u32[]{:S(2)}, u32[]{:S(2)}) collective-permute-start(s32[2,4]{1,0:T(2,128)S(1)} %pad_add_fusion.2), channel_id=1, source_target_pairs={{0,8},{4,12},{8,16},{12,20},{16,24},{20,28},{1,9},{5,13},{9,17},{1... | collective-permute-start | bytes 104 | tf_op jit(solution)/shard_map/ppermute | solution.py:249
  12.2 1.3 %copy-start.4 = (s32[16,4]{0,1:T(4,128)S(1)}, s32[16,4]{0,1:T(4,128)}, u32[]{:S(2)}) copy-start(s32[16,4]{0,1:T(4,128)} %param.8) | copy-start | bytes 772
  12.2 6.4 %collective-permute-start.2 = (s32[4,4]{1,0:T(4,128)S(1)}, s32[4,4]{1,0:T(4,128)S(1)}, u32[]{:S(2)}, u32[]{:S(2)}) collective-permute-start(s32[4,4]{1,0:T(4,128)S(1)} %pad_add_fusion.1), channel_id=1, source_target_pairs={{0,16},{4,20},{8,24},{12,28},{1,17},{5,21},{9,25},{13,29},{2,18},{... | collective-permute-start | bytes 200 | tf_op jit(solution)/shard_map/ppermute | solution.py:249
  13.5 1.2 %copy-start = (bf16[16,4,64,64]{3,2,1,0:T(8,128)(2,1)S(1)}, bf16[16,4,64,64]{3,2,1,0:T(8,128)(2,1)}, u32[]{:S(2)}) copy-start(bf16[16,4,64,64]{3,2,1,0:T(8,128)(2,1)} %blocks_ref.1) | copy-start | bytes 1572868
  14.8 3.9 %copy-start.1 = (f32[256,1024]{1,0:T(8,128)S(1)}, f32[256,1024]{1,0:T(8,128)}, u32[]{:S(2)}) copy-start(f32[256,1024]{1,0:T(8,128)} %symbol_ref.1) | copy-start | bytes 3145732
  14.8 3.9 %copy-start.2 = (f32[16,1024]{1,0:T(8,128)S(1)}, f32[16,1024]{1,0:T(8,128)}, u32[]{:S(2)}) copy-start(f32[16,1024]{1,0:T(8,128)} %cluster_emit_ref.1) | copy-start | bytes 196612
  18.6 0.7 %copy-start.5 = (s32[256]{0:T(256)S(1)}, s32[256]{0:T(256)}, u32[]{:S(2)}) copy-start(s32[256]{0:T(256)} %cluster_ref.1) | copy-start | bytes 3076

commit v12 on v8

--- a/solution.py
+++ b/solution.py
@@ -96,14 +96,27 @@
     def store(target_ref, low_ref, j, h, new):
         target_ref[h, j, first:, :] = new
         target_ref[h, j, :first, :] = new[size - first :, :]
-        low_ref[j * size : (j + 1) * size, h * LANES : (h + 1) * LANES] = new.astype(jnp.bfloat16)
+        if low_ref is not None:
+            rows, part = slice(j * size, (j + 1) * size), slice(h * LANES, (h + 1) * LANES)
+            low_ref[rows, part] = new.astype(jnp.bfloat16)
 
     state = lax.broadcasted_iota(jnp.int32, (size, LANES), 0)
     row = lax.broadcasted_iota(jnp.int32, (size, LANES), 1)
     for j in range(n_blocks):
         for h in range(n_half):
             start = state + j * size == row + (row_start + h * LANES)
-            store(base_ref, low_a_ref, j, h, start.astype(jnp.float32))
+            store(base_ref, None, j, h, start.astype(jnp.float32))
+
+    def moved_from_identity(j):
+        own = [jnp.zeros((size, LANES), jnp.float32) for _ in range(n_half)]
+        lane_block = lax.broadcasted_iota(jnp.int32, (size, LANES), 1) // size + row_start // size
+        for k in range(n_source):
+            tile = weight_ref[j, :, k // per * LANES : (k // per + 1) * LANES]
+            tile = twice(tile.astype(jnp.float32), k % per, size)
+            for h in range(n_half):
+                here = lane_block + h * per == pattern_ref[k, j]
+                own[h] = own[h] + jnp.where(here, tile, 0.0)
+        return jnp.concatenate(own, axis=1)
     emit_ref[...] = jnp.zeros_like(emit_ref)
     for refs in part_refs:
         for ref in refs:
@@ -214,15 +227,18 @@
             now, later = lows[s % 2], lows[(s + 1) % 2]
             for j in range(n_blocks):
                 states = slice(j * size, (j + 1) * size)
-                picked = [
-                    now[pl.ds(pl.multiple_of(pattern_ref[k, j] * size, size), size), :]
-                    for k in range(n_source)
-                ]
-                moved = jnp.dot(
-                    weight_ref[j],
-                    jnp.concatenate(picked, axis=0),
-                    preferred_element_type=jnp.float32,
-                )
+                if is_first and s == 0:
+                    moved = moved_from_identity(j)
+                else:
+                    picked = [
+                        now[pl.ds(pl.multiple_of(pattern_ref[k, j] * size, size), size), :]
+                        for k in range(n_source)
+                    ]
+                    moved = jnp.dot(
+                        weight_ref[j],
+                        jnp.concatenate(picked, axis=0),
+                        preferred_element_type=jnp.float32,
+                    )
                 emission = jnp.broadcast_to(emit_col_ref[states, s : s + 1], (size, LANES))
                 stay = stay_ref[states, :]
                 from_ref = base_ref if s == 0 else cur_ref
@@ -237,11 +253,11 @@
                     part = slice(h * LANES, (h + 1) * LANES)
                     kept = from_ref[h, j, first - 1 : padded - 1, :] * stay
                     new = (kept + moved[:, part]) * emission
-                    if s == 0:
-                        new = new * scale[:, part]
                     if s == steps - 1:
                         start = base_ref[h, j, first - steps : padded - steps, :]
-                        new = new + start * change * scale[:, part]
+                        new = new + start * change
+                        if not is_first:
+                            new = new * scale[:, part]
                         sums[h] = sums[h] + jnp.sum(new.reshape(-1, SUBLANES, LANES), axis=0)
                     store(to_ref, later, j, h, new)
         if steps % 2:
@@ -254,17 +270,22 @@
     scale, log_scale = lax.fori_loop(1, n_segments, segment, carried)
     scale = scale * n_states
     out = []
+    n_tiles = n_states // LANES
+    per_out = n_half * n_tiles // out_sems.shape[0]
     for h in range(n_half):
         part = slice(h * LANES, (h + 1) * LANES)
-        for j in range(n_states // LANES):
+        for j in range(n_tiles):
             block = [base_ref[h, j * per + i, first:, :] for i in range(per)]
             block = jnp.concatenate(block, axis=0) * scale[:, part]
             rows_ref[part, j * LANES : (j + 1) * LANES] = block.T
-        rows = pl.ds(h * LANES, LANES)
-        out.append(
-            pltpu.make_async_copy(rows_ref.at[rows], rows_hbm.at[0, rows], out_sems.at[h])
-        )
-        out[-1].start()
+            if (j + 1) % per_out == 0:
+                rows = pl.ds(h * LANES, LANES)
+                cols = pl.ds((j + 1 - per_out) * LANES, per_out * LANES)
+                sem = out_sems.at[len(out)]
+                out.append(
+                    pltpu.make_async_copy(rows_ref.at[rows, cols], rows_hbm.at[0, rows, cols], sem)
+                )
+                out[-1].start()
     divisor = (n_segments * steps).astype(jnp.float32)
     rate_ref[...] = (log_scale - jnp.log(jnp.full_like(ones, n_states))) / divisor
     for copy in out:
@@ -319,7 +340,7 @@
             pltpu.VMEM((n_tm, n_states), f32),
             pltpu.SemaphoreType.DMA((5,)),
             pltpu.SemaphoreType.DMA((4,)),
-            pltpu.SemaphoreType.DMA((n_rows // LANES,)),
+            pltpu.SemaphoreType.DMA((2 * n_rows // LANES,)),
         ],
         compiler_params=pltpu.CompilerParams(vmem_limit_bytes=60 << 20),
         cost_estimate=pl.CostEstimate(flops=1 << 34, bytes_accessed=4 << 20, transcendentals=0),

time: 33.9 us -> 33.5 us (0.988)
  Pallas kernels: 24.2 us -> 23.8 us
    pallas_call x1, Pallas kernels: 24.2 us -> 23.8 us  [body(): pl.pallas_call(chain_kernel, out_shape=[jax.ShapeDtypeStruct((1, n_rows,...]
where the time goes in v12:
time: 33.5 us; the launch traced here: 33.3 us
  Pallas kernels  23.8 us (71%)
  blocking collectives  8.18 us (24%)
  local copies, waits for them, and re-layouts  0.66 us (2%)
  between operations  0.63 us (2%)
    pallas_call x1, Pallas kernels, body(): pl.pallas_call(chain_kernel, out_shape=[jax.ShapeDtypeStruct((1, n_rows,...  23.8 us
    all_to_all x1, blocking collectives, body(): all_observed = lax.all_to_all(own, 'tm', 0, 0, tiled=True)  8.18 us

profile of v12, /device:TPU:26, one launch (start us, length us, event | category | flops | bytes accessed | tf_op | source)
XLA Modules:
  0.0 33.3 jit_solution(17767354029161113365)
XLA Ops:
  0.6 0.7 %broadcast_in_dim.2 = s32[8,1,4]{2,1,0:T(1,128)S(1)} broadcast(s32[4]{0:T(128)} %param.7), dimensions={2} | broadcast | bytes 144 | tf_op jit(solution)/shard_map/broadcast_in_dim | solution.py:301
  1.3 8.2 %all_to_all.8 = s32[8,1,4]{2,1,0:T(1,128)} all-to-all(s32[8,1,4]{2,1,0:T(1,128)S(1)} %broadcast_in_dim.2), channel_id=1, replica_groups=mesh['tm'=8,'rows'=4] {'tm'}, dimensions={0} | all-to-all | bytes 256 | tf_op jit(solution)/shard_map/all_to_all | solution.py:302
  9.5 23.8 %chain.1 = (f32[1,256,1024]{2,1,0:T(8,128)}, f32[1,256]{1,0:T(1,128)}) custom-call(s32[8,4]{1,0:T(8,128)} %bitcast.3, s32[4,16]{1,0:T(4,128)} %bitcast.5, s32[256]{0:T(256)} %cluster_hbm.1, f32[1,1024]{1,0:T(1,128)} %bitcast.4, bf16[16,4,64,64]{3,2,1,0:T(8,128)(2,1)} %blocks_hbm.1, f32[16,1024]{1,0:T(8,128)} %cluster_emit_hbm.1, f32[256,1024]{1,0:T(8,128)} %symbol_hbm.1), custom_call_target="tpu_custom_call" | custom-call | flops 17179869184 | bytes 4194304 | tf_op jit(solution)/shard_map/chain/pallas_call | solution.py:307

commit v13 on v12

--- a/solution.py
+++ b/solution.py
@@ -90,7 +90,7 @@
         )
         for i in range(n_chunks)
     ]
-    for copy in small[:2] + chunks + small[2:]:
+    for copy in small + chunks:
         copy.start()
 
     def store(target_ref, low_ref, j, h, new):
@@ -135,8 +135,10 @@
     for j in range(n_blocks):
         own = leave_col[j * size : (j + 1) * size]
         stay_ref[j * size : (j + 1) * size, :] = 1.0 - pltpu.roll(own, 1, 0)
-    small[1].wait()
-    for j in range(n_blocks):
+    for copy in small[1:]:
+        copy.wait()
+
+    def build(j):
         if j % per_chunk == 0:
             chunks[j // per_chunk].wait()
         parts = []
@@ -144,8 +146,6 @@
             rows = pl.ds(pl.multiple_of(pattern_ref[k, j] * size, size), size)
             parts.append(blocks_ref[j, k].astype(jnp.float32) * leave_col_ref[rows, :size])
         weight_ref[j] = jnp.concatenate(parts, axis=0).T.astype(jnp.bfloat16)
-    for copy in small[2:]:
-        copy.wait()
 
     def emission_of(g, s):
         symbol = observed_ref[g, s]
@@ -160,6 +160,7 @@
             for j in range(n_blocks):
                 tile = emission[:, j // per * LANES : (j // per + 1) * LANES]
                 emit_slab_ref[s, j] = twice(tile, j % per, size)
+        yield
 
         def row_sums(l, p):
             return sum_refs[l][p].reshape(rows, LANES)
@@ -183,12 +184,14 @@
                     source = pattern_ref[k, j]
                     for p in range(n_pos):
                         ref[p, source] = ref[p, source] + tile[p]
+                yield
             for p in range(n_pos):
                 sides = [ref[p].reshape(rows, LANES) for ref in part_refs[l]]
                 total = jnp.where(low_half, sides[0], sides[1])
                 total = total + pltpu.roll(total, size, 1)
                 total = total + stays * pltpu.roll(images[p], LANES - 1, 1)
                 sum_refs[l][p] = total.reshape(n_blocks, n_tm, LANES)
+            yield
 
         exact = jnp.ones((rows, LANES), jnp.float32)
         weight = exact
@@ -205,6 +208,7 @@
             rounded = rounded * (row_sum * (1.0 / n_states))
             deviation.append(rounded - weight)
             weight = rounded
+            yield
         change = (weight - exact).reshape(n_blocks, n_tm, LANES)
         for m in range(n_states // LANES):
             tile = change[m * per + per - 1]
@@ -219,13 +223,22 @@
         if not is_first:
             emit_ref[steps : steps + 1, :] = change_ref[pl.ds(g, 1), :]
         emit_col_ref[...] = emit_ref[...].T
+        beside = iter(())
         if is_first:
-            find_changes()
-            change_col_ref[...] = column(change_ref[:1, :])
+            beside = find_changes()
+            next(beside)
         sums = [jnp.zeros((SUBLANES, LANES), jnp.float32) for _ in range(n_half)]
         for s in range(steps):
             now, later = lows[s % 2], lows[(s + 1) % 2]
+            if is_first and s == steps - 1:
+                for _ in beside:
+                    pass
+                change_col_ref[...] = column(change_ref[:1, :])
             for j in range(n_blocks):
+                if is_first and s == 0:
+                    build(j)
+                for _ in range(2 if s else 1):
+                    next(beside, None)
                 states = slice(j * size, (j + 1) * size)
                 if is_first and s == 0:
                     moved = moved_from_identity(j)

time: 33.5 us -> 34.2 us (1.021)
  Pallas kernels: 23.8 us -> 24.5 us
    pallas_call x1, Pallas kernels: 23.8 us -> 24.5 us  [body(): pl.pallas_call(chain_kernel, out_shape=[jax.ShapeDtypeStruct((1, n_rows,...]
where the time goes in v13:
time: 34.2 us; the launch traced here: 34 us
  Pallas kernels  24.5 us (72%)
  blocking collectives  8.18 us (24%)
  local copies, waits for them, and re-layouts  0.66 us (2%)
  between operations  0.63 us (2%)
    pallas_call x1, Pallas kernels, body(): pl.pallas_call(chain_kernel, out_shape=[jax.ShapeDtypeStruct((1, n_rows,...  24.5 us
    all_to_all x1, blocking collectives, body(): all_observed = lax.all_to_all(own, 'tm', 0, 0, tiled=True)  8.18 us

profile of v13, /device:TPU:26, one launch (start us, length us, event | category | flops | bytes accessed | tf_op | source)
XLA Modules:
  0.0 34.0 jit_solution(16822280996991121614)
XLA Ops:
  0.6 0.7 %broadcast_in_dim.2 = s32[8,1,4]{2,1,0:T(1,128)S(1)} broadcast(s32[4]{0:T(128)} %param.7), dimensions={2} | broadcast | bytes 144 | tf_op jit(solution)/shard_map/broadcast_in_dim | solution.py:314
  1.3 8.2 %all_to_all.8 = s32[8,1,4]{2,1,0:T(1,128)} all-to-all(s32[8,1,4]{2,1,0:T(1,128)S(1)} %broadcast_in_dim.2), channel_id=1, replica_groups=mesh['tm'=8,'rows'=4] {'tm'}, dimensions={0} | all-to-all | bytes 256 | tf_op jit(solution)/shard_map/all_to_all | solution.py:315
  9.5 24.5 %chain.1 = (f32[1,256,1024]{2,1,0:T(8,128)}, f32[1,256]{1,0:T(1,128)}) custom-call(s32[8,4]{1,0:T(8,128)} %bitcast.3, s32[4,16]{1,0:T(4,128)} %bitcast.5, s32[256]{0:T(256)} %cluster_hbm.1, f32[1,1024]{1,0:T(1,128)} %bitcast.4, bf16[16,4,64,64]{3,2,1,0:T(8,128)(2,1)} %blocks_hbm.1, f32[16,1024]{1,0:T(8,128)} %cluster_emit_hbm.1, f32[256,1024]{1,0:T(8,128)} %symbol_hbm.1), custom_call_target="tpu_custom_call" | custom-call | flops 17179869184 | bytes 4194304 | tf_op jit(solution)/shard_map/chain/pallas_call | solution.py:320

commit v14 on v12

--- a/solution.py
+++ b/solution.py
@@ -35,8 +35,8 @@
     cluster_ref,
     leave_ref,
     blocks_ref,
-    cluster_emit_ref,
-    symbol_ref,
+    cluster_rows_ref,
+    emit_ref,
     rows_ref,
     leave_col_ref,
     stay_ref,
@@ -45,15 +45,14 @@
     base_ref,
     low_a_ref,
     low_b_ref,
-    emit_ref,
     emit_col_ref,
-    change_col_ref,
+    all_col_ref,
     stay_slab_ref,
     emit_slab_ref,
     sum_refs,
     part_refs,
-    change_ref,
     sems,
+    row_sems,
     block_sems,
     out_sems,
 ):
@@ -75,8 +74,6 @@
                 (leave_hbm, leave_ref),
                 (pattern_hbm, pattern_ref),
                 (cluster_hbm, cluster_ref),
-                (cluster_emit_hbm, cluster_emit_ref),
-                (symbol_hbm, symbol_ref),
             ]
         )
     ]
@@ -90,8 +87,23 @@
         )
         for i in range(n_chunks)
     ]
-    for copy in small[:2] + chunks + small[2:]:
+    emit_ref[...] = jnp.zeros_like(emit_ref)
+    small[2].start()
+    for copy in small[:2] + chunks:
         copy.start()
+    n_all = n_tm * steps
+    small[2].wait()
+    row_copies = []
+    for s in range(steps):
+        for g in range(n_tm):
+            symbol = observed_ref[g, s]
+            row = pl.ds(s * n_tm + g, 1)
+            for source, target, index, sem in (
+                (symbol_hbm, emit_ref, symbol, row_sems.at[0]),
+                (cluster_emit_hbm, cluster_rows_ref, cluster_ref[symbol], row_sems.at[1]),
+            ):
+                copy = pltpu.make_async_copy(source.at[pl.ds(index, 1)], target.at[row], sem)
+                copy.start()
 
     def store(target_ref, low_ref, j, h, new):
         target_ref[h, j, first:, :] = new
@@ -117,7 +129,6 @@
                 here = lane_block + h * per == pattern_ref[k, j]
                 own[h] = own[h] + jnp.where(here, tile, 0.0)
         return jnp.concatenate(own, axis=1)
-    emit_ref[...] = jnp.zeros_like(emit_ref)
     for refs in part_refs:
         for ref in refs:
             ref[...] = jnp.zeros_like(ref)
@@ -144,21 +155,19 @@
             rows = pl.ds(pl.multiple_of(pattern_ref[k, j] * size, size), size)
             parts.append(blocks_ref[j, k].astype(jnp.float32) * leave_col_ref[rows, :size])
         weight_ref[j] = jnp.concatenate(parts, axis=0).T.astype(jnp.bfloat16)
-    for copy in small[2:]:
-        copy.wait()
-
-    def emission_of(g, s):
-        symbol = observed_ref[g, s]
-        row = symbol_ref[pl.ds(symbol, 1), :]
-        return row * cluster_emit_ref[pl.ds(cluster_ref[symbol], 1), :]
+    rows = pl.ds(0, n_all)
+    pltpu.make_async_copy(symbol_hbm.at[rows], emit_ref.at[rows], row_sems.at[0]).wait()
+    rows = pl.ds(0, cluster_rows_ref.shape[0])
+    pltpu.make_async_copy(cluster_rows_ref, cluster_rows_ref, row_sems.at[1]).wait()
+    emit_ref[:n_all, :] = emit_ref[:n_all, :] * cluster_rows_ref[...]
 
     def find_changes():
         rows = n_blocks * n_tm
         stays = stay_slab_ref[...].reshape(rows, LANES)
         for s in range(steps):
-            emission = jnp.concatenate([emission_of(g, s) for g in range(n_tm)], axis=0)
             for j in range(n_blocks):
-                tile = emission[:, j // per * LANES : (j // per + 1) * LANES]
+                cols = slice(j // per * LANES, (j // per + 1) * LANES)
+                tile = emit_ref[s * n_tm : (s + 1) * n_tm, cols]
                 emit_slab_ref[s, j] = twice(tile, j % per, size)
 
         def row_sums(l, p):
@@ -210,18 +219,16 @@
             tile = change[m * per + per - 1]
             for i in range(per - 1):
                 tile = jnp.where(low_half, change[m * per + i], tile)
-            change_ref[:, m * LANES : (m + 1) * LANES] = tile
+            emit_ref[n_all : n_all + n_tm, m * LANES : (m + 1) * LANES] = tile
 
     def segment(g, carried, is_first=False):
         scale, log_scale = carried
-        for s in range(steps):
-            emit_ref[s : s + 1, :] = emission_of(g, s)
-        if not is_first:
-            emit_ref[steps : steps + 1, :] = change_ref[pl.ds(g, 1), :]
-        emit_col_ref[...] = emit_ref[...].T
         if is_first:
+            emit_col_ref[...] = emit_ref[...].T
             find_changes()
-            change_col_ref[...] = column(change_ref[:1, :])
+            all_col_ref[...] = emit_ref[...].T
+        else:
+            emit_col_ref[...] = pltpu.roll(all_col_ref[...], LANES - g, 1)
         sums = [jnp.zeros((SUBLANES, LANES), jnp.float32) for _ in range(n_half)]
         for s in range(steps):
             now, later = lows[s % 2], lows[(s + 1) % 2]
@@ -239,16 +246,14 @@
                         jnp.concatenate(picked, axis=0),
                         preferred_element_type=jnp.float32,
                     )
-                emission = jnp.broadcast_to(emit_col_ref[states, s : s + 1], (size, LANES))
+                emission = jnp.broadcast_to(emit_col_ref[states, s * n_tm : s * n_tm + 1], (size, LANES))
                 stay = stay_ref[states, :]
                 from_ref = base_ref if s == 0 else cur_ref
                 to_ref = base_ref if s == steps - 1 else cur_ref
                 if s == steps - 1:
-                    if is_first:
-                        change = change_col_ref[states, :]
-                    else:
-                        change = emit_col_ref[states, steps : steps + 1]
-                        change = jnp.broadcast_to(change, (size, LANES))
+                    change_ref = all_col_ref if is_first else emit_col_ref
+                    change = change_ref[states, n_all : n_all + 1]
+                    change = jnp.broadcast_to(change, (size, LANES))
                 for h in range(n_half):
                     part = slice(h * LANES, (h + 1) * LANES)
                     kept = from_ref[h, j, first - 1 : padded - 1, :] * stay
@@ -317,8 +322,8 @@
             pltpu.SMEM(symbol_cluster.shape, jnp.int32),
             pltpu.VMEM((1, n_states), f32),
             pltpu.VMEM(trans_blocks.shape, bf16),
-            pltpu.VMEM(cluster_emit.shape, f32),
-            pltpu.VMEM(symbol_emit.shape, f32),
+            pltpu.VMEM((n_tm * steps, n_states), f32),
+            pltpu.VMEM((LANES, n_states), f32),
             pltpu.VMEM((n_rows, n_states), f32),
             pltpu.VMEM((n_states, LANES), f32),
             pltpu.VMEM((n_states, LANES), f32),
@@ -327,7 +332,6 @@
             pltpu.VMEM((n_rows // LANES, n_blocks, size + SUBLANES, LANES), f32),
             pltpu.VMEM((n_states, n_rows), bf16),
             pltpu.VMEM((n_states, n_rows), bf16),
-            pltpu.VMEM((LANES, n_states), f32),
             pltpu.VMEM((n_states, LANES), f32),
             pltpu.VMEM((n_states, LANES), f32),
             pltpu.VMEM((n_blocks, n_tm, LANES), f32),
@@ -337,8 +341,8 @@
                 [pltpu.VMEM((steps - l, n_blocks, n_tm, LANES), f32) for _ in range(LANES // size)]
                 for l in range(steps)
             ],
-            pltpu.VMEM((n_tm, n_states), f32),
-            pltpu.SemaphoreType.DMA((5,)),
+            pltpu.SemaphoreType.DMA((3,)),
+            pltpu.SemaphoreType.DMA((2,)),
             pltpu.SemaphoreType.DMA((4,)),
             pltpu.SemaphoreType.DMA((2 * n_rows // LANES,)),
         ],

time: 33.5 us -> 34 us (1.015)
  Pallas kernels: 23.8 us -> 24.3 us
    pallas_call x1, Pallas kernels: 23.8 us -> 24.3 us  [body(): pl.pallas_call(chain_kernel, out_shape=[jax.ShapeDtypeStruct((1, n_rows,...]
where the time goes in v14:
time: 34 us; the launch traced here: 33.8 us
  Pallas kernels  24.3 us (71%)
  blocking collectives  8.18 us (24%)
  local copies, waits for them, and re-layouts  0.66 us (2%)
  between operations  0.63 us (2%)
    pallas_call x1, Pallas kernels, body(): pl.pallas_call(chain_kernel, out_shape=[jax.ShapeDtypeStruct((1, n_rows,...  24.3 us
    all_to_all x1, blocking collectives, body(): all_observed = lax.all_to_all(own, 'tm', 0, 0, tiled=True)  8.18 us

profile of v14, /device:TPU:26, one launch (start us, length us, event | category | flops | bytes accessed | tf_op | source)
XLA Modules:
  0.0 33.8 jit_solution(6567452942006842258)
XLA Ops:
  0.6 0.7 %broadcast_in_dim.2 = s32[8,1,4]{2,1,0:T(1,128)S(1)} broadcast(s32[4]{0:T(128)} %param.7), dimensions={2} | broadcast | bytes 144 | tf_op jit(solution)/shard_map/broadcast_in_dim | solution.py:306
  1.3 8.2 %all_to_all.8 = s32[8,1,4]{2,1,0:T(1,128)} all-to-all(s32[8,1,4]{2,1,0:T(1,128)S(1)} %broadcast_in_dim.2), channel_id=1, replica_groups=mesh['tm'=8,'rows'=4] {'tm'}, dimensions={0} | all-to-all | bytes 256 | tf_op jit(solution)/shard_map/all_to_all | solution.py:307
  9.5 24.3 %chain.1 = (f32[1,256,1024]{2,1,0:T(8,128)}, f32[1,256]{1,0:T(1,128)}) custom-call(s32[8,4]{1,0:T(8,128)} %bitcast.3, s32[4,16]{1,0:T(4,128)} %bitcast.5, s32[256]{0:T(256)} %cluster_hbm.1, f32[1,1024]{1,0:T(1,128)} %bitcast.4, bf16[16,4,64,64]{3,2,1,0:T(8,128)(2,1)} %blocks_hbm.1, f32[16,1024]{1,0:T(8,128)} %cluster_emit_hbm.1, f32[256,1024]{1,0:T(8,128)} %symbol_hbm.1), custom_call_target="tpu_custom_call" | custom-call | flops 17179869184 | bytes 4194304 | tf_op jit(solution)/shard_map/chain/pallas_call | solution.py:312

commit v15 on v12

--- a/solution.py
+++ b/solution.py
@@ -22,7 +22,7 @@
 
 
 def chain_kernel(
-    observed_ref,
+    observed_hbm,
     pattern_hbm,
     cluster_hbm,
     leave_hbm,
@@ -30,6 +30,8 @@
     cluster_emit_hbm,
     symbol_hbm,
     rows_hbm,
+    rate_hbm,
+    observed_ref,
     rate_ref,
     pattern_ref,
     cluster_ref,
@@ -74,6 +76,7 @@
             [
                 (leave_hbm, leave_ref),
                 (pattern_hbm, pattern_ref),
+                (observed_hbm, observed_ref),
                 (cluster_hbm, cluster_ref),
                 (cluster_emit_hbm, cluster_emit_ref),
                 (symbol_hbm, symbol_ref),
@@ -269,9 +272,13 @@
     carried = segment(0, (ones, jnp.zeros_like(ones)), is_first=True)
     scale, log_scale = lax.fori_loop(1, n_segments, segment, carried)
     scale = scale * n_states
-    out = []
+    n_out = out_sems.shape[0]
+    divisor = (n_segments * steps).astype(jnp.float32)
+    rate_ref[...] = (log_scale - jnp.log(jnp.full_like(ones, n_states))) / divisor
+    out = [pltpu.make_async_copy(rate_ref, rate_hbm, out_sems.at[0])]
+    out[0].start()
     n_tiles = n_states // LANES
-    per_out = n_half * n_tiles // out_sems.shape[0]
+    per_out = n_half * n_tiles // (n_out - 1)
     for h in range(n_half):
         part = slice(h * LANES, (h + 1) * LANES)
         for j in range(n_tiles):
@@ -286,8 +293,6 @@
                     pltpu.make_async_copy(rows_ref.at[rows, cols], rows_hbm.at[0, rows, cols], sem)
                 )
                 out[-1].start()
-    divisor = (n_segments * steps).astype(jnp.float32)
-    rate_ref[...] = (log_scale - jnp.log(jnp.full_like(ones, n_states))) / divisor
     for copy in out:
         copy.wait()
 
@@ -300,8 +305,6 @@
     n_tm = lax.axis_size("tm")
     own = jnp.broadcast_to(observed[None, :], (n_tm, steps))
     all_observed = lax.all_to_all(own, "tm", 0, 0, tiled=True)
-    vmem = pl.BlockSpec(memory_space=pltpu.VMEM)
-    smem = pl.BlockSpec(memory_space=pltpu.SMEM)
     hbm = pl.BlockSpec(memory_space=pltpu.HBM)
     f32, bf16 = jnp.float32, jnp.bfloat16
     return pl.pallas_call(
@@ -310,9 +313,11 @@
             jax.ShapeDtypeStruct((1, n_rows, n_states), f32),
             jax.ShapeDtypeStruct((1, n_rows), f32),
         ],
-        in_specs=[smem] + [hbm] * 6,
-        out_specs=[hbm, vmem],
+        in_specs=[hbm] * 7,
+        out_specs=[hbm, hbm],
         scratch_shapes=[
+            pltpu.SMEM((n_tm, steps), jnp.int32),
+            pltpu.VMEM((1, n_rows), f32),
             pltpu.SMEM((n_source, n_blocks), jnp.int32),
             pltpu.SMEM(symbol_cluster.shape, jnp.int32),
             pltpu.VMEM((1, n_states), f32),
@@ -338,9 +343,9 @@
                 for l in range(steps)
             ],
             pltpu.VMEM((n_tm, n_states), f32),
-            pltpu.SemaphoreType.DMA((5,)),
+            pltpu.SemaphoreType.DMA((6,)),
             pltpu.SemaphoreType.DMA((4,)),
-            pltpu.SemaphoreType.DMA((2 * n_rows // LANES,)),
+            pltpu.SemaphoreType.DMA((1 + 2 * n_rows // LANES,)),
         ],
         compiler_params=pltpu.CompilerParams(vmem_limit_bytes=60 << 20),
         cost_estimate=pl.CostEstimate(flops=1 << 34, bytes_accessed=4 << 20, transcendentals=0),

time: 33.5 us -> 32.3 us (0.964)
  Pallas kernels: 23.8 us -> 22.7 us
    pallas_call x1, Pallas kernels: 23.8 us -> 22.7 us  [body(): pl.pallas_call(chain_kernel, out_shape=[jax.ShapeDtypeStruct((1, n_rows,...]
where the time goes in v15:
time: 32.3 us; the launch traced here: 32.1 us
  Pallas kernels  22.7 us (70%)
  blocking collectives  8.18 us (25%)
  local copies, waits for them, and re-layouts  0.66 us (2%)
  between operations  0.63 us (2%)
    pallas_call x1, Pallas kernels, body(): pl.pallas_call(chain_kernel, out_shape=[jax.ShapeDtypeStruct((1, n_rows,...  22.7 us
    all_to_all x1, blocking collectives, body(): all_observed = lax.all_to_all(own, 'tm', 0, 0, tiled=True)  8.18 us
    broadcast_in_dim x1, local copies, waits for them, and re-layouts, body(): own = jnp.broadcast_to(observed[None, :], (n_tm, steps))  0.66 us

profile of v15, /device:TPU:26, one launch (start us, length us, event | category | flops | bytes accessed | tf_op | source)
XLA Modules:
  0.0 32.1 jit_solution(3900195174392772919)
XLA Ops:
  0.6 0.7 %broadcast_in_dim.2 = s32[8,1,4]{2,1,0:T(1,128)S(1)} broadcast(s32[4]{0:T(128)} %param.7), dimensions={2} | broadcast | bytes 144 | tf_op jit(solution)/shard_map/broadcast_in_dim | solution.py:306
  1.3 8.2 %all_to_all.8 = s32[8,1,4]{2,1,0:T(1,128)} all-to-all(s32[8,1,4]{2,1,0:T(1,128)S(1)} %broadcast_in_dim.2), channel_id=1, replica_groups=mesh['tm'=8,'rows'=4] {'tm'}, dimensions={0} | all-to-all | bytes 256 | tf_op jit(solution)/shard_map/all_to_all | solution.py:307
  9.5 22.7 %chain.1 = (f32[1,256,1024]{2,1,0:T(8,128)}, f32[1,256]{1,0:T(1,128)}) custom-call(s32[8,4]{1,0:T(8,128)} %bitcast.3, s32[4,16]{1,0:T(4,128)} %bitcast.5, s32[256]{0:T(256)} %cluster_hbm.1, f32[1,1024]{1,0:T(1,128)} %bitcast.4, bf16[16,4,64,64]{3,2,1,0:T(8,128)(2,1)} %blocks_hbm.1, f32[16,1024]{1,0:T(8,128)} %cluster_emit_hbm.1, f32[256,1024]{1,0:T(8,128)} %symbol_hbm.1), custom_call_target="tpu_custom_call" | custom-call | flops 17179869184 | bytes 4194304 | tf_op jit(solution)/shard_map/chain/pallas_call | solution.py:310

commit v16 on v15

--- a/solution.py
+++ b/solution.py
@@ -163,6 +163,7 @@
             for j in range(n_blocks):
                 tile = emission[:, j // per * LANES : (j // per + 1) * LANES]
                 emit_slab_ref[s, j] = twice(tile, j % per, size)
+        yield
 
         def row_sums(l, p):
             return sum_refs[l][p].reshape(rows, LANES)
@@ -186,12 +187,14 @@
                     source = pattern_ref[k, j]
                     for p in range(n_pos):
                         ref[p, source] = ref[p, source] + tile[p]
+                yield
             for p in range(n_pos):
                 sides = [ref[p].reshape(rows, LANES) for ref in part_refs[l]]
                 total = jnp.where(low_half, sides[0], sides[1])
                 total = total + pltpu.roll(total, size, 1)
                 total = total + stays * pltpu.roll(images[p], LANES - 1, 1)
                 sum_refs[l][p] = total.reshape(n_blocks, n_tm, LANES)
+            yield
 
         exact = jnp.ones((rows, LANES), jnp.float32)
         weight = exact
@@ -208,6 +211,7 @@
             rounded = rounded * (row_sum * (1.0 / n_states))
             deviation.append(rounded - weight)
             weight = rounded
+            yield
         change = (weight - exact).reshape(n_blocks, n_tm, LANES)
         for m in range(n_states // LANES):
             tile = change[m * per + per - 1]
@@ -222,13 +226,17 @@
         if not is_first:
             emit_ref[steps : steps + 1, :] = change_ref[pl.ds(g, 1), :]
         emit_col_ref[...] = emit_ref[...].T
-        if is_first:
-            find_changes()
-            change_col_ref[...] = column(change_ref[:1, :])
+        beside = find_changes() if is_first else iter(())
         sums = [jnp.zeros((SUBLANES, LANES), jnp.float32) for _ in range(n_half)]
         for s in range(steps):
             now, later = lows[s % 2], lows[(s + 1) % 2]
+            if is_first and s == steps - 1:
+                for _ in beside:
+                    pass
+                change_col_ref[...] = column(change_ref[:1, :])
             for j in range(n_blocks):
+                for _ in range(2):
+                    next(beside, None)
                 states = slice(j * size, (j + 1) * size)
                 if is_first and s == 0:
                     moved = moved_from_identity(j)

time: 32.3 us -> 32.3 us (level)
  no operation moved by 1% of the time
where the time goes in v16:
time: 32.3 us; the launch traced here: 32.1 us
  Pallas kernels  22.6 us (70%)
  blocking collectives  8.18 us (25%)
  local copies, waits for them, and re-layouts  0.66 us (2%)
  between operations  0.63 us (2%)
    pallas_call x1, Pallas kernels, body(): pl.pallas_call(chain_kernel, out_shape=[jax.ShapeDtypeStruct((1, n_rows,...  22.6 us
    all_to_all x1, blocking collectives, body(): all_observed = lax.all_to_all(own, 'tm', 0, 0, tiled=True)  8.18 us
    broadcast_in_dim x1, local copies, waits for them, and re-layouts, body(): own = jnp.broadcast_to(observed[None, :], (n_tm, steps))  0.66 us

profile of v16, /device:TPU:26, one launch (start us, length us, event | category | flops | bytes accessed | tf_op | source)
XLA Modules:
  0.0 32.1 jit_solution(13677012622372832579)
XLA Ops:
  0.6 0.7 %broadcast_in_dim.2 = s32[8,1,4]{2,1,0:T(1,128)S(1)} broadcast(s32[4]{0:T(128)} %param.7), dimensions={2} | broadcast | bytes 144 | tf_op jit(solution)/shard_map/broadcast_in_dim | solution.py:314
  1.3 8.2 %all_to_all.8 = s32[8,1,4]{2,1,0:T(1,128)} all-to-all(s32[8,1,4]{2,1,0:T(1,128)S(1)} %broadcast_in_dim.2), channel_id=1, replica_groups=mesh['tm'=8,'rows'=4] {'tm'}, dimensions={0} | all-to-all | bytes 256 | tf_op jit(solution)/shard_map/all_to_all | solution.py:315
  9.5 22.6 %chain.1 = (f32[1,256,1024]{2,1,0:T(8,128)}, f32[1,256]{1,0:T(1,128)}) custom-call(s32[8,4]{1,0:T(8,128)} %bitcast.3, s32[4,16]{1,0:T(4,128)} %bitcast.5, s32[256]{0:T(256)} %cluster_hbm.1, f32[1,1024]{1,0:T(1,128)} %bitcast.4, bf16[16,4,64,64]{3,2,1,0:T(8,128)(2,1)} %blocks_hbm.1, f32[16,1024]{1,0:T(8,128)} %cluster_emit_hbm.1, f32[256,1024]{1,0:T(8,128)} %symbol_hbm.1), custom_call_target="tpu_custom_call" | custom-call | flops 17179869184 | bytes 4194304 | tf_op jit(solution)/shard_map/chain/pallas_call | solution.py:318

commit v17 on v15

--- a/solution.py
+++ b/solution.py
@@ -344,8 +344,8 @@
             ],
             pltpu.VMEM((n_tm, n_states), f32),
             pltpu.SemaphoreType.DMA((6,)),
-            pltpu.SemaphoreType.DMA((4,)),
-            pltpu.SemaphoreType.DMA((1 + 2 * n_rows // LANES,)),
+            pltpu.SemaphoreType.DMA((n_blocks,)),
+            pltpu.SemaphoreType.DMA((1 + 4 * n_rows // LANES,)),
         ],
         compiler_params=pltpu.CompilerParams(vmem_limit_bytes=60 << 20),
         cost_estimate=pl.CostEstimate(flops=1 << 34, bytes_accessed=4 << 20, transcendentals=0),

time: 32.3 us -> 33.6 us (1.040)
  Pallas kernels: 22.7 us -> 23.9 us
    pallas_call x1, Pallas kernels: 22.7 us -> 23.9 us  [body(): pl.pallas_call(chain_kernel, out_shape=[jax.ShapeDtypeStruct((1, n_rows,...]
where the time goes in v17:
time: 33.6 us; the launch traced here: 33.4 us
  Pallas kernels  23.9 us (71%)
  blocking collectives  8.18 us (24%)
  local copies, waits for them, and re-layouts  0.66 us (2%)
  between operations  0.63 us (2%)
    pallas_call x1, Pallas kernels, body(): pl.pallas_call(chain_kernel, out_shape=[jax.ShapeDtypeStruct((1, n_rows,...  23.9 us
    all_to_all x1, blocking collectives, body(): all_observed = lax.all_to_all(own, 'tm', 0, 0, tiled=True)  8.18 us

profile of v17, /device:TPU:26, one launch (start us, length us, event | category | flops | bytes accessed | tf_op | source)
XLA Modules:
  0.0 33.4 jit_solution(15138965501648193788)
XLA Ops:
  0.6 0.7 %broadcast_in_dim.2 = s32[8,1,4]{2,1,0:T(1,128)S(1)} broadcast(s32[4]{0:T(128)} %param.7), dimensions={2} | broadcast | bytes 144 | tf_op jit(solution)/shard_map/broadcast_in_dim | solution.py:306
  1.3 8.2 %all_to_all.8 = s32[8,1,4]{2,1,0:T(1,128)} all-to-all(s32[8,1,4]{2,1,0:T(1,128)S(1)} %broadcast_in_dim.2), channel_id=1, replica_groups=mesh['tm'=8,'rows'=4] {'tm'}, dimensions={0} | all-to-all | bytes 256 | tf_op jit(solution)/shard_map/all_to_all | solution.py:307
  9.5 23.9 %chain.1 = (f32[1,256,1024]{2,1,0:T(8,128)}, f32[1,256]{1,0:T(1,128)}) custom-call(s32[8,4]{1,0:T(8,128)} %bitcast.3, s32[4,16]{1,0:T(4,128)} %bitcast.5, s32[256]{0:T(256)} %cluster_hbm.1, f32[1,1024]{1,0:T(1,128)} %bitcast.4, bf16[16,4,64,64]{3,2,1,0:T(8,128)(2,1)} %blocks_hbm.1, f32[16,1024]{1,0:T(8,128)} %cluster_emit_hbm.1, f32[256,1024]{1,0:T(8,128)} %symbol_hbm.1), custom_call_target="tpu_custom_call" | custom-call | flops 17179869184 | bytes 4194304 | tf_op jit(solution)/shard_map/chain/pallas_call | solution.py:310
